TPU v7x, 32 devices: a whole 2x2x4 slice. The times are simulated.
32 devices in a mesh: ctx: 4 (over y, x), dp: 8 (over z, core).
Axes of the slice: x: 2, y: 2, z: 4, core: 2. Of those that a mesh axis runs over, the one named last changes fastest.
Arguments:
- query_rows: bfloat16 [8, 512, 32, 128], P('dp', 'ctx'), may hold values from -6 to 6
- key_rows: bfloat16 [8, 512, 4, 128], P('dp', 'ctx'), may hold values from -6 to 6
- value_matrix: bfloat16 [8, 512, 4, 128], P('dp', 'ctx'), may hold values from -6 to 6
- out_grad: bfloat16 [8, 512, 32, 128], P('dp', 'ctx'), may hold values from -6 to 6
- offsets: int32 [8, 5], P('dp'), may hold values from 0 to 512, as said below
- query_head_group: int32 [32], replicated, may hold values from 0 to 3, as said below
Outputs:
- query_grad: bfloat16 [8, 512, 32, 128], P('dp', 'ctx')
- key_grad: bfloat16 [8, 512, 4, 128], P('dp', 'ctx')
Inputs may be any that keep to these rules, and one draw needn't show every extreme that they name: offsets[b, 0] = 0 and offsets rise along each row; every pair holds 1 to 128 positions, and one pair of every sequence holds exactly 128; the positions from offsets[b, 4] to the end of the sequence are padding; the last sequence of the batch has no padding. `query_head_group`: each key and value head serves exactly 8 query heads.
All inputs are finite; a program needn't handle non-finite values.
Results may differ from a plain program's by a relative error of at most 0.005.
Values may be sent and summed in bfloat16 or wider, within the bound.
No kernel may reach another device: no remote copies, remote signals or barrier semaphores. Data moves between devices by JAX's collectives and lax.ppermute only.
A program may use at most 64 MiB of HBM per device.

v0:
```python
import math

import jax
import jax.numpy as jnp
from jax import lax
from jax.sharding import PartitionSpec as P


def pair_index(bounds, positions):
    inner_bounds = bounds[1:]
    found_count = jnp.sum((positions[:, None] >= inner_bounds[None, :]).astype(jnp.int32), axis=1)
    return jnp.where(positions < 0, -1, found_count)


def visible_mask(bounds, pos_rows, pos_cols):
    pairs_total = bounds.shape[0] - 1
    pair_rows = pair_index(bounds, pos_rows)
    pair_cols = pair_index(bounds, pos_cols)
    return (
        (pair_rows[:, None] == pair_cols[None, :])
        & (pair_rows[:, None] < pairs_total)
        & (pos_cols[None, :] <= pos_rows[:, None])
    )


def head_sorter(query_head_group, group_size):
    heads_total = query_head_group.shape[0]
    head_list = jnp.arange(heads_total, dtype=jnp.int32)
    earlier = head_list[None, :] < head_list[:, None]
    same_group = query_head_group[None, :] == query_head_group[:, None]
    sorted_slot = query_head_group * group_size + jnp.sum(
        (earlier & same_group).astype(jnp.int32), axis=1
    )
    return (sorted_slot[None, :] == head_list[:, None]).astype(jnp.bfloat16)


def pair_block(query_four, grad_four, key_win, value_win, visible, inv_root):
    scores = (
        jnp.einsum("rgjd,kgd->gjrk", query_four, key_win, preferred_element_type=jnp.float32)
        * inv_root
    )
    row_live = jnp.any(visible, axis=1)
    row_top = jnp.max(jnp.where(visible, scores, -1e30), axis=-1, keepdims=True)
    row_top = jnp.where(row_live[:, None], row_top, 0.0)
    expo_terms = jnp.where(visible, jnp.exp(scores - row_top), 0.0)
    totals = jnp.sum(expo_terms, axis=-1, keepdims=True) + jnp.where(row_live, 0.0, 1.0)[:, None]
    attn_prob = expo_terms / totals
    prob_grad = jnp.einsum(
        "rgjd,kgd->gjrk", grad_four, value_win, preferred_element_type=jnp.float32
    )
    row_delta = jnp.sum(attn_prob * prob_grad, axis=-1, keepdims=True)
    score_grad = (attn_prob * (prob_grad - row_delta)).astype(jnp.bfloat16)
    query_part = jnp.einsum(
        "gjrk,kgd->rgjd", score_grad, key_win, preferred_element_type=jnp.float32
    )
    key_part = jnp.einsum(
        "gjrk,rgjd->kgd", score_grad, query_four, preferred_element_type=jnp.float32
    )
    return (query_part, key_part)


def per_device(query_rows, key_rows, value_matrix, out_grad, offsets, query_head_group):
    tok_rows = query_rows.shape[1]
    heads_query = query_rows.shape[2]
    heads_kv = key_rows.shape[2]
    head_dim = query_rows.shape[3]
    ctx_size = lax.axis_size("ctx")
    seq_len = tok_rows * ctx_size
    group_size = heads_query // heads_kv
    inv_root = 1.0 / math.sqrt(head_dim)
    bounds = offsets[0]
    local_count = jnp.sum(offsets[:, -1]).astype(jnp.float32)
    count = lax.psum(local_count, "dp")
    tokens_all = offsets.shape[0] * lax.axis_size("dp") * seq_len
    grad_scale = jnp.float32(tokens_all) / count
    q_factor = grad_scale * inv_root
    sorter = head_sorter(query_head_group, group_size)
    sorted_query = jnp.einsum(
        "jh,rhd->rjd", sorter, query_rows[0], preferred_element_type=jnp.float32
    ).astype(jnp.bfloat16)
    sorted_grad = jnp.einsum(
        "jh,rhd->rjd", sorter, out_grad[0], preferred_element_type=jnp.float32
    ).astype(jnp.bfloat16)
    query_heads, grad_heads = (
        lax.all_to_all(sorted_query, "ctx", split_axis=1, concat_axis=0, tiled=True),
        lax.all_to_all(sorted_grad, "ctx", split_axis=1, concat_axis=0, tiled=True),
    )
    per_group = ctx_size // heads_kv
    key_copies = jnp.broadcast_to(
        key_rows[0][:, :, None, :], (tok_rows, heads_kv, per_group, head_dim)
    ).reshape(tok_rows, ctx_size, head_dim)
    value_copies = jnp.broadcast_to(
        value_matrix[0][:, :, None, :], (tok_rows, heads_kv, per_group, head_dim)
    ).reshape(tok_rows, ctx_size, head_dim)
    key_seq, value_seq = (
        lax.all_to_all(key_copies, "ctx", split_axis=1, concat_axis=0, tiled=True),
        lax.all_to_all(value_copies, "ctx", split_axis=1, concat_axis=0, tiled=True),
    )
    heads_here = query_heads.shape[1]
    block_rows = min(512, seq_len)
    window = block_rows + tok_rows
    zero_rows = jnp.zeros((tok_rows, 1, head_dim), jnp.bfloat16)
    key_pad = jnp.concatenate([zero_rows, key_seq], axis=0)
    value_pad = jnp.concatenate([zero_rows, value_seq], axis=0)

    def block_step(key_acc, block_number):
        row_start = block_number * block_rows
        query_block = lax.dynamic_slice_in_dim(query_heads, row_start, block_rows, 0)[:, None]
        grad_block = lax.dynamic_slice_in_dim(grad_heads, row_start, block_rows, 0)[:, None]
        key_win = lax.dynamic_slice_in_dim(key_pad, row_start, window, 0)
        value_win = lax.dynamic_slice_in_dim(value_pad, row_start, window, 0)
        pos_rows = row_start + jnp.arange(block_rows, dtype=jnp.int32)
        pos_cols = row_start - tok_rows + jnp.arange(window, dtype=jnp.int32)
        visible = visible_mask(bounds, pos_rows, pos_cols)
        query_part, key_part = pair_block(
            query_block, grad_block, key_win, value_win, visible, inv_root
        )
        key_acc = lax.dynamic_update_slice_in_dim(
            key_acc,
            lax.dynamic_slice_in_dim(key_acc, row_start, window, 0) + key_part,
            row_start,
            0,
        )
        return (key_acc, query_part[:, 0])

    empty_accumulator = jnp.zeros((seq_len + tok_rows, 1, head_dim), jnp.float32)
    key_acc, query_blocks = lax.scan(
        block_step, empty_accumulator, jnp.arange(seq_len // block_rows, dtype=jnp.int32)
    )
    query_grad_heads = (query_blocks.reshape(seq_len, heads_here, head_dim) * q_factor).astype(
        jnp.bfloat16
    )
    sorted_back = lax.all_to_all(query_grad_heads, "ctx", split_axis=0, concat_axis=1, tiled=True)
    key_parts = lax.all_to_all(key_acc[tok_rows:], "ctx", split_axis=0, concat_axis=1, tiled=True)
    key_total = jnp.sum(key_parts.reshape(tok_rows, heads_kv, per_group, head_dim), axis=2)
    query_grad = jnp.einsum(
        "jh,rjd->rhd", sorter, sorted_back, preferred_element_type=jnp.float32
    ).astype(jnp.bfloat16)
    key_grad = (key_total * q_factor).astype(jnp.bfloat16)
    return (query_grad[None], key_grad[None])


def solution(mesh):
    return jax.shard_map(
        per_device,
        mesh=mesh,
        in_specs=(
            P("dp", "ctx", None, None),
            P("dp", "ctx", None, None),
            P("dp", "ctx", None, None),
            P("dp", "ctx", None, None),
            P("dp", None),
            P(),
        ),
        out_specs=(P("dp", "ctx", None, None), P("dp", "ctx", None, None)),
        check_vma=False,
    )
```

profile of v0, /device:TPU:0, one launch (start us, length us, event | category | flops | bytes accessed | tf_op | source)
XLA Modules:
  0.0 116.5 jit_solution(634632205659912760)
XLA Ops:
  4.2 5.2 %all-to-all-start.1 = ((bf16[128,32,128]{2,0,1:T(8,128)(2,1)}), bf16[128,32,128]{2,0,1:T(8,128)(2,1)S(1)}, u32[]{:S(2)}, u32[]{:S(2)}) async-start(bf16[128,32,128]{2,0,1:T(8,128)(2,1)} %copy.55), calls=%async_computation.1 | async-start | bytes 2097152 | tf_op jit(solution)/shard_map/all_to_all | solution.py:85
  10.3 1.6 %copy.86 = bf16[1,128,4,128]{3,1,2,0:T(8,128)(2,1)} copy(bf16[1,128,4,128]{3,2,1,0:T(4,128)(2,1)} %param.7) | data formatting | bytes 262144 | tf_op args[1]
  12.3 1.8 %fusion.10 = bf16[128,32,128]{2,1,0:T(8,128)(2,1)S(1)} fusion(bf16[1,128,32,128]{3,2,1,0:T(8,128)(2,1)} %param.9, s32[32]{0:T(128)S(1)} %multiply_add_fusion), kind=kOutput, calls=%fused_computation.18 | convolution fusion | flops 34079744 | bytes 2097280 | tf_op jit(solution)/shard_map/jh,rhd->rjd/dot_general | solution.py:81
  14.1 8.9 %all-to-all-done.1 = bf16[128,32,128]{2,0,1:T(8,128)(2,1)S(1)} async-done(((bf16[128,32,128]{2,0,1:T(8,128)(2,1)}), bf16[128,32,128]{2,0,1:T(8,128)(2,1)S(1)}, u32[]{:S(2)}, u32[]{:S(2)}) %all-to-all-start.1) | async-done | bytes 1048608 | tf_op jit(solution)/shard_map/all_to_all | solution.py:85
  23.0 3.9 %all-to-all-start = ((bf16[128,4,128]{2,0,1:T(8,128)(2,1)}), bf16[128,4,128]{2,0,1:T(8,128)(2,1)}, u32[]{:S(2)}, u32[]{:S(2)}) async-start(bf16[128,4,128]{2,0,1:T(8,128)(2,1)} %bitcast.136), calls=%async_computation | async-start | bytes 262144 | tf_op jit(solution)/shard_map/all_to_all | solution.py:96
  28.8 17.1 %psum.7 = f32[]{:T(128)} all-reduce(f32[]{:T(128)} %bitcast.33), channel_id=1, replica_groups=mesh['ctx'=4,'dp'=8] {'dp'}, use_global_device_ids=true, to_apply=%region_7.8 | all-reduce | flops 1 | bytes 8 | tf_op jit(solution)/shard_map/psum | solution.py:73
  47.3 1.6 %copy.85 = bf16[1,128,4,128]{3,1,2,0:T(8,128)(2,1)} copy(bf16[1,128,4,128]{3,2,1,0:T(4,128)(2,1)} %param.8) | data formatting | bytes 262144 | tf_op args[2]
  49.6 3.9 %all-to-all-start.3 = ((bf16[128,32,128]{2,0,1:T(8,128)(2,1)}), bf16[128,32,128]{2,0,1:T(8,128)(2,1)S(1)}, u32[]{:S(2)}, u32[]{:S(2)}) async-start(bf16[128,32,128]{2,0,1:T(8,128)(2,1)} %copy.59), calls=%async_computation.3 | async-start | bytes 2097152 | tf_op jit(solution)/shard_map/all_to_all | solution.py:86
  53.5 2.8 %fusion.3 = (f32[8,512]{1,0:T(8,128)S(1)}, f32[640,512,8]{1,0,2:T(8,128)S(1)}) fusion(pred[512,640]{0,1:T(8,128)(4,1)S(1)} %get-tuple-element.23, bf16[512,8,128]{2,0,1:T(8,128)(2,1)S(1)} %bitcast.128, bf16[512,1,128]{2,0,1:T(8,128)(2,1)} %bitcast.3), kind=kOutput, calls=%fused_computation.7 | convolution fusion | flops 678948864 | bytes 12009472 | tf_op jit(solution)/shard_map/while/body/eval_jaxpr/rgjd,kgd->gjrk/dot_general | solution.py:39
  56.3 3.9 %copy-done.1 = f32[640,512,8]{1,0,2:T(8,128)} copy-done((f32[640,512,8]{1,0,2:T(8,128)}, f32[640,512,8]{1,0,2:T(8,128)S(1)}, u32[]{:S(2)}) %copy-start.1) | copy-done | bytes 10485784
  60.2 2.2 %fusion.7 = f32[8,512]{1,0:T(8,128)S(1)} fusion(f32[640,512,8]{1,0,2:T(8,128)S(1)} %get-tuple-element.33, f32[8,512]{1,0:T(8,128)S(1)} %broadcast_select_fusion, pred[512,640]{0,1:T(8,128)(4,1)S(1)} %get-tuple-element.23), kind=kLoop, calls=%fused_computation.11 | loop fusion | flops 10481664 | bytes 10846208 | tf_op jit(solution)/shard_map/while/body/eval_jaxpr/reduce_sum | solution.py:46
  62.4 3.0 %all-to-all-done.3 = bf16[128,32,128]{2,0,1:T(8,128)(2,1)S(1)} async-done(((bf16[128,32,128]{2,0,1:T(8,128)(2,1)}), bf16[128,32,128]{2,0,1:T(8,128)(2,1)S(1)}, u32[]{:S(2)}, u32[]{:S(2)}) %all-to-all-start.3) | async-done | bytes 1048608 | tf_op jit(solution)/shard_map/all_to_all | solution.py:86
  65.4 4.1 %all-to-all-start.2 = ((bf16[128,4,128]{2,0,1:T(8,128)(2,1)}), bf16[128,4,128]{2,0,1:T(8,128)(2,1)}, u32[]{:S(2)}, u32[]{:S(2)}) async-start(bf16[128,4,128]{2,0,1:T(8,128)(2,1)} %bitcast.135), calls=%async_computation.2 | async-start | bytes 262144 | tf_op jit(solution)/shard_map/all_to_all | solution.py:97
  69.6 2.5 %copy.60 = bf16[128,4,8,128]{3,0,1,2:T(8,128)(2,1)} copy(bf16[128,4,8,128]{3,0,2,1:T(8,128)(2,1)} %bitcast.132) | data formatting | bytes 2097152 | tf_op jit(solution)/shard_map/all_to_all | solution.py:86
  72.0 2.4 %all-to-all-done.2 = bf16[128,4,128]{2,0,1:T(8,128)(2,1)} async-done(((bf16[128,4,128]{2,0,1:T(8,128)(2,1)}), bf16[128,4,128]{2,0,1:T(8,128)(2,1)}, u32[]{:S(2)}, u32[]{:S(2)}) %all-to-all-start.2) | async-done | bytes 131104 | tf_op jit(solution)/shard_map/all_to_all | solution.py:97
  74.4 8.3 %fusion = (f32[8,512]{1,0:T(8,128)S(1)}, f32[640,512,8]{1,0,2:T(8,128)S(1)}) fusion(f32[8,512]{1,0:T(8,128)S(1)} %broadcast_add_fusion, f32[8,512]{1,0:T(8,128)S(1)} %broadcast_select_fusion, f32[640,512,8]{1,0,2:T(8,128)} %copy-done.1, pred[512,640]{0,1:T(8,128)(4,1)S(1)} %get-tuple-element.23, bf16[512,8,128]{2,0,1:T(8,128)(2,1)} %bitcast.133, ...), kind=kOutput, calls=%fused_computation.2 | convolution fusion | flops 686813184 | bytes 22528000 | tf_op jit(solution)/shard_map/while/body/eval_jaxpr/rgjd,kgd->gjrk/dot_general | solution.py:48
  82.8 3.4 %fusion.8 = bf16[8,512,640]{1,2,0:T(8,128)(2,1)S(1)} fusion(f32[640,512,8]{1,0,2:T(8,128)S(1)} %get-tuple-element.35, f32[8,512]{1,0:T(8,128)S(1)} %get-tuple-element.34, f32[8,512]{1,0:T(8,128)S(1)} %broadcast_add_fusion, f32[8,512]{1,0:T(8,128)S(1)} %broadcast_select_fusion, f32[640,512,8]{1,0,2:T(8,128)S(1)} %bitcast.127, ...), kind=kLoop, calls=%fused_computation.12 | loop fusion | flops 18350080 | bytes 26591232 | tf_op jit(solution)/shard_map/reshape.19
  86.2 2.3 %copy-done.2 = bf16[8,512,640]{1,2,0:T(8,128)(2,1)} copy-done((bf16[8,512,640]{1,2,0:T(8,128)(2,1)}, bf16[8,512,640]{1,2,0:T(8,128)(2,1)S(1)}, u32[]{:S(2)}) %copy-start.2) | copy-done | bytes 5242904
  88.5 1.7 %convolution_bitcast_fusion = f32[640,1,128]{0,2,1:T(8,128)S(1)} fusion(bf16[512,8,128]{2,0,1:T(8,128)(2,1)S(1)} %bitcast.129, bf16[8,512,640]{1,2,0:T(8,128)(2,1)S(1)} %fusion.8), kind=kOutput, calls=%fused_computation.23 | convolution fusion | flops 671088640 | bytes 6619136 | tf_op jit(solution)/shard_map/while/body/eval_jaxpr/gjrk,rgjd->kgd/dot_general | solution.py:56
  91.1 3.4 %all-to-all-start.5 = ((f32[512,1,128]{2,1,0:T(1,128)}), f32[512,1,128]{2,1,0:T(1,128)S(1)}, u32[]{:S(2)}, u32[]{:S(2)}) async-start(f32[512,1,128]{2,1,0:T(1,128)} %copy.67), calls=%async_computation.5 | async-start | bytes 524288 | tf_op jit(solution)/shard_map/all_to_all | solution.py:134
  94.5 3.6 %fusion.12 = bf16[512,8,128]{0,2,1:T(8,128)(2,1)S(1)} fusion(bf16[8,512,640]{1,2,0:T(8,128)(2,1)} %copy-done.2, f32[]{:T(128)S(6)} %mul.61, bf16[512,1,128]{2,0,1:T(8,128)(2,1)} %bitcast.3), kind=kOutput, calls=%fused_computation.20 | convolution fusion | flops 672137216 | bytes 6422532 | tf_op jit(solution)/shard_map/while/body/eval_jaxpr/gjrk,kgd->rgjd/dot_general | solution.py:53
  98.1 1.5 %copy.63 = bf16[512,8,128]{2,1,0:T(8,128)(2,1)} copy(bf16[512,8,128]{0,2,1:T(8,128)(2,1)S(1)} %fusion.12) | data formatting | bytes 2097152 | tf_op jit(solution)/shard_map/convert_element_type | solution.py:130
  99.8 3.9 %all-to-all-start.4 = ((bf16[512,8,128]{2,1,0:T(8,128)(2,1)}), bf16[512,8,128]{2,1,0:T(8,128)(2,1)S(1)}, u32[]{:S(2)}, u32[]{:S(2)}) async-start(bf16[512,8,128]{2,1,0:T(8,128)(2,1)} %copy.63), calls=%async_computation.4 | async-start | bytes 2097152 | tf_op jit(solution)/shard_map/all_to_all | solution.py:133
  104.5 10.6 %all-to-all-done.4 = bf16[512,8,128]{2,1,0:T(8,128)(2,1)S(1)} async-done(((bf16[512,8,128]{2,1,0:T(8,128)(2,1)}), bf16[512,8,128]{2,1,0:T(8,128)(2,1)S(1)}, u32[]{:S(2)}, u32[]{:S(2)}) %all-to-all-start.4) | async-done | bytes 1048608 | tf_op jit(solution)/shard_map/all_to_all | solution.py:133
  (41 shorter events, 11.0 us)
Async XLA Ops:
  0.6 1.6 %copy-start = (bf16[1,128,32,128]{3,2,1,0:T(8,128)(2,1)S(1)}, bf16[1,128,32,128]{3,2,1,0:T(8,128)(2,1)}, u32[]{:S(2)}) copy-start(bf16[1,128,32,128]{3,2,1,0:T(8,128)(2,1)} %param.6) | copy-start | bytes 3145732
  4.2 18.8 %all-to-all-start.1 = ((bf16[128,32,128]{2,0,1:T(8,128)(2,1)}), bf16[128,32,128]{2,0,1:T(8,128)(2,1)S(1)}, u32[]{:S(2)}, u32[]{:S(2)}) async-start(bf16[128,32,128]{2,0,1:T(8,128)(2,1)} %copy.55), calls=%async_computation.1 | async-start | bytes 2097152 | tf_op jit(solution)/shard_map/all_to_all | solution.py:85
  23.0 26.6 %all-to-all-start = ((bf16[128,4,128]{2,0,1:T(8,128)(2,1)}), bf16[128,4,128]{2,0,1:T(8,128)(2,1)}, u32[]{:S(2)}, u32[]{:S(2)}) async-start(bf16[128,4,128]{2,0,1:T(8,128)(2,1)} %bitcast.136), calls=%async_computation | async-start | bytes 262144 | tf_op jit(solution)/shard_map/all_to_all | solution.py:96
  49.6 12.8 %copy-start.3 = (bf16[128,4,8,128]{3,0,1,2:T(8,128)(2,1)}, bf16[128,4,8,128]{3,0,1,2:T(8,128)(2,1)S(1)}, u32[]{:S(2)}) copy-start(bf16[128,4,8,128]{3,0,1,2:T(8,128)(2,1)S(1)} %copy.56) | copy-start | bytes 3145732
  49.6 15.8 %all-to-all-start.3 = ((bf16[128,32,128]{2,0,1:T(8,128)(2,1)}), bf16[128,32,128]{2,0,1:T(8,128)(2,1)S(1)}, u32[]{:S(2)}, u32[]{:S(2)}) async-start(bf16[128,32,128]{2,0,1:T(8,128)(2,1)} %copy.59), calls=%async_computation.3 | async-start | bytes 2097152 | tf_op jit(solution)/shard_map/all_to_all | solution.py:86
  56.3 4.0 %copy-start.1 = (f32[640,512,8]{1,0,2:T(8,128)}, f32[640,512,8]{1,0,2:T(8,128)S(1)}, u32[]{:S(2)}) copy-start(f32[640,512,8]{1,0,2:T(8,128)S(1)} %get-tuple-element.33) | copy-start | bytes 31457284
  65.4 4.2 %copy-start.5 = (bf16[128,32,128]{2,0,1:T(8,128)(2,1)}, bf16[128,32,128]{2,0,1:T(8,128)(2,1)S(1)}, u32[]{:S(2)}) copy-start(bf16[128,32,128]{2,0,1:T(8,128)(2,1)S(1)} %all-to-all-done.3) | copy-start | bytes 3145732
  65.4 9.0 %all-to-all-start.2 = ((bf16[128,4,128]{2,0,1:T(8,128)(2,1)}), bf16[128,4,128]{2,0,1:T(8,128)(2,1)}, u32[]{:S(2)}, u32[]{:S(2)}) async-start(bf16[128,4,128]{2,0,1:T(8,128)(2,1)} %bitcast.135), calls=%async_computation.2 | async-start | bytes 262144 | tf_op jit(solution)/shard_map/all_to_all | solution.py:97
  69.6 13.2 %slice-start = ((s8[10485760]{0:T(1024)(128)(4,1)}), s8[2097152]{0:T(1024)(128)(4,1)S(1)}, s32[]{:S(2)}) async-start(s8[10485760]{0:T(1024)(128)(4,1)} %bitcast.126), calls=%async_computation.6 | async-start | bytes 4194304
  74.4 8.3 %slice-start.1 = ((s8[10485760]{0:T(1024)(128)(4,1)}), s8[4194304]{0:T(1024)(128)(4,1)S(1)}, s32[]{:S(2)}) async-start(s8[10485760]{0:T(1024)(128)(4,1)} %bitcast.126), calls=%async_computation.7 | async-start | bytes 8388608
  74.4 8.3 %slice-start.2 = ((s8[10485760]{0:T(1024)(128)(4,1)}), s8[4194304]{0:T(1024)(128)(4,1)S(1)}, s32[]{:S(2)}) async-start(s8[10485760]{0:T(1024)(128)(4,1)} %bitcast.126), calls=%async_computation.8 | async-start | bytes 8388608
  82.8 5.7 %copy-start.4 = (bf16[128,4,8,128]{3,0,1,2:T(8,128)(2,1)S(1)}, bf16[128,4,8,128]{3,0,1,2:T(8,128)(2,1)}, u32[]{:S(2)}) copy-start(bf16[128,4,8,128]{3,0,1,2:T(8,128)(2,1)} %copy-done.3) | copy-start | bytes 3145732
  86.2 2.3 %copy-start.2 = (bf16[8,512,640]{1,2,0:T(8,128)(2,1)}, bf16[8,512,640]{1,2,0:T(8,128)(2,1)S(1)}, u32[]{:S(2)}) copy-start(bf16[8,512,640]{1,2,0:T(8,128)(2,1)S(1)} %fusion.8) | copy-start | bytes 15728644
  91.1 8.8 %all-to-all-start.5 = ((f32[512,1,128]{2,1,0:T(1,128)}), f32[512,1,128]{2,1,0:T(1,128)S(1)}, u32[]{:S(2)}, u32[]{:S(2)}) async-start(f32[512,1,128]{2,1,0:T(1,128)} %copy.67), calls=%async_computation.5 | async-start | bytes 524288 | tf_op jit(solution)/shard_map/all_to_all | solution.py:134
  99.8 15.2 %all-to-all-start.4 = ((bf16[512,8,128]{2,1,0:T(8,128)(2,1)}), bf16[512,8,128]{2,1,0:T(8,128)(2,1)S(1)}, u32[]{:S(2)}, u32[]{:S(2)}) async-start(bf16[512,8,128]{2,1,0:T(8,128)(2,1)} %copy.63), calls=%async_computation.4 | async-start | bytes 2097152 | tf_op jit(solution)/shard_map/all_to_all | solution.py:133
where the time goes:
time: 117 us
  waiting for transfers between devices  25.2 us (22%)
  starting transfers between devices  24.3 us (21%)
  matrix products  20.1 us (17%)
  local copies, waits for them, and re-layouts  19.8 us (17%)
  blocking collectives  17.1 us (15%)
  other arithmetic  7.87 us (7%)
  between operations  2.18 us (2%)
    psum x1, blocking collectives, per_device(): count = lax.psum(local_count, 'dp')  17.1 us
    all_to_all x1, waiting for transfers between devices, per_device(): lax.all_to_all(query_grad_heads, 'ctx', split_axis=0, concat_axis=1, tile...  10.6 us
    unnamed x21, local copies, waits for them, and re-layouts  10.2 us
    all_to_all x1, waiting for transfers between devices, per_device(): lax.all_to_all(sorted_query, 'ctx', split_axis=1, concat_axis=0, tiled=True)  8.91 us
    dot_general x1, matrix products, pair_block(): jnp.einsum('rgjd,kgd->gjrk', grad_four, value_win, preferred_element_type...  8.27 us
    all_to_all x1, starting transfers between devices, per_device(): lax.all_to_all(sorted_query, 'ctx', split_axis=1, concat_axis=0, tiled=True)  5.15 us
    all_to_all x1, starting transfers between devices, per_device(): lax.all_to_all(value_copies, 'ctx', split_axis=1, concat_axis=0, tiled=True)  4.12 us
    all_to_all x1, starting transfers between devices, per_device(): lax.all_to_all(key_copies, 'ctx', split_axis=1, concat_axis=0, tiled=True)  3.94 us
  transfers between devices with their start and end apart: 6, of which 5 were waited for; matrix products, arithmetic and copies ran while one was open for 19% of the time, Pallas kernels for 0%

commit v1 on v0

v1 whole, which is shorter than its diff:
```python
import functools
import math

import jax
import jax.numpy as jnp
from jax import lax
from jax.experimental import pallas as pl
from jax.experimental.pallas import tpu as pltpu
from jax.sharding import PartitionSpec as P

NT = (((1,), (1,)), ((), ()))
NN = (((1,), (0,)), ((), ()))
F32, BF16 = jnp.float32, jnp.bfloat16
BLOCK = 256
CHUNK = 128


def dot(a, b, dims=NN):
    return lax.dot_general(a, b, dims, preferred_element_type=F32)


def split_heads(packed, flat, out, rows, groups, first):
    flat[...] = packed[...].astype(F32)
    for g in range(groups):
        out[g, first : first + rows, :] = flat[pl.ds(g, rows, stride=groups), :].astype(BF16)


def arrange_kernel(sizes, bounds, group, query, grad, key, value, sorted_query, sorted_grad, query_t, unsort, bias, own_key, own_value, flat):
    tok, heads, groups, per = sizes
    step = BLOCK // heads
    share = step * per
    lanes = lax.broadcasted_iota(jnp.int32, (8, BLOCK), 1)
    head = lanes % heads
    seen = [jnp.int32(0)] * groups
    target = (lanes // heads) * per
    for h in range(heads):
        mine = group[h]
        slot = mine * share
        for g in range(groups):
            here = mine == g
            slot = slot + jnp.where(here, seen[g], 0)
            seen[g] = seen[g] + jnp.where(here, 1, 0)
        target = target + jnp.where(head == h, slot, 0)
    rows = lax.broadcasted_iota(jnp.int32, (BLOCK, BLOCK), 0)
    sort = jnp.where(rows == target[:1], 1.0, 0.0).astype(F32)
    unsort[...] = sort.T.astype(BF16)
    sort = sort.astype(BF16)
    for b in range(tok // step):
        part = slice(b * BLOCK, (b + 1) * BLOCK)
        both = jnp.concatenate([query[part, :], grad[part, :]], axis=1)
        both = dot(sort, both).astype(BF16)
        depth = query.shape[1]
        for g in range(groups):
            sorted_query[g, b * share : (b + 1) * share, :] = both[g * share : (g + 1) * share, :depth]
            sorted_grad[g, b * share : (b + 1) * share, :] = both[g * share : (g + 1) * share, depth:]
    for g in range(groups):
        query_t[g] = sorted_query[g].T
    split_heads(key, flat, own_key, tok, groups, 0)
    split_heads(value, flat, own_value, tok, groups, 0)
    start = lax.axis_index("ctx") * tok
    cube = (tok, per, tok)
    row = lax.broadcasted_iota(jnp.int32, cube, 0).reshape(tok * per, tok)
    col = lax.broadcasted_iota(jnp.int32, (tok * per, tok), 1)
    place = row + start
    low = jnp.zeros_like(place)
    last = bounds.shape[1] - 1
    for i in range(1, last):
        low = jnp.where(place >= bounds[0, i], bounds[0, i], low)
    low = jnp.where(place >= bounds[0, last], jnp.int32(1 << 30), low)
    where = start + col - jnp.where(col > row, tok, 0)
    bias[...] = jnp.where(where >= low, 0.0, -1e30).astype(F32)


def score_kernel(sizes, bias, query, grad, query_t, own_key, own_value, back_key, back_value, score_grad, keys, own_t, back, values, flat):
    tok, heads, groups, per = sizes
    depth = query.shape[2]
    split_heads(back_key, flat, keys, tok, groups, tok)
    split_heads(back_value, flat, values, tok, groups, tok)
    keys[:, :tok, :] = own_key[...]
    values[:, :tok, :] = own_value[...]
    rate = math.log2(math.e) / math.sqrt(depth)

    def one_group(g, carry):
        for c in range(tok * per // CHUNK):
            part = slice(c * CHUNK, (c + 1) * CHUNK)
            here = CHUNK // per
            row = c * here + lax.broadcasted_iota(jnp.int32, (here, per, tok), 0).reshape(CHUNK, tok)
            own = lax.broadcasted_iota(jnp.int32, (CHUNK, tok), 1) <= row
            two = dot(query[g, part, :], keys[g], NT)
            scores = jnp.where(own, two[:, :tok], two[:, tok:]) + bias[part, :]
            two = dot(grad[g, part, :], values[g], NT)
            prob_grad = jnp.where(own, two[:, :tok], two[:, tok:])
            top = jnp.maximum(jnp.max(scores, axis=1, keepdims=True), -1e29)
            terms = jnp.exp2((scores - top) * rate)
            scale = 1.0 / jnp.maximum(jnp.sum(terms, axis=1, keepdims=True), 1.0)
            delta = jnp.sum(terms * prob_grad, axis=1, keepdims=True) * scale
            out = (terms * scale) * (prob_grad - delta)
            score_grad[g, part, :tok] = jnp.where(own, out, 0.0).astype(BF16)
            score_grad[g, part, tok:] = jnp.where(own, 0.0, out).astype(BF16)
        both = dot(query_t[g], score_grad[g])
        own_t[g] = both[:, :tok]
        flat[pl.ds(g, tok, stride=groups), :] = both[:, tok:].T
        return carry

    lax.fori_loop(0, groups, one_group, 0)
    back[...] = flat[...].astype(BF16)


def factor_of(count, tokens, depth):
    last = count.shape[1] - 1
    return (tokens / count[0:1, last : last + 1].astype(F32)) * (1.0 / math.sqrt(depth))


def query_kernel(sizes, tokens, count, score_grad, keys, unsort, own_t, query_grad, key_grad, part_grad):
    tok, heads, groups, per = sizes
    depth = keys.shape[2]
    factor = factor_of(count, tokens, depth)
    step = BLOCK // heads
    share = step * per

    def one_group(g, carry):
        for c in range(tok * per // BLOCK):
            part = slice(c * BLOCK, (c + 1) * BLOCK)
            part_grad[g, part, :] = (dot(score_grad[g, part, :], keys[g]) * factor).astype(BF16)
        key_grad[pl.ds(g, tok, stride=groups), :] = own_t[g].T
        return carry

    lax.fori_loop(0, groups, one_group, 0)
    for b in range(0, tok // step, 2):
        both = [
            jnp.concatenate([part_grad[g, (b + i) * share : (b + i + 1) * share, :] for g in range(groups)], axis=0)
            for i in range(2)
        ]
        both = dot(unsort[...], jnp.concatenate(both, axis=1)).astype(BF16)
        query_grad[b * BLOCK : (b + 1) * BLOCK, :] = both[:, :depth]
        query_grad[(b + 1) * BLOCK : (b + 2) * BLOCK, :] = both[:, depth:]


def key_kernel(tokens, count, own, back, key_grad):
    factor = factor_of(count, tokens, own.shape[1])
    key_grad[...] = ((own[...] + back[...].astype(F32)) * factor).astype(BF16)


VMEM = pl.BlockSpec(memory_space=pltpu.VMEM)
SMEM = pl.BlockSpec(memory_space=pltpu.SMEM)


def call(kernel, ins, outs, scratch=()):
    return pl.pallas_call(
        kernel,
        out_shape=[jax.ShapeDtypeStruct(shape, dtype) for shape, dtype in outs],
        in_specs=ins,
        out_specs=[VMEM] * len(outs),
        scratch_shapes=[pltpu.VMEM(shape, dtype) for shape, dtype in scratch],
        compiler_params=pltpu.CompilerParams(vmem_limit_bytes=32 * 1024 * 1024),
    )


def sum_over(value, axis):
    size = lax.axis_size(axis)
    if size & (size - 1):
        return lax.psum(value, axis)
    hop = 1
    while hop < size:
        value = value + lax.ppermute(value, axis, [(i, i ^ hop) for i in range(size)])
        hop *= 2
    return value


def per_device(query_rows, key_rows, value_matrix, out_grad, offsets, query_head_group):
    _, tok, heads, depth = query_rows.shape
    groups = key_rows.shape[2]
    per = heads // groups
    sizes = (tok, heads, groups, per)
    ctx = lax.axis_size("ctx")
    tokens = float(offsets.shape[0] * lax.axis_size("dp") * tok * ctx)
    ahead = [(i, (i + 1) % ctx) for i in range(ctx)]
    behind = [((i + 1) % ctx, i) for i in range(ctx)]

    back_key = lax.ppermute(key_rows, "ctx", ahead).reshape(tok * groups, depth)
    back_value = lax.ppermute(value_matrix, "ctx", ahead).reshape(tok * groups, depth)
    count = sum_over(offsets, "dp")

    sorted_shape = (groups, tok * per, depth)
    sorted_query, sorted_grad, query_t, unsort, bias, own_key, own_value = call(
        functools.partial(arrange_kernel, sizes),
        [SMEM, SMEM, VMEM, VMEM, VMEM, VMEM],
        [
            (sorted_shape, BF16),
            (sorted_shape, BF16),
            ((groups, depth, tok * per), BF16),
            ((BLOCK, BLOCK), BF16),
            ((tok * per, tok), F32),
            ((groups, tok, depth), BF16),
            ((groups, tok, depth), BF16),
        ],
        [((tok * groups, depth), F32)],
    )(
        offsets,
        query_head_group,
        query_rows.reshape(tok * heads, depth),
        out_grad.reshape(tok * heads, depth),
        key_rows.reshape(tok * groups, depth),
        value_matrix.reshape(tok * groups, depth),
    )

    score_grad, keys, own_t, back = call(
        functools.partial(score_kernel, sizes),
        [VMEM] * 8,
        [
            ((groups, tok * per, 2 * tok), BF16),
            ((groups, 2 * tok, depth), BF16),
            ((groups, depth, tok), F32),
            ((tok * groups, depth), BF16),
        ],
        [((groups, 2 * tok, depth), BF16), ((tok * groups, depth), F32)],
    )(bias, sorted_query, sorted_grad, query_t, own_key, own_value, back_key, back_value)

    back = lax.ppermute(back, "ctx", behind)

    query_grad, own = call(
        functools.partial(query_kernel, sizes, tokens),
        [VMEM] * 5,
        [((tok * heads, depth), BF16), ((tok * groups, depth), F32)],
        [(sorted_shape, BF16)],
    )(count, score_grad, keys, unsort, own_t)
    (key_grad,) = call(
        functools.partial(key_kernel, tokens), [VMEM] * 3, [((tok * groups, depth), BF16)]
    )(count, own, back)
    return (query_grad.reshape(query_rows.shape), key_grad.reshape(key_rows.shape))


def solution(mesh):
    return jax.shard_map(
        per_device,
        mesh=mesh,
        in_specs=(
            P("dp", "ctx", None, None),
            P("dp", "ctx", None, None),
            P("dp", "ctx", None, None),
            P("dp", "ctx", None, None),
            P("dp", None),
            P(),
        ),
        out_specs=(P("dp", "ctx", None, None), P("dp", "ctx", None, None)),
        check_vma=False,
    )
```

time: 117 us -> 31.2 us (0.27)
  waiting for transfers between devices: 25.2 us -> 4.98 us
  matrix products: 20.1 us -> 0 us
  blocking collectives: 17.1 us -> 0 us
  local copies, waits for them, and re-layouts: 19.8 us -> 5.57 us
  starting transfers between devices: 24.3 us -> 10.1 us
  Pallas kernels: 0 us -> 9.65 us
  other arithmetic: 7.87 us -> 0.01 us
  between operations: 2.18 us -> 0.67 us
    all_to_all x6 -> x0, waiting for transfers between devices: 25.2 us -> none  [the longest x1 10.6 us: per_device(): lax.all_to_all(query_grad_heads, 'ctx', split_axis=0, concat_axis=1, tile...]
    all_to_all x6 -> x0, starting transfers between devices: 24.3 us -> none  [the longest x1 5.15 us: per_device(): lax.all_to_all(sorted_query, 'ctx', split_axis=1, concat_axis=0, tiled=True)]
    dot_general x7 -> x0, matrix products: 20.1 us -> none  [the longest x1 8.27 us: pair_block(): jnp.einsum('rgjd,kgd->gjrk', grad_four, value_win, preferred_element_type...]
    psum x1 -> x0, blocking collectives: 17.1 us -> none  [per_device(): count = lax.psum(local_count, 'dp')]
    ppermute x0 -> x6, starting transfers between devices: none -> 10.1 us  [the longest x3 4.13 us: sum_over(): lax.ppermute(value, axis, [(i, i ^ hop) for i in range(size)])]
    pallas_call x0 -> x4, Pallas kernels: none -> 9.65 us  [the longest x1 4.02 us: per_device(): call(functools.partial(score_kernel, sizes), [VMEM] * 8, [((groups, tok *...]
    ppermute x0 -> x6, waiting for transfers between devices: none -> 4.98 us  [the longest x3 4.97 us: sum_over(): lax.ppermute(value, axis, [(i, i ^ hop) for i in range(size)])]
    unnamed x21 -> x12, local copies, waits for them, and re-layouts: 10.2 us -> 5.57 us
  transfers between devices with their start and end apart: 6 -> 6, of which waited for: 5 -> 3; matrix products, arithmetic and copies ran while one was open for 19% -> 0% of each run, Pallas kernels for 0% -> 16%
where the time goes in v1:
time: 31.2 us; the launch traced here: 31 us
  starting transfers between devices  10.1 us (32%)
  Pallas kernels  9.65 us (31%)
  local copies, waits for them, and re-layouts  5.57 us (18%)
  waiting for transfers between devices  4.98 us (16%)
  between operations  0.67 us (2%)
    unnamed x12, local copies, waits for them, and re-layouts  5.57 us
    ppermute x3, waiting for transfers between devices, sum_over(): lax.ppermute(value, axis, [(i, i ^ hop) for i in range(size)])  4.97 us
    ppermute x3, starting transfers between devices, sum_over(): lax.ppermute(value, axis, [(i, i ^ hop) for i in range(size)])  4.13 us
    pallas_call x1, Pallas kernels, per_device(): call(functools.partial(score_kernel, sizes), [VMEM] * 8, [((groups, tok *...  4.02 us
    ppermute x1, starting transfers between devices, per_device(): back_key = lax.ppermute(key_rows, 'ctx', ahead).reshape(tok * groups, depth)  2.99 us
    pallas_call x1, Pallas kernels, per_device(): call(functools.partial(query_kernel, sizes, tokens), [VMEM] * 5, [((tok *...  2.59 us
    pallas_call x1, Pallas kernels, per_device(): call(functools.partial(arrange_kernel, sizes), [SMEM, SMEM, VMEM, VMEM, V...  2.28 us
    ppermute x1, starting transfers between devices, per_device(): lax.ppermute(value_matrix, 'ctx', ahead).reshape(tok * groups, depth)  1.49 us
  transfers between devices with their start and end apart: 6, of which 3 were waited for; matrix products, arithmetic and copies ran while one was open for 0% of the time, Pallas kernels for 16%

profile of v1, /device:TPU:0, one launch (start us, length us, event | category | flops | bytes accessed | tf_op | source)
XLA Modules:
  0.0 31.0 jit_solution(2827983707273338035)
XLA Ops:
  0.6 3.0 %collective-permute-start.3 = (bf16[1,128,4,128]{3,2,1,0:T(4,128)(2,1)}, bf16[1,128,4,128]{3,2,1,0:T(4,128)(2,1)S(1)}, u32[]{:S(2)}, u32[]{:S(2)}) collective-permute-start(bf16[1,128,4,128]{3,2,1,0:T(4,128)(2,1)} %param.7), channel_id=1, source_target_pairs={{0,8},{8,16},{16,24},{24,0},{1,9},{9,17},{17,25},{25,1},{2,10},{10... | collective-permute-start | bytes 393224 | tf_op jit(solution)/shard_map/ppermute | solution.py:180
  3.6 1.5 %collective-permute-start.4 = (bf16[1,128,4,128]{3,2,1,0:T(4,128)(2,1)}, bf16[1,128,4,128]{3,2,1,0:T(4,128)(2,1)S(1)}, u32[]{:S(2)}, u32[]{:S(2)}) collective-permute-start(bf16[1,128,4,128]{3,2,1,0:T(4,128)(2,1)} %param.8), channel_id=1, source_target_pairs={{0,8},{8,16},{16,24},{24,0},{1,9},{9,17},{17,25},{25,1},{2,10},{10... | collective-permute-start | bytes 393224 | tf_op jit(solution)/shard_map/ppermute | solution.py:181
  5.1 0.0 copy-start
  5.1 1.2 %copy-done = bf16[1,128,32,128]{3,2,1,0:T(8,128)(2,1)S(1)} copy-done((bf16[1,128,32,128]{3,2,1,0:T(8,128)(2,1)S(1)}, bf16[1,128,32,128]{3,2,1,0:T(8,128)(2,1)}, u32[]{:S(2)}) %copy-start) | copy-done | bytes 1048600
  6.3 0.0 copy-start.1
  6.3 1.2 %copy-done.1 = bf16[1,128,32,128]{3,2,1,0:T(8,128)(2,1)S(1)} copy-done((bf16[1,128,32,128]{3,2,1,0:T(8,128)(2,1)S(1)}, bf16[1,128,32,128]{3,2,1,0:T(8,128)(2,1)}, u32[]{:S(2)}) %copy-start.1) | copy-done | bytes 1048600
  7.6 0.9 %copy-done.2 = bf16[1,128,4,128]{3,2,1,0:T(4,128)(2,1)S(1)} copy-done((bf16[1,128,4,128]{3,2,1,0:T(4,128)(2,1)S(1)}, bf16[1,128,4,128]{3,2,1,0:T(4,128)(2,1)}, u32[]{:S(2)}) %copy-start.2) | copy-done | bytes 131096
  8.5 0.9 %copy-done.3 = bf16[1,128,4,128]{3,2,1,0:T(4,128)(2,1)S(1)} copy-done((bf16[1,128,4,128]{3,2,1,0:T(4,128)(2,1)S(1)}, bf16[1,128,4,128]{3,2,1,0:T(4,128)(2,1)}, u32[]{:S(2)}) %copy-start.3) | copy-done | bytes 131096
  9.4 0.7 %copy-done.4 = s32[32]{0:T(128)S(1)} copy-done((s32[32]{0:T(128)S(1)}, s32[32]{0:T(128)}, u32[]{:S(2)}) %copy-start.4) | copy-done | bytes 152
  10.0 0.7 %copy-done.5 = s32[1,5]{1,0:T(1,128)S(1)} copy-done((s32[1,5]{1,0:T(1,128)S(1)}, s32[1,5]{1,0:T(1,128)}, u32[]{:S(2)}) %copy-start.5) | copy-done | bytes 44
  10.7 2.3 %shard_map.77 = (bf16[4,1024,128]{2,1,0:T(8,128)(2,1)S(1)}, bf16[4,1024,128]{2,1,0:T(8,128)(2,1)S(1)}, bf16[4,128,1024]{2,1,0:T(8,128)(2,1)S(1)}, bf16[256,256]{...) custom-call(s32[1,5]{1,0:T(1,128)S(1)} %copy-done.5, ...), custom_call_target="tpu_custom_call" | custom-call | tf_op jit(solution)/shard_map/pallas_call | solution.py:185
  13.0 0.0 collective-permute-done.3
  13.0 0.0 collective-permute-done.4
  13.0 4.0 %shard_map.78 = (bf16[4,1024,256]{2,1,0:T(8,128)(2,1)S(1)}, bf16[4,256,128]{2,1,0:T(8,128)(2,1)S(1)}, f32[4,128,128]{2,1,0:T(8,128)S(1)}, bf16[512,128]{1,0:T(8,128)(2,1)S(1)}) custom-call(f32[1024,128]{1,0:T(8,128)S(1)} %get-tuple-element.15.bias, bf16[4,1024,128]{2,1,0:T(8,128)(2,1)S(1)} %get-tuple-element.16.query, ...), custom_call_target="tpu_custom_call" | custom-call | tf_op jit(solution)/shard_map/pallas_call | solution.py:207
  17.0 1.5 %collective-permute-start.5 = (bf16[512,128]{1,0:T(8,128)(2,1)S(1)}, bf16[512,128]{1,0:T(8,128)(2,1)S(1)}, u32[]{:S(2)}, u32[]{:S(2)}) collective-permute-start(bf16[512,128]{1,0:T(8,128)(2,1)S(1)} %get-tuple-element.27), channel_id=1, source_target_pairs={{8,0},{16,8},{24,16},{0,24},{9,1},{17,9},{25,17},{1,25},{10,2},{18... | collective-permute-start | bytes 393224 | tf_op jit(solution)/shard_map/ppermute | solution.py:219
  18.5 0.0 collective-permute-start
  18.5 1.1 %collective-permute-done = s32[1,5]{1,0:T(1,128)S(1)} collective-permute-done((s32[1,5]{1,0:T(1,128)S(1)}, s32[1,5]{1,0:T(1,128)S(1)}, u32[]{:S(2)}, u32[]{:S(2)}) %collective-permute-start) | collective-permute-done | bytes 52 | tf_op jit(solution)/shard_map/ppermute | solution.py:165
  19.6 1.6 %collective-permute-start.1 = (s32[1,5]{1,0:T(1,128)S(1)}, s32[1,5]{1,0:T(1,128)S(1)}, u32[]{:S(2)}, u32[]{:S(2)}) collective-permute-start(s32[1,5]{1,0:T(1,128)S(1)} %add.9), channel_id=1, source_target_pairs={{0,2},{1,3},{2,0},{3,1},{4,6},{5,7},{6,4},{7,5},{8,10},{9,11},{10,... | collective-permute-start | bytes 68 | tf_op jit(solution)/shard_map/ppermute | solution.py:165
  21.2 2.0 %collective-permute-done.1 = s32[1,5]{1,0:T(1,128)S(1)} collective-permute-done((s32[1,5]{1,0:T(1,128)S(1)}, s32[1,5]{1,0:T(1,128)S(1)}, u32[]{:S(2)}, u32[]{:S(2)}) %collective-permute-start.1) | collective-permute-done | bytes 52 | tf_op jit(solution)/shard_map/ppermute | solution.py:165
  23.2 2.6 %collective-permute-start.2 = (s32[1,5]{1,0:T(1,128)S(1)}, s32[1,5]{1,0:T(1,128)S(1)}, u32[]{:S(2)}, u32[]{:S(2)}) collective-permute-start(s32[1,5]{1,0:T(1,128)S(1)} %add.10), channel_id=1, source_target_pairs={{0,4},{1,5},{2,6},{3,7},{4,0},{5,1},{6,2},{7,3},{8,12},{9,13},{10,... | collective-permute-start | bytes 68 | tf_op jit(solution)/shard_map/ppermute | solution.py:165
  25.7 1.9 %collective-permute-done.2 = s32[1,5]{1,0:T(1,128)S(1)} collective-permute-done((s32[1,5]{1,0:T(1,128)S(1)}, s32[1,5]{1,0:T(1,128)S(1)}, u32[]{:S(2)}, u32[]{:S(2)}) %collective-permute-start.2) | collective-permute-done | bytes 52 | tf_op jit(solution)/shard_map/ppermute | solution.py:165
  27.6 2.6 %shard_map.79 = (bf16[4096,128]{1,0:T(8,128)(2,1)}, f32[512,128]{1,0:T(8,128)S(1)}) custom-call(s32[1,5]{1,0:T(1,128)S(1)} %add.11.count, bf16[4,1024,256]{2,1,0:T(8,128)(2,1)S(1)} %get-tuple-element.21.score_grad, bf16[4,256,128]{2,1,0:T(8,128)(2,1)S(1)} %get-tuple-element.22.keys, bf16[256,256]{1,0:T(8,128)(2,1)S(1)} %get-tuple-element.23.unsort, ...), custom_call_target="tpu_custom_call" | custom-call | tf_op jit(solution)/shard_map/pallas_call | solution.py:221
  30.2 0.0 collective-permute-done.5.back
  30.2 0.8 %shard_map.80 = bf16[512,128]{1,0:T(8,128)(2,1)} custom-call(s32[1,5]{1,0:T(1,128)S(1)} %add.11.count, f32[512,128]{1,0:T(8,128)S(1)} %get-tuple-element.26.own, bf16[512,128]{1,0:T(8,128)(2,1)S(1)} %collective-permute-done.5.back), custom_call_target="tpu_custom_call" | custom-call | tf_op jit(solution)/shard_map/pallas_call | solution.py:227
  (7 shorter events, 0.0 us)
Async XLA Ops:
  0.6 12.3 %collective-permute-start.3 = (bf16[1,128,4,128]{3,2,1,0:T(4,128)(2,1)}, bf16[1,128,4,128]{3,2,1,0:T(4,128)(2,1)S(1)}, u32[]{:S(2)}, u32[]{:S(2)}) collective-permute-start(bf16[1,128,4,128]{3,2,1,0:T(4,128)(2,1)} %param.7), channel_id=1, source_target_pairs={{0,8},{8,16},{16,24},{24,0},{1,9},{9,17},{17,25},{25,1},{2,10},{10... | collective-permute-start | bytes 393224 | tf_op jit(solution)/shard_map/ppermute | solution.py:180
  3.6 9.4 %collective-permute-start.4 = (bf16[1,128,4,128]{3,2,1,0:T(4,128)(2,1)}, bf16[1,128,4,128]{3,2,1,0:T(4,128)(2,1)S(1)}, u32[]{:S(2)}, u32[]{:S(2)}) collective-permute-start(bf16[1,128,4,128]{3,2,1,0:T(4,128)(2,1)} %param.8), channel_id=1, source_target_pairs={{0,8},{8,16},{16,24},{24,0},{1,9},{9,17},{17,25},{25,1},{2,10},{10... | collective-permute-start | bytes 393224 | tf_op jit(solution)/shard_map/ppermute | solution.py:181
  5.1 1.2 %copy-start = (bf16[1,128,32,128]{3,2,1,0:T(8,128)(2,1)S(1)}, bf16[1,128,32,128]{3,2,1,0:T(8,128)(2,1)}, u32[]{:S(2)}) copy-start(bf16[1,128,32,128]{3,2,1,0:T(8,128)(2,1)} %param.6) | copy-start | bytes 3145732
  6.3 1.2 %copy-start.1 = (bf16[1,128,32,128]{3,2,1,0:T(8,128)(2,1)S(1)}, bf16[1,128,32,128]{3,2,1,0:T(8,128)(2,1)}, u32[]{:S(2)}) copy-start(bf16[1,128,32,128]{3,2,1,0:T(8,128)(2,1)} %param.9) | copy-start | bytes 3145732
  7.6 0.9 %copy-start.2 = (bf16[1,128,4,128]{3,2,1,0:T(4,128)(2,1)S(1)}, bf16[1,128,4,128]{3,2,1,0:T(4,128)(2,1)}, u32[]{:S(2)}) copy-start(bf16[1,128,4,128]{3,2,1,0:T(4,128)(2,1)} %param.7) | copy-start | bytes 393220
  8.5 0.9 %copy-start.3 = (bf16[1,128,4,128]{3,2,1,0:T(4,128)(2,1)S(1)}, bf16[1,128,4,128]{3,2,1,0:T(4,128)(2,1)}, u32[]{:S(2)}) copy-start(bf16[1,128,4,128]{3,2,1,0:T(4,128)(2,1)} %param.8) | copy-start | bytes 393220
  9.4 0.7 %copy-start.4 = (s32[32]{0:T(128)S(1)}, s32[32]{0:T(128)}, u32[]{:S(2)}) copy-start(s32[32]{0:T(128)} %group.1) | copy-start | bytes 388
  10.0 0.7 %copy-start.5 = (s32[1,5]{1,0:T(1,128)S(1)}, s32[1,5]{1,0:T(1,128)}, u32[]{:S(2)}) copy-start(s32[1,5]{1,0:T(1,128)} %bounds.1) | copy-start | bytes 64
  17.0 13.2 %collective-permute-start.5 = (bf16[512,128]{1,0:T(8,128)(2,1)S(1)}, bf16[512,128]{1,0:T(8,128)(2,1)S(1)}, u32[]{:S(2)}, u32[]{:S(2)}) collective-permute-start(bf16[512,128]{1,0:T(8,128)(2,1)S(1)} %get-tuple-element.27), channel_id=1, source_target_pairs={{8,0},{16,8},{24,16},{0,24},{9,1},{17,9},{25,17},{1,25},{10,2},{18... | collective-permute-start | bytes 393224 | tf_op jit(solution)/shard_map/ppermute | solution.py:219
  18.5 1.1 %collective-permute-start = (s32[1,5]{1,0:T(1,128)S(1)}, s32[1,5]{1,0:T(1,128)S(1)}, u32[]{:S(2)}, u32[]{:S(2)}) collective-permute-start(s32[1,5]{1,0:T(1,128)S(1)} %copy-done.5), channel_id=1, source_target_pairs={{0,1},{1,0},{2,3},{3,2},{4,5},{5,4},{6,7},{7,6},{8,9},{9,8},{10,11... | collective-permute-start | bytes 68 | tf_op jit(solution)/shard_map/ppermute | solution.py:165
  19.6 3.5 %collective-permute-start.1 = (s32[1,5]{1,0:T(1,128)S(1)}, s32[1,5]{1,0:T(1,128)S(1)}, u32[]{:S(2)}, u32[]{:S(2)}) collective-permute-start(s32[1,5]{1,0:T(1,128)S(1)} %add.9), channel_id=1, source_target_pairs={{0,2},{1,3},{2,0},{3,1},{4,6},{5,7},{6,4},{7,5},{8,10},{9,11},{10,... | collective-permute-start | bytes 68 | tf_op jit(solution)/shard_map/ppermute | solution.py:165
  23.2 4.4 %collective-permute-start.2 = (s32[1,5]{1,0:T(1,128)S(1)}, s32[1,5]{1,0:T(1,128)S(1)}, u32[]{:S(2)}, u32[]{:S(2)}) collective-permute-start(s32[1,5]{1,0:T(1,128)S(1)} %add.10), channel_id=1, source_target_pairs={{0,4},{1,5},{2,6},{3,7},{4,0},{5,1},{6,2},{7,3},{8,12},{9,13},{10,... | collective-permute-start | bytes 68 | tf_op jit(solution)/shard_map/ppermute | solution.py:165

commit v2 on v1

v2 whole, which is shorter than its diff:
```python
import functools
import math

import jax
import jax.numpy as jnp
from jax import lax
from jax.experimental import pallas as pl
from jax.experimental.pallas import tpu as pltpu
from jax.sharding import PartitionSpec as P

NT = (((1,), (1,)), ((), ()))
NN = (((1,), (0,)), ((), ()))
TN = (((0,), (0,)), ((), ()))
F32, BF16 = jnp.float32, jnp.bfloat16
BLOCK = 256


def dot(a, b, dims=NN):
    return lax.dot_general(a, b, dims, preferred_element_type=F32)


def stack(*spans):
    pieces = [v[a:b] for v, a, b in spans if b > a]
    return pieces[0] if len(pieces) == 1 else jnp.concatenate(pieces, axis=0)


def split_heads(packed, flat, out, rows, groups):
    flat[...] = packed[...].astype(F32)
    for g in range(groups):
        out[g] = flat[pl.ds(g, rows, stride=groups), :].astype(BF16)


def arrange_kernel(sizes, bounds_in, group_in, query_in, grad_in, key_in, value_in, sorted_query, sorted_grad, unsort, bias, own_key, own_value, bounds, group, query, grad, key, value, flat, sems):
    tok, heads, groups, per = sizes
    step = BLOCK // heads
    share = step * per
    depth = query.shape[1]
    copies = [
        pltpu.make_async_copy(a, b, sems.at[i])
        for i, (a, b) in enumerate(
            [(group_in, group), (bounds_in, bounds), (query_in, query), (grad_in, grad), (key_in, key), (value_in, value)]
        )
    ]
    for copy in copies:
        copy.start()
    copies[0].wait()
    lanes = lax.broadcasted_iota(jnp.int32, (8, BLOCK), 1)
    head = lanes % heads
    seen = [jnp.int32(0)] * groups
    target = (lanes // heads) * per
    for h in range(heads):
        mine = group[h]
        slot = mine * share
        for g in range(groups):
            here = mine == g
            slot = slot + jnp.where(here, seen[g], 0)
            seen[g] = seen[g] + jnp.where(here, 1, 0)
        target = target + jnp.where(head == h, slot, 0)
    rows = lax.broadcasted_iota(jnp.int32, (BLOCK, BLOCK), 0)
    sort = jnp.where(rows == target[:1], 1.0, 0.0).astype(F32)
    unsort[...] = sort.T.astype(BF16)
    sort = sort.astype(BF16)
    copies[1].wait()
    start = lax.axis_index("ctx") * tok
    row = lax.broadcasted_iota(jnp.int32, (8, tok * per), 1) // per
    place = row + start
    low = jnp.zeros_like(place)
    last = bounds.shape[1] - 1
    for i in range(1, last):
        low = jnp.where(place >= bounds[0, i], bounds[0, i], low)
    low = jnp.where(place >= bounds[0, last], jnp.int32(1 << 30), low) - start
    for c in range(0, tok, 8):
        col = c + lax.broadcasted_iota(jnp.int32, (8, tok * per), 0)
        where = col - jnp.where(col > row, tok, 0)
        bias[c : c + 8, :] = jnp.where(where >= low, 0.0, -1e30).astype(F32)
    for copy in copies[2:]:
        copy.wait()
    for b in range(tok // step):
        part = slice(b * BLOCK, (b + 1) * BLOCK)
        both = jnp.concatenate([query[part, :], grad[part, :]], axis=1)
        both = dot(sort, both).astype(BF16)
        for g in range(groups):
            sorted_query[g, b * share : (b + 1) * share, :] = both[g * share : (g + 1) * share, :depth]
            sorted_grad[g, b * share : (b + 1) * share, :] = both[g * share : (g + 1) * share, depth:]
    split_heads(key, flat, own_key, tok, groups)
    split_heads(value, flat, own_value, tok, groups)


def score_kernel(sizes, bias, query, grad, own_key, own_value, back_in, value_in, score_grad, back_key, own_grad, back, back_value, flat):
    tok, heads, groups, per = sizes
    depth = query.shape[2]
    split_heads(back_in, flat, back_key, tok, groups)
    split_heads(value_in, flat, back_value, tok, groups)
    rate = math.log2(math.e) / math.sqrt(depth)
    here = BLOCK // per
    own = lax.broadcasted_iota(jnp.int32, (here, BLOCK), 0) <= lax.broadcasted_iota(jnp.int32, (here, BLOCK), 1) // per
    for g in range(groups):
        for t in range(tok // here):
            part = slice(t * BLOCK, (t + 1) * BLOCK)
            lo, hi = t * here, (t + 1) * here

            def product(left, right, rows):
                a, b = dot(left[g, :hi], rows, NT), dot(right[g, lo:], rows, NT)
                return stack((a, 0, lo), (jnp.where(own, a[lo:], b[:here]), 0, here), (b, here, tok - lo))

            scores = product(own_key, back_key, query[g, part, :]) + bias[:, part]
            prob_grad = product(own_value, back_value, grad[g, part, :])
            top = jnp.maximum(jnp.max(scores, axis=0, keepdims=True), -1e29)
            terms = jnp.exp2((scores - top) * rate)
            scale = 1.0 / jnp.maximum(jnp.sum(terms, axis=0, keepdims=True), 1.0)
            delta = jnp.sum(terms * prob_grad, axis=0, keepdims=True) * scale
            out = (terms * scale) * (prob_grad - delta)
            mid = out[lo:hi]
            score_grad[g, t, :hi, :] = stack((out, 0, lo), (jnp.where(own, mid, 0.0), 0, here)).astype(BF16)
            score_grad[g, t, hi:, :] = stack((jnp.where(own, 0.0, mid), 0, here), (out, hi, tok)).astype(BF16)
    for g in range(groups):
        own_sum, back_sum = [None] * (tok // here), [None] * (tok // here)
        for t in range(tok // here):
            both = dot(score_grad[g, t], query[g, t * BLOCK : (t + 1) * BLOCK, :])
            for i in range(t + 1):
                piece = both[i * here : (i + 1) * here]
                own_sum[i] = piece if own_sum[i] is None else own_sum[i] + piece
            for i in range(t, tok // here):
                piece = both[(i + 1) * here : (i + 2) * here]
                back_sum[i] = piece if back_sum[i] is None else back_sum[i] + piece
        own_grad[g] = jnp.concatenate(own_sum, axis=0)
        flat[pl.ds(g, tok, stride=groups), :] = jnp.concatenate(back_sum, axis=0)
    back[...] = flat[...].astype(BF16)


def factor_of(count, tokens, depth):
    last = count.shape[1] - 1
    return (tokens / count[0:1, last : last + 1].astype(F32)) * (1.0 / math.sqrt(depth))


def query_kernel(sizes, score_grad, own_key, back_key, own_grad, part_grad, key_grad):
    tok, heads, groups, per = sizes
    here = BLOCK // per
    for g in range(groups):
        for t in range(tok // here):
            keys = jnp.concatenate([own_key[g, : (t + 1) * here], back_key[g, t * here :]], axis=0)
            part_grad[g, t * BLOCK : (t + 1) * BLOCK, :] = dot(score_grad[g, t], keys, TN)
        key_grad[pl.ds(g, tok, stride=groups), :] = own_grad[g]


def unsort_kernel(sizes, tokens, count, part_grad, unsort, query_grad):
    tok, heads, groups, per = sizes
    depth = part_grad.shape[2]
    factor = factor_of(count, tokens, depth)
    step = BLOCK // heads
    share = step * per
    for b in range(0, tok // step, 2):
        both = [
            jnp.concatenate([part_grad[g, (b + i) * share : (b + i + 1) * share, :] for g in range(groups)], axis=0)
            for i in range(2)
        ]
        both = (jnp.concatenate(both, axis=1) * factor).astype(BF16)
        both = dot(unsort[...], both).astype(BF16)
        query_grad[b * BLOCK : (b + 1) * BLOCK, :] = both[:, :depth]
        query_grad[(b + 1) * BLOCK : (b + 2) * BLOCK, :] = both[:, depth:]


def key_kernel(tokens, count, own, back, key_grad):
    factor = factor_of(count, tokens, own.shape[1])
    key_grad[...] = ((own[...] + back[...].astype(F32)) * factor).astype(BF16)


VMEM = pl.BlockSpec(memory_space=pltpu.VMEM)
HBM = pl.BlockSpec(memory_space=pltpu.HBM)


def call(kernel, ins, outs, scratch=()):
    return pl.pallas_call(
        kernel,
        out_shape=[jax.ShapeDtypeStruct(shape, dtype) for shape, dtype in outs],
        in_specs=ins,
        out_specs=[VMEM] * len(outs),
        scratch_shapes=list(scratch),
        compiler_params=pltpu.CompilerParams(vmem_limit_bytes=32 * 1024 * 1024),
    )


def add_partner(value, axis, hop):
    return value + lax.ppermute(value, axis, [(i, i ^ hop) for i in range(lax.axis_size(axis))])


def per_device(query_rows, key_rows, value_matrix, out_grad, offsets, query_head_group):
    _, tok, heads, depth = query_rows.shape
    groups = key_rows.shape[2]
    per = heads // groups
    sizes = (tok, heads, groups, per)
    ctx = lax.axis_size("ctx")
    tokens = float(offsets.shape[0] * lax.axis_size("dp") * tok * ctx)
    ahead = [(i, (i + 1) % ctx) for i in range(ctx)]
    behind = [((i + 1) % ctx, i) for i in range(ctx)]

    back_key = lax.ppermute(key_rows, "ctx", ahead).reshape(tok * groups, depth)
    back_value = lax.ppermute(value_matrix, "ctx", ahead).reshape(tok * groups, depth)
    dp = lax.axis_size("dp")
    paired = dp >= 4 and dp & (dp - 1) == 0
    hops = [1 << i for i in range(dp.bit_length() - 1)] if paired else []
    count = add_partner(offsets, "dp", 1) if paired else lax.psum(offsets, "dp")

    sorted_shape = (groups, tok * per, depth)
    packed = (tok * groups, depth)
    split = (groups, tok, depth)
    here = BLOCK // per
    sorted_query, sorted_grad, unsort, bias, own_key, own_value = call(
        functools.partial(arrange_kernel, sizes),
        [HBM] * 6,
        [
            (sorted_shape, BF16),
            (sorted_shape, BF16),
            ((BLOCK, BLOCK), BF16),
            ((tok, tok * per), F32),
            (split, BF16),
            (split, BF16),
        ],
        [
            pltpu.SMEM(offsets.shape, jnp.int32),
            pltpu.SMEM((heads,), jnp.int32),
            pltpu.VMEM((tok * heads, depth), BF16),
            pltpu.VMEM((tok * heads, depth), BF16),
            pltpu.VMEM(packed, BF16),
            pltpu.VMEM(packed, BF16),
            pltpu.VMEM(packed, F32),
            pltpu.SemaphoreType.DMA((6,)),
        ],
    )(
        *[
            pltpu.with_memory_space_constraint(x, pltpu.HBM)
            for x in (
                offsets,
                query_head_group,
                query_rows.reshape(tok * heads, depth),
                out_grad.reshape(tok * heads, depth),
                key_rows.reshape(packed),
                value_matrix.reshape(packed),
            )
        ]
    )

    count, unsort = lax.optimization_barrier((count, unsort))
    for hop in hops[1:-1]:
        count = add_partner(count, "dp", hop)

    score_grad, back_key, own, back = call(
        functools.partial(score_kernel, sizes),
        [VMEM] * 7,
        [
            ((groups, tok // here, tok + here, BLOCK), BF16),
            (split, BF16),
            (split, F32),
            (packed, BF16),
        ],
        [pltpu.VMEM(split, BF16), pltpu.VMEM(packed, F32)],
    )(bias, sorted_query, sorted_grad, own_key, own_value, back_key, back_value)

    count, back = lax.optimization_barrier((count, back))
    back = lax.ppermute(back, "ctx", behind)
    for hop in hops[-1:]:
        count = add_partner(count, "dp", hop)

    part_grad, own = call(
        functools.partial(query_kernel, sizes), [VMEM] * 4, [(sorted_shape, F32), (packed, F32)]
    )(score_grad, own_key, back_key, own)
    (query_grad,) = call(
        functools.partial(unsort_kernel, sizes, tokens), [VMEM] * 3, [((tok * heads, depth), BF16)]
    )(count, part_grad, unsort)
    (key_grad,) = call(
        functools.partial(key_kernel, tokens), [VMEM] * 3, [((tok * groups, depth), BF16)]
    )(count, own, back)
    return (query_grad.reshape(query_rows.shape), key_grad.reshape(key_rows.shape))


def solution(mesh):
    return jax.shard_map(
        per_device,
        mesh=mesh,
        in_specs=(
            P("dp", "ctx", None, None),
            P("dp", "ctx", None, None),
            P("dp", "ctx", None, None),
            P("dp", "ctx", None, None),
            P("dp", None),
            P(),
        ),
        out_specs=(P("dp", "ctx", None, None), P("dp", "ctx", None, None)),
        check_vma=False,
    )
```

time: 31.2 us -> 21.5 us (0.69)
  local copies, waits for them, and re-layouts: 5.57 us -> 0.01 us
  Pallas kernels: 9.65 us -> 7.22 us
  waiting for transfers between devices: 4.98 us -> 3.04 us
    unnamed x12 -> x2, local copies, waits for them, and re-layouts: 5.57 us -> 0.01 us
    pallas_call x3 -> x4, Pallas kernels: 8.89 us -> 6.46 us  [the longest x1 2.41 us: per_device(): call(functools.partial(arrange_kernel, sizes), [HBM] * 6, [(sorted_shape,...]
    ppermute x3, waiting for transfers between devices: 4.97 us -> 3.04 us  [add_partner(): lax.ppermute(value, axis, [(i, i ^ hop) for i in range(lax.axis_size(axis...]
  transfers between devices with their start and end apart: 6 -> 6, of which waited for: 3 -> 2; matrix products, arithmetic and copies ran while one was open for 0% -> 0% of each run, Pallas kernels for 16% -> 22%
where the time goes in v2:
time: 21.5 us; the launch traced here: 21.4 us
  starting transfers between devices  10.4 us (48%)
  Pallas kernels  7.22 us (34%)
  waiting for transfers between devices  3.04 us (14%)
  between operations  0.69 us (3%)
    ppermute x3, starting transfers between devices, add_partner(): lax.ppermute(value, axis, [(i, i ^ hop) for i in range(lax.axis_size(axis...  4.24 us
    ppermute x3, waiting for transfers between devices, add_partner(): lax.ppermute(value, axis, [(i, i ^ hop) for i in range(lax.axis_size(axis...  3.04 us
    ppermute x1, starting transfers between devices, per_device(): back_key = lax.ppermute(key_rows, 'ctx', ahead).reshape(tok * groups, depth)  2.99 us
    pallas_call x1, Pallas kernels, per_device(): call(functools.partial(arrange_kernel, sizes), [HBM] * 6, [(sorted_shape,...  2.41 us
    pallas_call x1, Pallas kernels, per_device(): call(functools.partial(score_kernel, sizes), [VMEM] * 7, [((groups, tok /...  1.79 us
    ppermute x1, starting transfers between devices, per_device(): back = lax.ppermute(back, 'ctx', behind)  1.7 us
    pallas_call x1, Pallas kernels, per_device(): call(functools.partial(unsort_kernel, sizes, tokens), [VMEM] * 3, [((tok...  1.49 us
    ppermute x1, starting transfers between devices, per_device(): lax.ppermute(value_matrix, 'ctx', ahead).reshape(tok * groups, depth)  1.49 us
  transfers between devices with their start and end apart: 6, of which 2 were waited for; matrix products, arithmetic and copies ran while one was open for 0% of the time, Pallas kernels for 22%

profile of v2, /device:TPU:0, one launch (start us, length us, event | category | flops | bytes accessed | tf_op | source)
XLA Modules:
  0.0 21.4 jit_solution(4652924814836208017)
XLA Ops:
  0.6 0.0 copy-start
  0.6 3.0 %collective-permute-start.2 = (bf16[1,128,4,128]{3,2,1,0:T(4,128)(2,1)}, bf16[1,128,4,128]{3,2,1,0:T(4,128)(2,1)S(1)}, u32[]{:S(2)}, u32[]{:S(2)}) collective-permute-start(bf16[1,128,4,128]{3,2,1,0:T(4,128)(2,1)} %param.7), channel_id=1, source_target_pairs={{0,8},{8,16},{16,24},{24,0},{1,9},{9,17},{17,25},{25,1},{2,10},{10... | collective-permute-start | bytes 393224 | tf_op jit(solution)/shard_map/ppermute | solution.py:197
  3.6 1.5 %collective-permute-start.3 = (bf16[1,128,4,128]{3,2,1,0:T(4,128)(2,1)}, bf16[1,128,4,128]{3,2,1,0:T(4,128)(2,1)S(1)}, u32[]{:S(2)}, u32[]{:S(2)}) collective-permute-start(bf16[1,128,4,128]{3,2,1,0:T(4,128)(2,1)} %param.8), channel_id=1, source_target_pairs={{0,8},{8,16},{16,24},{24,0},{1,9},{9,17},{17,25},{25,1},{2,10},{10... | collective-permute-start | bytes 393224 | tf_op jit(solution)/shard_map/ppermute | solution.py:198
  5.1 0.0 collective-permute-start
  5.1 2.4 %shard_map.77 = (bf16[4,1024,128]{2,1,0:T(8,128)(2,1)S(1)}, bf16[4,1024,128]{2,1,0:T(8,128)(2,1)S(1)}, bf16[256,256]{1,0:T(8,128)(2,1)S(1)}, f32[128,1024]{1,0:T...) custom-call(s32[1,5]{1,0:T(1,128)} %bounds_in.1, s32[32]{0:T(128)} %group_in.1, ...), custom_call_target="tpu_custom_call" | custom-call | tf_op jit(solution)/shard_map/pallas_call | solution.py:208
  7.5 0.0 collective-permute-done
  7.6 0.0 copy-done
  7.6 1.6 %collective-permute-start.1 = (s32[1,5]{1,0:T(1,128)S(1)}, s32[1,5]{1,0:T(1,128)S(1)}, u32[]{:S(2)}, u32[]{:S(2)}) collective-permute-start(s32[1,5]{1,0:T(1,128)S(1)} %add.9), channel_id=1, source_target_pairs={{0,2},{1,3},{2,0},{3,1},{4,6},{5,7},{6,4},{7,5},{8,10},{9,11},{10,... | collective-permute-start | bytes 68 | tf_op jit(solution)/shard_map/ppermute | solution.py:184
  9.2 2.0 %collective-permute-done.1 = s32[1,5]{1,0:T(1,128)S(1)} collective-permute-done((s32[1,5]{1,0:T(1,128)S(1)}, s32[1,5]{1,0:T(1,128)S(1)}, u32[]{:S(2)}, u32[]{:S(2)}) %collective-permute-start.1) | collective-permute-done | bytes 52 | tf_op jit(solution)/shard_map/ppermute | solution.py:184
  11.2 0.0 collective-permute-done.2
  11.2 0.0 collective-permute-done.3
  11.2 1.8 %shard_map.78 = (bf16[4,4,160,256]{3,2,1,0:T(8,128)(2,1)S(1)}, bf16[4,128,128]{2,1,0:T(8,128)(2,1)S(1)}, f32[4,128,128]{2,1,0:T(8,128)S(1)}, bf16[512,128]{1,0:T(8,128)(2,1)S(1)}) custom-call(f32[128,1024]{1,0:T(8,128)S(1)} %get-tuple-element.20.bias, bf16[4,1024,128]{2,1,0:T(8,128)(2,1)S(1)} %get-tuple-element.21.query, ...), custom_call_target="tpu_custom_call" | custom-call | tf_op jit(solution)/shard_map/pallas_call | solution.py:247
  13.0 1.7 %collective-permute-start.5 = (bf16[512,128]{1,0:T(8,128)(2,1)S(1)}, bf16[512,128]{1,0:T(8,128)(2,1)S(1)}, u32[]{:S(2)}, u32[]{:S(2)}) collective-permute-start(bf16[512,128]{1,0:T(8,128)(2,1)S(1)} %get-tuple-element.33), channel_id=1, source_target_pairs={{8,0},{16,8},{24,16},{0,24},{9,1},{17,9},{25,17},{1,25},{10,2},{18... | collective-permute-start | bytes 393224 | tf_op jit(solution)/shard_map/ppermute | solution.py:260
  14.7 2.6 %collective-permute-start.4 = (s32[1,5]{1,0:T(1,128)S(1)}, s32[1,5]{1,0:T(1,128)S(1)}, u32[]{:S(2)}, u32[]{:S(2)}) collective-permute-start(s32[1,5]{1,0:T(1,128)S(1)} %add.10), channel_id=1, source_target_pairs={{0,4},{1,5},{2,6},{3,7},{4,0},{5,1},{6,2},{7,3},{8,12},{9,13},{10,... | collective-permute-start | bytes 68 | tf_op jit(solution)/shard_map/ppermute | solution.py:184
  17.3 0.8 %shard_map.79 = (f32[4,1024,128]{2,1,0:T(8,128)S(1)}, f32[512,128]{1,0:T(8,128)S(1)}) custom-call(bf16[4,4,160,256]{3,2,1,0:T(8,128)(2,1)S(1)} %get-tuple-element.27.score_grad, bf16[4,128,128]{2,1,0:T(8,128)(2,1)S(1)} %get-tuple-element.23.own_key, bf16[4,128,128]{2,1,0:T(8,128)(2,1)S(1)} %get-tuple-element.28.back_key, ...), custom_call_target="tpu_custom_call" | custom-call | tf_op jit(solution)/shard_map/pallas_call | solution.py:264
  18.1 1.1 %collective-permute-done.4 = s32[1,5]{1,0:T(1,128)S(1)} collective-permute-done((s32[1,5]{1,0:T(1,128)S(1)}, s32[1,5]{1,0:T(1,128)S(1)}, u32[]{:S(2)}, u32[]{:S(2)}) %collective-permute-start.4) | collective-permute-done | bytes 52 | tf_op jit(solution)/shard_map/ppermute | solution.py:184
  19.1 1.5 %shard_map.80 = bf16[4096,128]{1,0:T(8,128)(2,1)} custom-call(s32[1,5]{1,0:T(1,128)S(1)} %add.11.count, f32[4,1024,128]{2,1,0:T(8,128)S(1)} %get-tuple-element.30.part_grad, bf16[256,256]{1,0:T(8,128)(2,1)S(1)} %get-tuple-element.31.unsort), custom_call_target="tpu_custom_call" | custom-call | tf_op jit(solution)/shard_map/pallas_call | solution.py:267
  20.6 0.0 collective-permute-done.5.back
  20.6 0.8 %shard_map.81 = bf16[512,128]{1,0:T(8,128)(2,1)} custom-call(s32[1,5]{1,0:T(1,128)S(1)} %add.11.count, f32[512,128]{1,0:T(8,128)S(1)} %get-tuple-element.32.own, bf16[512,128]{1,0:T(8,128)(2,1)S(1)} %collective-permute-done.5.back), custom_call_target="tpu_custom_call" | custom-call | tf_op jit(solution)/shard_map/pallas_call | solution.py:270
  (3 shorter events, 0.0 us)
Async XLA Ops:
  0.6 6.9 %copy-start = (s32[1,5]{1,0:T(1,128)S(1)}, s32[1,5]{1,0:T(1,128)}, u32[]{:S(2)}) copy-start(s32[1,5]{1,0:T(1,128)} %bounds_in.1) | copy-start | bytes 64
  0.6 10.5 %collective-permute-start.2 = (bf16[1,128,4,128]{3,2,1,0:T(4,128)(2,1)}, bf16[1,128,4,128]{3,2,1,0:T(4,128)(2,1)S(1)}, u32[]{:S(2)}, u32[]{:S(2)}) collective-permute-start(bf16[1,128,4,128]{3,2,1,0:T(4,128)(2,1)} %param.7), channel_id=1, source_target_pairs={{0,8},{8,16},{16,24},{24,0},{1,9},{9,17},{17,25},{25,1},{2,10},{10... | collective-permute-start | bytes 393224 | tf_op jit(solution)/shard_map/ppermute | solution.py:197
  3.6 7.6 %collective-permute-start.3 = (bf16[1,128,4,128]{3,2,1,0:T(4,128)(2,1)}, bf16[1,128,4,128]{3,2,1,0:T(4,128)(2,1)S(1)}, u32[]{:S(2)}, u32[]{:S(2)}) collective-permute-start(bf16[1,128,4,128]{3,2,1,0:T(4,128)(2,1)} %param.8), channel_id=1, source_target_pairs={{0,8},{8,16},{16,24},{24,0},{1,9},{9,17},{17,25},{25,1},{2,10},{10... | collective-permute-start | bytes 393224 | tf_op jit(solution)/shard_map/ppermute | solution.py:198
  5.1 2.4 %collective-permute-start = (s32[1,5]{1,0:T(1,128)}, s32[1,5]{1,0:T(1,128)S(1)}, u32[]{:S(2)}, u32[]{:S(2)}) collective-permute-start(s32[1,5]{1,0:T(1,128)} %bounds_in.1), channel_id=1, source_target_pairs={{0,1},{1,0},{2,3},{3,2},{4,5},{5,4},{6,7},{7,6},{8,9},{9,8},{10,11... | collective-permute-start | bytes 68 | tf_op jit(solution)/shard_map/ppermute | solution.py:184
  7.6 3.6 %collective-permute-start.1 = (s32[1,5]{1,0:T(1,128)S(1)}, s32[1,5]{1,0:T(1,128)S(1)}, u32[]{:S(2)}, u32[]{:S(2)}) collective-permute-start(s32[1,5]{1,0:T(1,128)S(1)} %add.9), channel_id=1, source_target_pairs={{0,2},{1,3},{2,0},{3,1},{4,6},{5,7},{6,4},{7,5},{8,10},{9,11},{10,... | collective-permute-start | bytes 68 | tf_op jit(solution)/shard_map/ppermute | solution.py:184
  13.0 7.6 %collective-permute-start.5 = (bf16[512,128]{1,0:T(8,128)(2,1)S(1)}, bf16[512,128]{1,0:T(8,128)(2,1)S(1)}, u32[]{:S(2)}, u32[]{:S(2)}) collective-permute-start(bf16[512,128]{1,0:T(8,128)(2,1)S(1)} %get-tuple-element.33), channel_id=1, source_target_pairs={{8,0},{16,8},{24,16},{0,24},{9,1},{17,9},{25,17},{1,25},{10,2},{18... | collective-permute-start | bytes 393224 | tf_op jit(solution)/shard_map/ppermute | solution.py:260
  14.7 4.4 %collective-permute-start.4 = (s32[1,5]{1,0:T(1,128)S(1)}, s32[1,5]{1,0:T(1,128)S(1)}, u32[]{:S(2)}, u32[]{:S(2)}) collective-permute-start(s32[1,5]{1,0:T(1,128)S(1)} %add.10), channel_id=1, source_target_pairs={{0,4},{1,5},{2,6},{3,7},{4,0},{5,1},{6,2},{7,3},{8,12},{9,13},{10,... | collective-permute-start | bytes 68 | tf_op jit(solution)/shard_map/ppermute | solution.py:184

commit v3 on v2

--- a/solution.py
+++ b/solution.py
@@ -86,30 +86,47 @@
     split_heads(value, flat, own_value, tok, groups)
 
 
-def score_kernel(sizes, bias, query, grad, own_key, own_value, back_in, value_in, score_grad, back_key, own_grad, back, back_value, flat):
-    tok, heads, groups, per = sizes
-    depth = query.shape[2]
+def own_mask(per):
+    here = BLOCK // per
+    shape = (here, BLOCK)
+    return lax.broadcasted_iota(jnp.int32, shape, 0) <= lax.broadcasted_iota(jnp.int32, shape, 1) // per
+
+
+def product(left, right, g, t, rows, own):
+    here, tok = own.shape[0], left.shape[1]
+    lo, hi = t * here, (t + 1) * here
+    a, b = dot(left[g, :hi], rows, NT), dot(right[g, lo:], rows, NT)
+    return stack((a, 0, lo), (jnp.where(own, a[lo:], b[:here]), 0, here), (b, here, tok - lo))
+
+
+def probs_kernel(sizes, bias, query, own_key, back_in, probs, back_key, flat):
+    tok, heads, groups, per = sizes
     split_heads(back_in, flat, back_key, tok, groups)
+    rate = math.log2(math.e) / math.sqrt(query.shape[2])
+    own = own_mask(per)
+    for g in range(groups):
+        for t in range(tok * per // BLOCK):
+            part = slice(t * BLOCK, (t + 1) * BLOCK)
+            scores = product(own_key, back_key, g, t, query[g, part, :], own) + bias[:, part]
+            top = jnp.maximum(jnp.max(scores, axis=0, keepdims=True), -1e29)
+            terms = jnp.exp2((scores - top) * rate)
+            scale = 1.0 / jnp.maximum(jnp.sum(terms, axis=0, keepdims=True), 1.0)
+            probs[g, :, part] = terms * scale
+
+
+def score_kernel(sizes, probs, query, grad, own_value, value_in, score_grad, own_grad, back, back_value, flat):
+    tok, heads, groups, per = sizes
     split_heads(value_in, flat, back_value, tok, groups)
-    rate = math.log2(math.e) / math.sqrt(depth)
     here = BLOCK // per
-    own = lax.broadcasted_iota(jnp.int32, (here, BLOCK), 0) <= lax.broadcasted_iota(jnp.int32, (here, BLOCK), 1) // per
+    own = own_mask(per)
     for g in range(groups):
         for t in range(tok // here):
             part = slice(t * BLOCK, (t + 1) * BLOCK)
             lo, hi = t * here, (t + 1) * here
-
-            def product(left, right, rows):
-                a, b = dot(left[g, :hi], rows, NT), dot(right[g, lo:], rows, NT)
-                return stack((a, 0, lo), (jnp.where(own, a[lo:], b[:here]), 0, here), (b, here, tok - lo))
-
-            scores = product(own_key, back_key, query[g, part, :]) + bias[:, part]
-            prob_grad = product(own_value, back_value, grad[g, part, :])
-            top = jnp.maximum(jnp.max(scores, axis=0, keepdims=True), -1e29)
-            terms = jnp.exp2((scores - top) * rate)
-            scale = 1.0 / jnp.maximum(jnp.sum(terms, axis=0, keepdims=True), 1.0)
-            delta = jnp.sum(terms * prob_grad, axis=0, keepdims=True) * scale
-            out = (terms * scale) * (prob_grad - delta)
+            prob = probs[g, :, part]
+            prob_grad = product(own_value, back_value, g, t, grad[g, part, :], own)
+            delta = jnp.sum(prob * prob_grad, axis=0, keepdims=True)
+            out = prob * (prob_grad - delta)
             mid = out[lo:hi]
             score_grad[g, t, :hi, :] = stack((out, 0, lo), (jnp.where(own, mid, 0.0), 0, here)).astype(BF16)
             score_grad[g, t, hi:, :] = stack((jnp.where(own, 0.0, mid), 0, here), (out, hi, tok)).astype(BF16)
@@ -180,8 +197,12 @@
     )
 
 
+def partner(value, axis, hop):
+    return lax.ppermute(value, axis, [(i, i ^ hop) for i in range(lax.axis_size(axis))])
+
+
 def add_partner(value, axis, hop):
-    return value + lax.ppermute(value, axis, [(i, i ^ hop) for i in range(lax.axis_size(axis))])
+    return value + partner(value, axis, hop)
 
 
 def per_device(query_rows, key_rows, value_matrix, out_grad, offsets, query_head_group):
@@ -197,9 +218,9 @@
     back_key = lax.ppermute(key_rows, "ctx", ahead).reshape(tok * groups, depth)
     back_value = lax.ppermute(value_matrix, "ctx", ahead).reshape(tok * groups, depth)
     dp = lax.axis_size("dp")
-    paired = dp >= 4 and dp & (dp - 1) == 0
+    paired = dp >= 8 and dp & (dp - 1) == 0
     hops = [1 << i for i in range(dp.bit_length() - 1)] if paired else []
-    count = add_partner(offsets, "dp", 1) if paired else lax.psum(offsets, "dp")
+    count = add_partner(offsets, "dp", hops[-1]) if paired else lax.psum(offsets, "dp")
 
     sorted_shape = (groups, tok * per, depth)
     packed = (tok * groups, depth)
@@ -241,25 +262,27 @@
     )
 
     count, unsort = lax.optimization_barrier((count, unsort))
-    for hop in hops[1:-1]:
+    for hop in hops[2:-1]:
         count = add_partner(count, "dp", hop)
-
-    score_grad, back_key, own, back = call(
+    moved = partner(count, "dp", 1) if paired else count
+
+    probs, back_key = call(
+        functools.partial(probs_kernel, sizes),
+        [VMEM] * 4,
+        [((groups, tok, tok * per), F32), (split, BF16)],
+        [pltpu.VMEM(packed, F32)],
+    )(bias, sorted_query, own_key, back_key)
+    score_grad, own, back = call(
         functools.partial(score_kernel, sizes),
-        [VMEM] * 7,
-        [
-            ((groups, tok // here, tok + here, BLOCK), BF16),
-            (split, BF16),
-            (split, F32),
-            (packed, BF16),
-        ],
+        [VMEM] * 5,
+        [((groups, tok // here, tok + here, BLOCK), BF16), (split, F32), (packed, BF16)],
         [pltpu.VMEM(split, BF16), pltpu.VMEM(packed, F32)],
-    )(bias, sorted_query, sorted_grad, own_key, own_value, back_key, back_value)
-
-    count, back = lax.optimization_barrier((count, back))
+    )(probs, sorted_query, sorted_grad, own_value, back_value)
+
+    moved, back = lax.optimization_barrier((moved, back))
     back = lax.ppermute(back, "ctx", behind)
-    for hop in hops[-1:]:
-        count = add_partner(count, "dp", hop)
+    if paired:
+        count = add_partner(count + moved, "dp", 2)
 
     part_grad, own = call(
         functools.partial(query_kernel, sizes), [VMEM] * 4, [(sorted_shape, F32), (packed, F32)]

time: 21.5 us -> 20 us (0.930)
  waiting for transfers between devices: 3.04 us -> 1.2 us
  Pallas kernels: 7.22 us -> 7.59 us
    ppermute x3, waiting for transfers between devices: 3.04 us -> 1.19 us  [partner(): lax.ppermute(value, axis, [(i, i ^ hop) for i in range(lax.axis_size(axis...]
    pallas_call x1 -> x2, Pallas kernels: 1.79 us -> 2.16 us  [the longest x1 1.16 us: per_device(): call(functools.partial(score_kernel, sizes), [VMEM] * 5, [((groups, tok /...]
  transfers between devices with their start and end apart: 6 -> 6, of which waited for: 2 -> 1; matrix products, arithmetic and copies ran while one was open for 0% -> 0% of each run, Pallas kernels for 22% -> 34%
where the time goes in v3:
time: 20 us; the launch traced here: 19.9 us
  starting transfers between devices  10.3 us (52%)
  Pallas kernels  7.59 us (38%)
  waiting for transfers between devices  1.2 us (6%)
  between operations  0.72 us (4%)
    ppermute x3, starting transfers between devices, partner(): lax.ppermute(value, axis, [(i, i ^ hop) for i in range(lax.axis_size(axis...  4.24 us
    ppermute x1, starting transfers between devices, per_device(): back_key = lax.ppermute(key_rows, 'ctx', ahead).reshape(tok * groups, depth)  2.99 us
    pallas_call x1, Pallas kernels, per_device(): call(functools.partial(arrange_kernel, sizes), [HBM] * 6, [(sorted_shape,...  2.41 us
    ppermute x1, starting transfers between devices, per_device(): back = lax.ppermute(back, 'ctx', behind)  1.62 us
    pallas_call x1, Pallas kernels, per_device(): call(functools.partial(unsort_kernel, sizes, tokens), [VMEM] * 3, [((tok...  1.49 us
    ppermute x1, starting transfers between devices, per_device(): lax.ppermute(value_matrix, 'ctx', ahead).reshape(tok * groups, depth)  1.49 us
    ppermute x3, waiting for transfers between devices, partner(): lax.ppermute(value, axis, [(i, i ^ hop) for i in range(lax.axis_size(axis...  1.19 us
    pallas_call x1, Pallas kernels, per_device(): call(functools.partial(score_kernel, sizes), [VMEM] * 5, [((groups, tok /...  1.16 us
  transfers between devices with their start and end apart: 6, of which 1 were waited for; matrix products, arithmetic and copies ran while one was open for 0% of the time, Pallas kernels for 34%

profile of v3, /device:TPU:0, one launch (start us, length us, event | category | flops | bytes accessed | tf_op | source)
XLA Modules:
  0.0 19.9 jit_solution(16600184599791926946)
XLA Ops:
  0.6 0.0 copy-start
  0.6 3.0 %collective-permute-start.2 = (bf16[1,128,4,128]{3,2,1,0:T(4,128)(2,1)}, bf16[1,128,4,128]{3,2,1,0:T(4,128)(2,1)S(1)}, u32[]{:S(2)}, u32[]{:S(2)}) collective-permute-start(bf16[1,128,4,128]{3,2,1,0:T(4,128)(2,1)} %param.7), channel_id=1, source_target_pairs={{0,8},{8,16},{16,24},{24,0},{1,9},{9,17},{17,25},{25,1},{2,10},{10... | collective-permute-start | bytes 393224 | tf_op jit(solution)/shard_map/ppermute | solution.py:218
  3.6 1.5 %collective-permute-start.3 = (bf16[1,128,4,128]{3,2,1,0:T(4,128)(2,1)}, bf16[1,128,4,128]{3,2,1,0:T(4,128)(2,1)S(1)}, u32[]{:S(2)}, u32[]{:S(2)}) collective-permute-start(bf16[1,128,4,128]{3,2,1,0:T(4,128)(2,1)} %param.8), channel_id=1, source_target_pairs={{0,8},{8,16},{16,24},{24,0},{1,9},{9,17},{17,25},{25,1},{2,10},{10... | collective-permute-start | bytes 393224 | tf_op jit(solution)/shard_map/ppermute | solution.py:219
  5.1 2.6 %collective-permute-start = (s32[1,5]{1,0:T(1,128)}, s32[1,5]{1,0:T(1,128)S(1)}, u32[]{:S(2)}, u32[]{:S(2)}) collective-permute-start(s32[1,5]{1,0:T(1,128)} %bounds_in.1), channel_id=1, source_target_pairs={{0,4},{1,5},{2,6},{3,7},{4,0},{5,1},{6,2},{7,3},{8,12},{9,13},{10,... | collective-permute-start | bytes 68 | tf_op jit(solution)/shard_map/ppermute | solution.py:201
  7.7 2.4 %shard_map.77 = (bf16[4,1024,128]{2,1,0:T(8,128)(2,1)S(1)}, bf16[4,1024,128]{2,1,0:T(8,128)(2,1)S(1)}, bf16[256,256]{1,0:T(8,128)(2,1)S(1)}, f32[128,1024]{1,0:T...) custom-call(s32[1,5]{1,0:T(1,128)} %bounds_in.1, s32[32]{0:T(128)} %group_in.1, ...), custom_call_target="tpu_custom_call" | custom-call | tf_op jit(solution)/shard_map/pallas_call | solution.py:229
  10.1 0.0 collective-permute-done
  10.1 0.0 copy-done
  10.2 0.1 collective-permute-start.1
  10.2 0.0 collective-permute-done.2
  10.3 1.0 %shard_map.78 = (f32[4,128,1024]{2,1,0:T(8,128)S(1)}, bf16[4,128,128]{2,1,0:T(8,128)(2,1)S(1)}) custom-call(f32[128,1024]{1,0:T(8,128)S(1)} %get-tuple-element.21.bias, bf16[4,1024,128]{2,1,0:T(8,128)(2,1)S(1)} %get-tuple-element.22.query, bf16[4,128,128]{2,1,0:T(8,128)(2,1)S(1)} %get-tuple-element.23.own_key, bf16[512,128]{1,0:T(8,128)(2,1)S(1)} %bitcast.8), custom_call_target="tpu_custom_call" | custom-call | tf_op jit(solution)/shard_map/pallas_call | solution.py:269
  11.3 0.0 collective-permute-done.3
  11.3 1.2 %shard_map.79 = (bf16[4,4,160,256]{3,2,1,0:T(8,128)(2,1)S(1)}, f32[4,128,128]{2,1,0:T(8,128)S(1)}, bf16[512,128]{1,0:T(8,128)(2,1)S(1)}) custom-call(f32[4,128,1024]{2,1,0:T(8,128)S(1)} %get-tuple-element.24.probs, bf16[4,1024,128]{2,1,0:T(8,128)(2,1)S(1)} %get-tuple-element.22.query, bf16[4,1024,128]{2,1,0:T(8,128)(2,1)S(1)} %get-tuple-element.25.grad, ...), custom_call_target="tpu_custom_call" | custom-call | tf_op jit(solution)/shard_map/pallas_call | solution.py:275
  12.4 0.0 collective-permute-done.1
  12.4 1.6 %collective-permute-start.5 = (bf16[512,128]{1,0:T(8,128)(2,1)S(1)}, bf16[512,128]{1,0:T(8,128)(2,1)S(1)}, u32[]{:S(2)}, u32[]{:S(2)}) collective-permute-start(bf16[512,128]{1,0:T(8,128)(2,1)S(1)} %get-tuple-element.35), channel_id=1, source_target_pairs={{8,0},{16,8},{24,16},{0,24},{9,1},{17,9},{25,17},{1,25},{10,2},{18... | collective-permute-start | bytes 393224 | tf_op jit(solution)/shard_map/ppermute | solution.py:283
  14.1 1.6 %collective-permute-start.4 = (s32[1,5]{1,0:T(1,128)S(1)}, s32[1,5]{1,0:T(1,128)S(1)}, u32[]{:S(2)}, u32[]{:S(2)}) collective-permute-start(s32[1,5]{1,0:T(1,128)S(1)} %add.10), channel_id=1, source_target_pairs={{0,2},{1,3},{2,0},{3,1},{4,6},{5,7},{6,4},{7,5},{8,10},{9,11},{10,... | collective-permute-start | bytes 68 | tf_op jit(solution)/shard_map/ppermute | solution.py:201
  15.6 0.8 %shard_map.80 = (f32[4,1024,128]{2,1,0:T(8,128)S(1)}, f32[512,128]{1,0:T(8,128)S(1)}) custom-call(bf16[4,4,160,256]{3,2,1,0:T(8,128)(2,1)S(1)} %get-tuple-element.29.score_grad, bf16[4,128,128]{2,1,0:T(8,128)(2,1)S(1)} %get-tuple-element.23.own_key, bf16[4,128,128]{2,1,0:T(8,128)(2,1)S(1)} %get-tuple-element.30.back_key, ...), custom_call_target="tpu_custom_call" | custom-call | tf_op jit(solution)/shard_map/pallas_call | solution.py:287
  16.4 1.2 %collective-permute-done.4 = s32[1,5]{1,0:T(1,128)S(1)} collective-permute-done((s32[1,5]{1,0:T(1,128)S(1)}, s32[1,5]{1,0:T(1,128)S(1)}, u32[]{:S(2)}, u32[]{:S(2)}) %collective-permute-start.4) | collective-permute-done | bytes 52 | tf_op jit(solution)/shard_map/ppermute | solution.py:201
  17.6 1.5 %shard_map.81 = bf16[4096,128]{1,0:T(8,128)(2,1)} custom-call(s32[1,5]{1,0:T(1,128)S(1)} %add.11.count, f32[4,1024,128]{2,1,0:T(8,128)S(1)} %get-tuple-element.32.part_grad, bf16[256,256]{1,0:T(8,128)(2,1)S(1)} %get-tuple-element.33.unsort), custom_call_target="tpu_custom_call" | custom-call | tf_op jit(solution)/shard_map/pallas_call | solution.py:290
  19.1 0.0 collective-permute-done.5.back
  19.1 0.8 %shard_map.82 = bf16[512,128]{1,0:T(8,128)(2,1)} custom-call(s32[1,5]{1,0:T(1,128)S(1)} %add.11.count, f32[512,128]{1,0:T(8,128)S(1)} %get-tuple-element.34.own, bf16[512,128]{1,0:T(8,128)(2,1)S(1)} %collective-permute-done.5.back), custom_call_target="tpu_custom_call" | custom-call | tf_op jit(solution)/shard_map/pallas_call | solution.py:293
  (3 shorter events, 0.0 us)
Async XLA Ops:
  0.6 9.5 %copy-start = (s32[1,5]{1,0:T(1,128)S(1)}, s32[1,5]{1,0:T(1,128)}, u32[]{:S(2)}) copy-start(s32[1,5]{1,0:T(1,128)} %bounds_in.1) | copy-start | bytes 64
  0.6 9.6 %collective-permute-start.2 = (bf16[1,128,4,128]{3,2,1,0:T(4,128)(2,1)}, bf16[1,128,4,128]{3,2,1,0:T(4,128)(2,1)S(1)}, u32[]{:S(2)}, u32[]{:S(2)}) collective-permute-start(bf16[1,128,4,128]{3,2,1,0:T(4,128)(2,1)} %param.7), channel_id=1, source_target_pairs={{0,8},{8,16},{16,24},{24,0},{1,9},{9,17},{17,25},{25,1},{2,10},{10... | collective-permute-start | bytes 393224 | tf_op jit(solution)/shard_map/ppermute | solution.py:218
  3.6 7.6 %collective-permute-start.3 = (bf16[1,128,4,128]{3,2,1,0:T(4,128)(2,1)}, bf16[1,128,4,128]{3,2,1,0:T(4,128)(2,1)S(1)}, u32[]{:S(2)}, u32[]{:S(2)}) collective-permute-start(bf16[1,128,4,128]{3,2,1,0:T(4,128)(2,1)} %param.8), channel_id=1, source_target_pairs={{0,8},{8,16},{16,24},{24,0},{1,9},{9,17},{17,25},{25,1},{2,10},{10... | collective-permute-start | bytes 393224 | tf_op jit(solution)/shard_map/ppermute | solution.py:219
  5.1 5.0 %collective-permute-start = (s32[1,5]{1,0:T(1,128)}, s32[1,5]{1,0:T(1,128)S(1)}, u32[]{:S(2)}, u32[]{:S(2)}) collective-permute-start(s32[1,5]{1,0:T(1,128)} %bounds_in.1), channel_id=1, source_target_pairs={{0,4},{1,5},{2,6},{3,7},{4,0},{5,1},{6,2},{7,3},{8,12},{9,13},{10,... | collective-permute-start | bytes 68 | tf_op jit(solution)/shard_map/ppermute | solution.py:201
  10.2 2.3 %collective-permute-start.1 = (s32[1,5]{1,0:T(1,128)S(1)}, s32[1,5]{1,0:T(1,128)S(1)}, u32[]{:S(2)}, u32[]{:S(2)}) collective-permute-start(s32[1,5]{1,0:T(1,128)S(1)} %add.9), channel_id=1, source_target_pairs={{0,1},{1,0},{2,3},{3,2},{4,5},{5,4},{6,7},{7,6},{8,9},{9,8},{10,11... | collective-permute-start | bytes 68 | tf_op jit(solution)/shard_map/ppermute | solution.py:201
  12.4 6.7 %collective-permute-start.5 = (bf16[512,128]{1,0:T(8,128)(2,1)S(1)}, bf16[512,128]{1,0:T(8,128)(2,1)S(1)}, u32[]{:S(2)}, u32[]{:S(2)}) collective-permute-start(bf16[512,128]{1,0:T(8,128)(2,1)S(1)} %get-tuple-element.35), channel_id=1, source_target_pairs={{8,0},{16,8},{24,16},{0,24},{9,1},{17,9},{25,17},{1,25},{10,2},{18... | collective-permute-start | bytes 393224 | tf_op jit(solution)/shard_map/ppermute | solution.py:283
  14.1 3.5 %collective-permute-start.4 = (s32[1,5]{1,0:T(1,128)S(1)}, s32[1,5]{1,0:T(1,128)S(1)}, u32[]{:S(2)}, u32[]{:S(2)}) collective-permute-start(s32[1,5]{1,0:T(1,128)S(1)} %add.10), channel_id=1, source_target_pairs={{0,2},{1,3},{2,0},{3,1},{4,6},{5,7},{6,4},{7,5},{8,10},{9,11},{10,... | collective-permute-start | bytes 68 | tf_op jit(solution)/shard_map/ppermute | solution.py:201

commit v4 on v3

--- a/solution.py
+++ b/solution.py
@@ -30,55 +30,50 @@
         out[g] = flat[pl.ds(g, rows, stride=groups), :].astype(BF16)
 
 
-def arrange_kernel(sizes, bounds_in, group_in, query_in, grad_in, key_in, value_in, sorted_query, sorted_grad, unsort, bias, own_key, own_value, bounds, group, query, grad, key, value, flat, sems):
+def place_kernel(sizes, places):
+    tok, heads, groups, per = sizes
+    shape = (tok, tok * per)
+    col = lax.broadcasted_iota(jnp.int32, shape, 0)
+    row = lax.broadcasted_iota(jnp.int32, shape, 1) // per
+    places[...] = col - jnp.where(col > row, tok, 0)
+
+
+def plan_kernel(sizes, bounds, group, places, sort, unsort, bias):
     tok, heads, groups, per = sizes
     step = BLOCK // heads
     share = step * per
-    depth = query.shape[1]
-    copies = [
-        pltpu.make_async_copy(a, b, sems.at[i])
-        for i, (a, b) in enumerate(
-            [(group_in, group), (bounds_in, bounds), (query_in, query), (grad_in, grad), (key_in, key), (value_in, value)]
-        )
-    ]
-    for copy in copies:
-        copy.start()
-    copies[0].wait()
-    lanes = lax.broadcasted_iota(jnp.int32, (8, BLOCK), 1)
-    head = lanes % heads
-    seen = [jnp.int32(0)] * groups
-    target = (lanes // heads) * per
-    for h in range(heads):
-        mine = group[h]
-        slot = mine * share
-        for g in range(groups):
-            here = mine == g
-            slot = slot + jnp.where(here, seen[g], 0)
-            seen[g] = seen[g] + jnp.where(here, 1, 0)
-        target = target + jnp.where(head == h, slot, 0)
+    first = lax.broadcasted_iota(jnp.int32, (heads, heads), 0)
+    second = lax.broadcasted_iota(jnp.int32, (heads, heads), 1)
+    along = jnp.broadcast_to(group[...], (heads, heads))
+    down = jnp.sum(jnp.where(first == second, along, 0), axis=1, keepdims=True)
+    earlier = (first < second) & (down == along)
+    slot = group[...] * share + jnp.sum(jnp.where(earlier, 1, 0), axis=0, keepdims=True)
+    target = jnp.concatenate([slot + i * per for i in range(step)], axis=1)
     rows = lax.broadcasted_iota(jnp.int32, (BLOCK, BLOCK), 0)
-    sort = jnp.where(rows == target[:1], 1.0, 0.0).astype(F32)
-    unsort[...] = sort.T.astype(BF16)
-    sort = sort.astype(BF16)
-    copies[1].wait()
+    moves = jnp.where(rows == target, 1.0, 0.0).astype(F32)
+    unsort[...] = moves.T.astype(BF16)
+    sort[...] = moves.astype(BF16)
     start = lax.axis_index("ctx") * tok
     row = lax.broadcasted_iota(jnp.int32, (8, tok * per), 1) // per
     place = row + start
     low = jnp.zeros_like(place)
     last = bounds.shape[1] - 1
     for i in range(1, last):
-        low = jnp.where(place >= bounds[0, i], bounds[0, i], low)
-    low = jnp.where(place >= bounds[0, last], jnp.int32(1 << 30), low) - start
+        low = jnp.where(place >= bounds[:, i : i + 1], bounds[:, i : i + 1], low)
+    low = jnp.where(place >= bounds[:, last : last + 1], jnp.int32(1 << 30), low) - start
     for c in range(0, tok, 8):
-        col = c + lax.broadcasted_iota(jnp.int32, (8, tok * per), 0)
-        where = col - jnp.where(col > row, tok, 0)
-        bias[c : c + 8, :] = jnp.where(where >= low, 0.0, -1e30).astype(F32)
-    for copy in copies[2:]:
-        copy.wait()
+        bias[c : c + 8, :] = jnp.where(places[c : c + 8, :] >= low, 0.0, -1e30).astype(F32)
+
+
+def arrange_kernel(sizes, sort, query, grad, key, value, sorted_query, sorted_grad, own_key, own_value, flat):
+    tok, heads, groups, per = sizes
+    step = BLOCK // heads
+    share = step * per
+    depth = query.shape[1]
     for b in range(tok // step):
         part = slice(b * BLOCK, (b + 1) * BLOCK)
         both = jnp.concatenate([query[part, :], grad[part, :]], axis=1)
-        both = dot(sort, both).astype(BF16)
+        both = dot(sort[...], both).astype(BF16)
         for g in range(groups):
             sorted_query[g, b * share : (b + 1) * share, :] = both[g * share : (g + 1) * share, :depth]
             sorted_grad[g, b * share : (b + 1) * share, :] = both[g * share : (g + 1) * share, depth:]
@@ -183,16 +178,16 @@
 
 
 VMEM = pl.BlockSpec(memory_space=pltpu.VMEM)
-HBM = pl.BlockSpec(memory_space=pltpu.HBM)
-
-
-def call(kernel, ins, outs, scratch=()):
+
+
+def call(kernel, ins, outs, scratch=(), flops=None):
     return pl.pallas_call(
         kernel,
         out_shape=[jax.ShapeDtypeStruct(shape, dtype) for shape, dtype in outs],
         in_specs=ins,
         out_specs=[VMEM] * len(outs),
         scratch_shapes=list(scratch),
+        cost_estimate=None if flops is None else pl.CostEstimate(flops=flops, bytes_accessed=0, transcendentals=0),
         compiler_params=pltpu.CompilerParams(vmem_limit_bytes=32 * 1024 * 1024),
     )
 
@@ -226,42 +221,26 @@
     packed = (tok * groups, depth)
     split = (groups, tok, depth)
     here = BLOCK // per
-    sorted_query, sorted_grad, unsort, bias, own_key, own_value = call(
+    (places,) = call(functools.partial(place_kernel, sizes), [], [((tok, tok * per), jnp.int32)], flops=1_000_000_000)()
+    sort, unsort, bias = call(
+        functools.partial(plan_kernel, sizes),
+        [VMEM] * 3,
+        [((BLOCK, BLOCK), BF16), ((BLOCK, BLOCK), BF16), ((tok, tok * per), F32)],
+    )(offsets, query_head_group.reshape(1, heads), places)
+    sorted_query, sorted_grad, own_key, own_value = call(
         functools.partial(arrange_kernel, sizes),
-        [HBM] * 6,
-        [
-            (sorted_shape, BF16),
-            (sorted_shape, BF16),
-            ((BLOCK, BLOCK), BF16),
-            ((tok, tok * per), F32),
-            (split, BF16),
-            (split, BF16),
-        ],
-        [
-            pltpu.SMEM(offsets.shape, jnp.int32),
-            pltpu.SMEM((heads,), jnp.int32),
-            pltpu.VMEM((tok * heads, depth), BF16),
-            pltpu.VMEM((tok * heads, depth), BF16),
-            pltpu.VMEM(packed, BF16),
-            pltpu.VMEM(packed, BF16),
-            pltpu.VMEM(packed, F32),
-            pltpu.SemaphoreType.DMA((6,)),
-        ],
+        [VMEM] * 5,
+        [(sorted_shape, BF16), (sorted_shape, BF16), (split, BF16), (split, BF16)],
+        [pltpu.VMEM(packed, F32)],
     )(
-        *[
-            pltpu.with_memory_space_constraint(x, pltpu.HBM)
-            for x in (
-                offsets,
-                query_head_group,
-                query_rows.reshape(tok * heads, depth),
-                out_grad.reshape(tok * heads, depth),
-                key_rows.reshape(packed),
-                value_matrix.reshape(packed),
-            )
-        ]
+        sort,
+        query_rows.reshape(tok * heads, depth),
+        out_grad.reshape(tok * heads, depth),
+        key_rows.reshape(packed),
+        value_matrix.reshape(packed),
     )
 
-    count, unsort = lax.optimization_barrier((count, unsort))
+    count, sorted_query = lax.optimization_barrier((count, sorted_query))
     for hop in hops[2:-1]:
         count = add_partner(count, "dp", hop)
     moved = partner(count, "dp", 1) if paired else count

time: 20 us -> 20.1 us (level)
  Pallas kernels: 7.59 us -> 6.33 us
  waiting for transfers between devices: 1.2 us -> 2.34 us
    pallas_call x1 -> x3, Pallas kernels: 2.41 us -> 1.14 us  [the longest x1 0.75 us: per_device(): call(functools.partial(arrange_kernel, sizes), [VMEM] * 5, [(sorted_shape...]
    ppermute x3, waiting for transfers between devices: 1.19 us -> 1.95 us  [partner(): lax.ppermute(value, axis, [(i, i ^ hop) for i in range(lax.axis_size(axis...]
    ppermute x1, waiting for transfers between devices: 0.01 us -> 0.38 us  [per_device(): lax.ppermute(value_matrix, 'ctx', ahead).reshape(tok * groups, depth)]
  transfers between devices with their start and end apart: 6 -> 6, of which waited for: 1 -> 3; matrix products, arithmetic and copies ran while one was open for 0% -> 0% of each run, Pallas kernels for 34% -> 28%
where the time goes in v4:
time: 20.1 us; the launch traced here: 19.9 us
  starting transfers between devices  10.5 us (52%)
  Pallas kernels  6.33 us (31%)
  waiting for transfers between devices  2.34 us (12%)
  between operations  0.78 us (4%)
    ppermute x3, starting transfers between devices, partner(): lax.ppermute(value, axis, [(i, i ^ hop) for i in range(lax.axis_size(axis...  4.17 us
    ppermute x1, starting transfers between devices, per_device(): back_key = lax.ppermute(key_rows, 'ctx', ahead).reshape(tok * groups, depth)  2.99 us
    ppermute x3, waiting for transfers between devices, partner(): lax.ppermute(value, axis, [(i, i ^ hop) for i in range(lax.axis_size(axis...  1.95 us
    ppermute x1, starting transfers between devices, per_device(): back = lax.ppermute(back, 'ctx', behind)  1.8 us
    pallas_call x1, Pallas kernels, per_device(): call(functools.partial(unsort_kernel, sizes, tokens), [VMEM] * 3, [((tok...  1.51 us
    ppermute x1, starting transfers between devices, per_device(): lax.ppermute(value_matrix, 'ctx', ahead).reshape(tok * groups, depth)  1.49 us
    pallas_call x1, Pallas kernels, per_device(): call(functools.partial(score_kernel, sizes), [VMEM] * 5, [((groups, tok /...  1.15 us
    pallas_call x1, Pallas kernels, per_device(): call(functools.partial(probs_kernel, sizes), [VMEM] * 4, [((groups, tok,...  1 us
  transfers between devices with their start and end apart: 6, of which 3 were waited for; matrix products, arithmetic and copies ran while one was open for 0% of the time, Pallas kernels for 28%

profile of v4, /device:TPU:0, one launch (start us, length us, event | category | flops | bytes accessed | tf_op | source)
XLA Modules:
  0.0 19.9 jit_solution(11483073545298485482)
XLA Ops:
  0.6 0.0 copy-start.2
  0.6 0.0 copy-start.3
  0.7 0.0 copy-start.5
  0.7 0.0 copy-start.4
  0.7 0.0 copy-start
  0.7 3.0 %collective-permute-start.2 = (bf16[1,128,4,128]{3,2,1,0:T(4,128)(2,1)}, bf16[1,128,4,128]{3,2,1,0:T(4,128)(2,1)S(1)}, u32[]{:S(2)}, u32[]{:S(2)}) collective-permute-start(bf16[1,128,4,128]{3,2,1,0:T(4,128)(2,1)} %param.7), channel_id=1, source_target_pairs={{0,8},{8,16},{16,24},{24,0},{1,9},{9,17},{17,25},{25,1},{2,10},{10... | collective-permute-start | bytes 393224 | tf_op jit(solution)/shard_map/ppermute | solution.py:213
  3.7 1.5 %collective-permute-start.3 = (bf16[1,128,4,128]{3,2,1,0:T(4,128)(2,1)}, bf16[1,128,4,128]{3,2,1,0:T(4,128)(2,1)S(1)}, u32[]{:S(2)}, u32[]{:S(2)}) collective-permute-start(bf16[1,128,4,128]{3,2,1,0:T(4,128)(2,1)} %param.8), channel_id=1, source_target_pairs={{0,8},{8,16},{16,24},{24,0},{1,9},{9,17},{17,25},{25,1},{2,10},{10... | collective-permute-start | bytes 393224 | tf_op jit(solution)/shard_map/ppermute | solution.py:214
  5.2 2.6 %collective-permute-start = (s32[1,5]{1,0:T(1,128)}, s32[1,5]{1,0:T(1,128)S(1)}, u32[]{:S(2)}, u32[]{:S(2)}) collective-permute-start(s32[1,5]{1,0:T(1,128)} %bounds.1), channel_id=1, source_target_pairs={{0,4},{1,5},{2,6},{3,7},{4,0},{5,1},{6,2},{7,3},{8,12},{9,13},{10,... | collective-permute-start | bytes 68 | tf_op jit(solution)/shard_map/ppermute | solution.py:196
  7.8 0.4 %shard_map.78 = (bf16[256,256]{1,0:T(8,128)(2,1)S(1)}, bf16[256,256]{1,0:T(8,128)(2,1)S(1)}, f32[128,1024]{1,0:T(8,128)S(1)}) custom-call(s32[1,5]{1,0:T(1,128)S(1)} %copy-done.5, s32[1,32]{1,0:T(1,128)S(1)} %bitcast.15, s32[128,1024]{1,0:T(8,128)S(1)} %shard_map.77.places), custom_call_target="tpu_custom_call" | custom-call | tf_op jit(solution)/shard_map/pallas_call | solution.py:225
  8.2 0.8 %shard_map.79 = (bf16[4,1024,128]{2,1,0:T(8,128)(2,1)S(1)}, bf16[4,1024,128]{2,1,0:T(8,128)(2,1)S(1)}, bf16[4,128,128]{2,1,0:T(8,128)(2,1)S(1)}, bf16[4,128,128]{2,1,0:T(8,128)(2,1)S(1)}) custom-call(bf16[256,256]{1,0:T(8,128)(2,1)S(1)} %get-tuple-element.20.sort, bf16[4096,128]{1,0:T(8,128)(2,1)S(1)} %bitcast.9, bf16[4096,128]{1,0:T(8,128)(2,1)S(1)} %bitcast.10, ...), custom_call_target="tpu_custom_call" | custom-call | tf_op jit(solution)/shard_map/pallas_call | solution.py:230
  9.0 0.8 %collective-permute-done = s32[1,5]{1,0:T(1,128)S(1)} collective-permute-done((s32[1,5]{1,0:T(1,128)}, s32[1,5]{1,0:T(1,128)S(1)}, u32[]{:S(2)}, u32[]{:S(2)}) %collective-permute-start) | collective-permute-done | bytes 52 | tf_op jit(solution)/shard_map/ppermute | solution.py:196
  9.8 0.0 collective-permute-start.1
  9.8 0.0 collective-permute-done.2
  9.8 1.0 %shard_map.80 = (f32[4,128,1024]{2,1,0:T(8,128)S(1)}, bf16[4,128,128]{2,1,0:T(8,128)(2,1)S(1)}) custom-call(f32[128,1024]{1,0:T(8,128)S(1)} %get-tuple-element.23.bias, bf16[4,1024,128]{2,1,0:T(8,128)(2,1)S(1)} %get-tuple-element.24.query, bf16[4,128,128]{2,1,0:T(8,128)(2,1)S(1)} %get-tuple-element.25.own_key, bf16[512,128]{1,0:T(8,128)(2,1)S(1)} %bitcast.11), custom_call_target="tpu_custom_call" | custom-call | tf_op jit(solution)/shard_map/pallas_call | solution.py:248
  10.8 0.4 %collective-permute-done.3 = bf16[1,128,4,128]{3,2,1,0:T(4,128)(2,1)S(1)} collective-permute-done((bf16[1,128,4,128]{3,2,1,0:T(4,128)(2,1)}, bf16[1,128,4,128]{3,2,1,0:T(4,128)(2,1)S(1)}, u32[]{:S(2)}, u32[]{:S(2)}) %collective-permute-start.3) | collective-permute-done | bytes 131104 | tf_op jit(solution)/shard_map/ppermute | solution.py:214
  11.2 1.1 %shard_map.81 = (bf16[4,4,160,256]{3,2,1,0:T(8,128)(2,1)S(1)}, f32[4,128,128]{2,1,0:T(8,128)S(1)}, bf16[512,128]{1,0:T(8,128)(2,1)S(1)}) custom-call(f32[4,128,1024]{2,1,0:T(8,128)S(1)} %get-tuple-element.26.probs, bf16[4,1024,128]{2,1,0:T(8,128)(2,1)S(1)} %get-tuple-element.24.query, bf16[4,1024,128]{2,1,0:T(8,128)(2,1)S(1)} %get-tuple-element.27.grad, ...), custom_call_target="tpu_custom_call" | custom-call | tf_op jit(solution)/shard_map/pallas_call | solution.py:254
  12.3 0.0 collective-permute-done.1
  12.3 1.8 %collective-permute-start.5 = (bf16[512,128]{1,0:T(8,128)(2,1)S(1)}, bf16[512,128]{1,0:T(8,128)(2,1)S(1)}, u32[]{:S(2)}, u32[]{:S(2)}) collective-permute-start(bf16[512,128]{1,0:T(8,128)(2,1)S(1)} %get-tuple-element.37), channel_id=1, source_target_pairs={{8,0},{16,8},{24,16},{0,24},{9,1},{17,9},{25,17},{1,25},{10,2},{18... | collective-permute-start | bytes 393224 | tf_op jit(solution)/shard_map/ppermute | solution.py:262
  14.1 1.6 %collective-permute-start.4 = (s32[1,5]{1,0:T(1,128)S(1)}, s32[1,5]{1,0:T(1,128)S(1)}, u32[]{:S(2)}, u32[]{:S(2)}) collective-permute-start(s32[1,5]{1,0:T(1,128)S(1)} %add.10), channel_id=1, source_target_pairs={{0,2},{1,3},{2,0},{3,1},{4,6},{5,7},{6,4},{7,5},{8,10},{9,11},{10,... | collective-permute-start | bytes 68 | tf_op jit(solution)/shard_map/ppermute | solution.py:196
  15.7 0.8 %shard_map.82 = (f32[4,1024,128]{2,1,0:T(8,128)S(1)}, f32[512,128]{1,0:T(8,128)S(1)}) custom-call(bf16[4,4,160,256]{3,2,1,0:T(8,128)(2,1)S(1)} %get-tuple-element.31.score_grad, bf16[4,128,128]{2,1,0:T(8,128)(2,1)S(1)} %get-tuple-element.25.own_key, bf16[4,128,128]{2,1,0:T(8,128)(2,1)S(1)} %get-tuple-element.32.back_key, ...), custom_call_target="tpu_custom_call" | custom-call | tf_op jit(solution)/shard_map/pallas_call | solution.py:266
  16.5 1.2 %collective-permute-done.4 = s32[1,5]{1,0:T(1,128)S(1)} collective-permute-done((s32[1,5]{1,0:T(1,128)S(1)}, s32[1,5]{1,0:T(1,128)S(1)}, u32[]{:S(2)}, u32[]{:S(2)}) %collective-permute-start.4) | collective-permute-done | bytes 52 | tf_op jit(solution)/shard_map/ppermute | solution.py:196
  17.7 1.5 %shard_map.83 = bf16[4096,128]{1,0:T(8,128)(2,1)} custom-call(s32[1,5]{1,0:T(1,128)S(1)} %add.11.count, f32[4,1024,128]{2,1,0:T(8,128)S(1)} %get-tuple-element.34.part_grad, bf16[256,256]{1,0:T(8,128)(2,1)S(1)} %get-tuple-element.35.unsort), custom_call_target="tpu_custom_call" | custom-call | tf_op jit(solution)/shard_map/pallas_call | solution.py:269
  19.2 0.0 collective-permute-done.5.back
  19.2 0.8 %shard_map.84 = bf16[512,128]{1,0:T(8,128)(2,1)} custom-call(s32[1,5]{1,0:T(1,128)S(1)} %add.11.count, f32[512,128]{1,0:T(8,128)S(1)} %get-tuple-element.36.own, bf16[512,128]{1,0:T(8,128)(2,1)S(1)} %collective-permute-done.5.back), custom_call_target="tpu_custom_call" | custom-call | tf_op jit(solution)/shard_map/pallas_call | solution.py:272
  (11 shorter events, 0.1 us)
Async XLA Ops:
  0.6 7.6 %copy-start.2 = (bf16[1,128,4,128]{3,2,1,0:T(4,128)(2,1)S(1)}, bf16[1,128,4,128]{3,2,1,0:T(4,128)(2,1)}, u32[]{:S(2)}) copy-start(bf16[1,128,4,128]{3,2,1,0:T(4,128)(2,1)} %param.7) | copy-start | bytes 393220
  0.6 7.6 %copy-start.3 = (bf16[1,128,4,128]{3,2,1,0:T(4,128)(2,1)S(1)}, bf16[1,128,4,128]{3,2,1,0:T(4,128)(2,1)}, u32[]{:S(2)}) copy-start(bf16[1,128,4,128]{3,2,1,0:T(4,128)(2,1)} %param.8) | copy-start | bytes 393220
  0.7 7.2 %copy-start.5 = (s32[1,5]{1,0:T(1,128)S(1)}, s32[1,5]{1,0:T(1,128)}, u32[]{:S(2)}) copy-start(s32[1,5]{1,0:T(1,128)} %bounds.1) | copy-start | bytes 64
  0.7 7.2 %copy-start.4 = (s32[32]{0:T(128)S(1)}, s32[32]{0:T(128)}, u32[]{:S(2)}) copy-start(s32[32]{0:T(128)} %param.11) | copy-start | bytes 388
  0.7 7.5 %copy-start = (bf16[1,128,32,128]{3,2,1,0:T(8,128)(2,1)S(1)}, bf16[1,128,32,128]{3,2,1,0:T(8,128)(2,1)}, u32[]{:S(2)}) copy-start(bf16[1,128,32,128]{3,2,1,0:T(8,128)(2,1)} %param.6) | copy-start | bytes 3145732
  0.7 7.5 %copy-start.1 = (bf16[1,128,32,128]{3,2,1,0:T(8,128)(2,1)S(1)}, bf16[1,128,32,128]{3,2,1,0:T(8,128)(2,1)}, u32[]{:S(2)}) copy-start(bf16[1,128,32,128]{3,2,1,0:T(8,128)(2,1)} %param.9) | copy-start | bytes 3145732
  0.7 9.1 %collective-permute-start.2 = (bf16[1,128,4,128]{3,2,1,0:T(4,128)(2,1)}, bf16[1,128,4,128]{3,2,1,0:T(4,128)(2,1)S(1)}, u32[]{:S(2)}, u32[]{:S(2)}) collective-permute-start(bf16[1,128,4,128]{3,2,1,0:T(4,128)(2,1)} %param.7), channel_id=1, source_target_pairs={{0,8},{8,16},{16,24},{24,0},{1,9},{9,17},{17,25},{25,1},{2,10},{10... | collective-permute-start | bytes 393224 | tf_op jit(solution)/shard_map/ppermute | solution.py:213
  3.7 7.5 %collective-permute-start.3 = (bf16[1,128,4,128]{3,2,1,0:T(4,128)(2,1)}, bf16[1,128,4,128]{3,2,1,0:T(4,128)(2,1)S(1)}, u32[]{:S(2)}, u32[]{:S(2)}) collective-permute-start(bf16[1,128,4,128]{3,2,1,0:T(4,128)(2,1)} %param.8), channel_id=1, source_target_pairs={{0,8},{8,16},{16,24},{24,0},{1,9},{9,17},{17,25},{25,1},{2,10},{10... | collective-permute-start | bytes 393224 | tf_op jit(solution)/shard_map/ppermute | solution.py:214
  5.2 4.6 %collective-permute-start = (s32[1,5]{1,0:T(1,128)}, s32[1,5]{1,0:T(1,128)S(1)}, u32[]{:S(2)}, u32[]{:S(2)}) collective-permute-start(s32[1,5]{1,0:T(1,128)} %bounds.1), channel_id=1, source_target_pairs={{0,4},{1,5},{2,6},{3,7},{4,0},{5,1},{6,2},{7,3},{8,12},{9,13},{10,... | collective-permute-start | bytes 68 | tf_op jit(solution)/shard_map/ppermute | solution.py:196
  9.8 2.6 %collective-permute-start.1 = (s32[1,5]{1,0:T(1,128)S(1)}, s32[1,5]{1,0:T(1,128)S(1)}, u32[]{:S(2)}, u32[]{:S(2)}) collective-permute-start(s32[1,5]{1,0:T(1,128)S(1)} %add.9), channel_id=1, source_target_pairs={{0,1},{1,0},{2,3},{3,2},{4,5},{5,4},{6,7},{7,6},{8,9},{9,8},{10,11... | collective-permute-start | bytes 68 | tf_op jit(solution)/shard_map/ppermute | solution.py:196
  12.3 6.9 %collective-permute-start.5 = (bf16[512,128]{1,0:T(8,128)(2,1)S(1)}, bf16[512,128]{1,0:T(8,128)(2,1)S(1)}, u32[]{:S(2)}, u32[]{:S(2)}) collective-permute-start(bf16[512,128]{1,0:T(8,128)(2,1)S(1)} %get-tuple-element.37), channel_id=1, source_target_pairs={{8,0},{16,8},{24,16},{0,24},{9,1},{17,9},{25,17},{1,25},{10,2},{18... | collective-permute-start | bytes 393224 | tf_op jit(solution)/shard_map/ppermute | solution.py:262
  14.1 3.5 %collective-permute-start.4 = (s32[1,5]{1,0:T(1,128)S(1)}, s32[1,5]{1,0:T(1,128)S(1)}, u32[]{:S(2)}, u32[]{:S(2)}) collective-permute-start(s32[1,5]{1,0:T(1,128)S(1)} %add.10), channel_id=1, source_target_pairs={{0,2},{1,3},{2,0},{3,1},{4,6},{5,7},{6,4},{7,5},{8,10},{9,11},{10,... | collective-permute-start | bytes 68 | tf_op jit(solution)/shard_map/ppermute | solution.py:196

commit v5 on v4

--- a/solution.py
+++ b/solution.py
@@ -13,6 +13,7 @@
 TN = (((0,), (0,)), ((), ()))
 F32, BF16 = jnp.float32, jnp.bfloat16
 BLOCK = 256
+PIECES = 2
 
 
 def dot(a, b, dims=NN):
@@ -90,8 +91,8 @@
 def product(left, right, g, t, rows, own):
     here, tok = own.shape[0], left.shape[1]
     lo, hi = t * here, (t + 1) * here
-    a, b = dot(left[g, :hi], rows, NT), dot(right[g, lo:], rows, NT)
-    return stack((a, 0, lo), (jnp.where(own, a[lo:], b[:here]), 0, here), (b, here, tok - lo))
+    both = dot(jnp.concatenate([left[g, :hi], right[g, lo:]], axis=0), rows, NT)
+    return stack((both, 0, lo), (jnp.where(own, both[lo:hi], both[hi : hi + here]), 0, here), (both, hi + here, tok + here))
 
 
 def probs_kernel(sizes, bias, query, own_key, back_in, probs, back_key, flat):
@@ -145,47 +146,56 @@
     return (tokens / count[0:1, last : last + 1].astype(F32)) * (1.0 / math.sqrt(depth))
 
 
-def query_kernel(sizes, score_grad, own_key, back_key, own_grad, part_grad, key_grad):
-    tok, heads, groups, per = sizes
+def query_kernel(sizes, score_grad, own_key, back_key, own_grad, unsort, query_grad, key_grad, part_grad):
+    tok, heads, groups, per = sizes
+    depth = own_key.shape[2]
+    step = BLOCK // heads
+    share = step * per
     here = BLOCK // per
     for g in range(groups):
         for t in range(tok // here):
             keys = jnp.concatenate([own_key[g, : (t + 1) * here], back_key[g, t * here :]], axis=0)
             part_grad[g, t * BLOCK : (t + 1) * BLOCK, :] = dot(score_grad[g, t], keys, TN)
         key_grad[pl.ds(g, tok, stride=groups), :] = own_grad[g]
-
-
-def unsort_kernel(sizes, tokens, count, part_grad, unsort, query_grad):
-    tok, heads, groups, per = sizes
-    depth = part_grad.shape[2]
-    factor = factor_of(count, tokens, depth)
-    step = BLOCK // heads
-    share = step * per
     for b in range(0, tok // step, 2):
         both = [
             jnp.concatenate([part_grad[g, (b + i) * share : (b + i + 1) * share, :] for g in range(groups)], axis=0)
             for i in range(2)
         ]
-        both = (jnp.concatenate(both, axis=1) * factor).astype(BF16)
-        both = dot(unsort[...], both).astype(BF16)
+        both = jnp.concatenate(both, axis=1)
+        high = both.astype(BF16)
+        low = (both - high.astype(F32)).astype(BF16)
+        both = dot(unsort[...], high) + dot(unsort[...], low)
         query_grad[b * BLOCK : (b + 1) * BLOCK, :] = both[:, :depth]
         query_grad[(b + 1) * BLOCK : (b + 2) * BLOCK, :] = both[:, depth:]
 
 
-def key_kernel(tokens, count, own, back, key_grad):
-    factor = factor_of(count, tokens, own.shape[1])
+def scale_kernel(tokens, count, query_in, own, back, query_out, key_out, query_grad, key_grad, sems):
+    rows, depth = query_in.shape
+    last = count.shape[1] - 1
+    factor = (tokens / count[0:1, last : last + 1].astype(F32)) * (1.0 / math.sqrt(depth))
     key_grad[...] = ((own[...] + back[...].astype(F32)) * factor).astype(BF16)
+    copies = [pltpu.make_async_copy(key_grad, key_out, sems.at[0])]
+    copies[0].start()
+    for i in range(PIECES):
+        part = pl.ds(i * (rows // PIECES), rows // PIECES)
+        query_grad[part, :] = (query_in[part, :] * factor).astype(BF16)
+        copies.append(pltpu.make_async_copy(query_grad.at[part], query_out.at[part], sems.at[1 + i]))
+        copies[-1].start()
+    for copy in copies:
+        copy.wait()
 
 
 VMEM = pl.BlockSpec(memory_space=pltpu.VMEM)
-
-
-def call(kernel, ins, outs, scratch=(), flops=None):
+HBM = pl.BlockSpec(memory_space=pltpu.HBM)
+
+
+def call(kernel, ins, outs, scratch=(), flops=None, out_spec=VMEM):
     return pl.pallas_call(
         kernel,
         out_shape=[jax.ShapeDtypeStruct(shape, dtype) for shape, dtype in outs],
         in_specs=ins,
-        out_specs=[VMEM] * len(outs),
+        out_specs=[out_spec] * len(outs),
         scratch_shapes=list(scratch),
         cost_estimate=None if flops is None else pl.CostEstimate(flops=flops, bytes_accessed=0, transcendentals=0),
         compiler_params=pltpu.CompilerParams(vmem_limit_bytes=32 * 1024 * 1024),
@@ -263,15 +273,23 @@
     if paired:
         count = add_partner(count + moved, "dp", 2)
 
-    part_grad, own = call(
-        functools.partial(query_kernel, sizes), [VMEM] * 4, [(sorted_shape, F32), (packed, F32)]
-    )(score_grad, own_key, back_key, own)
-    (query_grad,) = call(
-        functools.partial(unsort_kernel, sizes, tokens), [VMEM] * 3, [((tok * heads, depth), BF16)]
-    )(count, part_grad, unsort)
-    (key_grad,) = call(
-        functools.partial(key_kernel, tokens), [VMEM] * 3, [((tok * groups, depth), BF16)]
-    )(count, own, back)
+    plain_grad, own = call(
+        functools.partial(query_kernel, sizes),
+        [VMEM] * 5,
+        [((tok * heads, depth), F32), (packed, F32)],
+        [pltpu.VMEM(sorted_shape, F32)],
+    )(score_grad, own_key, back_key, own, unsort)
+    query_grad, key_grad = call(
+        functools.partial(scale_kernel, tokens),
+        [VMEM] * 4,
+        [((tok * heads, depth), BF16), (packed, BF16)],
+        [
+            pltpu.VMEM((tok * heads, depth), BF16),
+            pltpu.VMEM(packed, BF16),
+            pltpu.SemaphoreType.DMA((1 + PIECES,)),
+        ],
+        out_spec=HBM,
+    )(count, plain_grad, own, back)
     return (query_grad.reshape(query_rows.shape), key_grad.reshape(key_rows.shape))
 
 

time: 20.1 us -> 19.1 us (0.950)
  Pallas kernels: 6.33 us -> 5.67 us
  waiting for transfers between devices: 2.34 us -> 2 us
    ppermute x3, waiting for transfers between devices: 1.95 us -> 1.37 us  [partner(): lax.ppermute(value, axis, [(i, i ^ hop) for i in range(lax.axis_size(axis...]
    pallas_call x3 -> x2, Pallas kernels: 3.04 us -> 2.55 us  [the longest x1 1.36 us: per_device(): call(functools.partial(query_kernel, sizes), [VMEM] * 5, [((tok * heads,...]
    ppermute x1, waiting for transfers between devices: 0.01 us -> 0.27 us  [per_device(): back = lax.ppermute(back, 'ctx', behind)]
  transfers between devices with their start and end apart: 6 -> 6, of which waited for: 3 -> 4; matrix products, arithmetic and copies ran while one was open for 0% -> 0% of each run, Pallas kernels for 28% -> 24%
where the time goes in v5:
time: 19.1 us; the launch traced here: 18.9 us
  starting transfers between devices  10.4 us (54%)
  Pallas kernels  5.67 us (30%)
  waiting for transfers between devices  2 us (10%)
  between operations  0.78 us (4%)
    ppermute x3, starting transfers between devices, partner(): lax.ppermute(value, axis, [(i, i ^ hop) for i in range(lax.axis_size(axis...  4.17 us
    ppermute x1, starting transfers between devices, per_device(): back_key = lax.ppermute(key_rows, 'ctx', ahead).reshape(tok * groups, depth)  2.99 us
    ppermute x1, starting transfers between devices, per_device(): back = lax.ppermute(back, 'ctx', behind)  1.79 us
    ppermute x1, starting transfers between devices, per_device(): lax.ppermute(value_matrix, 'ctx', ahead).reshape(tok * groups, depth)  1.49 us
    ppermute x3, waiting for transfers between devices, partner(): lax.ppermute(value, axis, [(i, i ^ hop) for i in range(lax.axis_size(axis...  1.37 us
    pallas_call x1, Pallas kernels, per_device(): call(functools.partial(query_kernel, sizes), [VMEM] * 5, [((tok * heads,...  1.36 us
    pallas_call x1, Pallas kernels, per_device(): call(functools.partial(scale_kernel, tokens), [VMEM] * 4, [((tok * heads,...  1.19 us
    pallas_call x1, Pallas kernels, per_device(): call(functools.partial(probs_kernel, sizes), [VMEM] * 4, [((groups, tok,...  1.02 us
  transfers between devices with their start and end apart: 6, of which 4 were waited for; matrix products, arithmetic and copies ran while one was open for 0% of the time, Pallas kernels for 24%

profile of v5, /device:TPU:0, one launch (start us, length us, event | category | flops | bytes accessed | tf_op | source)
XLA Modules:
  0.0 18.9 jit_solution(10908344290774859876)
XLA Ops:
  0.6 0.0 copy-start.2
  0.6 0.0 copy-start.3
  0.7 0.0 copy-start.5
  0.7 0.0 copy-start.4
  0.7 3.0 %collective-permute-start.2 = (bf16[1,128,4,128]{3,2,1,0:T(4,128)(2,1)}, bf16[1,128,4,128]{3,2,1,0:T(4,128)(2,1)S(1)}, u32[]{:S(2)}, u32[]{:S(2)}) collective-permute-start(bf16[1,128,4,128]{3,2,1,0:T(4,128)(2,1)} %param.7), channel_id=1, source_target_pairs={{0,8},{8,16},{16,24},{24,0},{1,9},{9,17},{17,25},{25,1},{2,10},{10... | collective-permute-start | bytes 393224 | tf_op jit(solution)/shard_map/ppermute | solution.py:223
  3.7 1.5 %collective-permute-start.3 = (bf16[1,128,4,128]{3,2,1,0:T(4,128)(2,1)}, bf16[1,128,4,128]{3,2,1,0:T(4,128)(2,1)S(1)}, u32[]{:S(2)}, u32[]{:S(2)}) collective-permute-start(bf16[1,128,4,128]{3,2,1,0:T(4,128)(2,1)} %param.8), channel_id=1, source_target_pairs={{0,8},{8,16},{16,24},{24,0},{1,9},{9,17},{17,25},{25,1},{2,10},{10... | collective-permute-start | bytes 393224 | tf_op jit(solution)/shard_map/ppermute | solution.py:224
  5.2 2.6 %collective-permute-start = (s32[1,5]{1,0:T(1,128)}, s32[1,5]{1,0:T(1,128)S(1)}, u32[]{:S(2)}, u32[]{:S(2)}) collective-permute-start(s32[1,5]{1,0:T(1,128)} %bounds.1), channel_id=1, source_target_pairs={{0,4},{1,5},{2,6},{3,7},{4,0},{5,1},{6,2},{7,3},{8,12},{9,13},{10,... | collective-permute-start | bytes 68 | tf_op jit(solution)/shard_map/ppermute | solution.py:206
  7.8 0.0 copy-done.5
  7.8 0.0 copy-done.4
  7.8 0.4 %shard_map.78 = (bf16[256,256]{1,0:T(8,128)(2,1)S(1)}, bf16[256,256]{1,0:T(8,128)(2,1)S(1)}, f32[128,1024]{1,0:T(8,128)S(1)}) custom-call(s32[1,5]{1,0:T(1,128)S(1)} %copy-done.5, s32[1,32]{1,0:T(1,128)S(1)} %bitcast.15, s32[128,1024]{1,0:T(8,128)S(1)} %shard_map.77.places), custom_call_target="tpu_custom_call" | custom-call | tf_op jit(solution)/shard_map/pallas_call | solution.py:235
  8.2 0.8 %shard_map.79 = (bf16[4,1024,128]{2,1,0:T(8,128)(2,1)S(1)}, bf16[4,1024,128]{2,1,0:T(8,128)(2,1)S(1)}, bf16[4,128,128]{2,1,0:T(8,128)(2,1)S(1)}, bf16[4,128,128]{2,1,0:T(8,128)(2,1)S(1)}) custom-call(bf16[256,256]{1,0:T(8,128)(2,1)S(1)} %get-tuple-element.22.sort, bf16[4096,128]{1,0:T(8,128)(2,1)S(1)} %bitcast.9, bf16[4096,128]{1,0:T(8,128)(2,1)S(1)} %bitcast.10, ...), custom_call_target="tpu_custom_call" | custom-call | tf_op jit(solution)/shard_map/pallas_call | solution.py:240
  9.0 0.8 %collective-permute-done = s32[1,5]{1,0:T(1,128)S(1)} collective-permute-done((s32[1,5]{1,0:T(1,128)}, s32[1,5]{1,0:T(1,128)S(1)}, u32[]{:S(2)}, u32[]{:S(2)}) %collective-permute-start) | collective-permute-done | bytes 52 | tf_op jit(solution)/shard_map/ppermute | solution.py:206
  9.8 0.0 collective-permute-start.1
  9.8 0.0 collective-permute-done.2
  9.8 1.0 %shard_map.80 = (f32[4,128,1024]{2,1,0:T(8,128)S(1)}, bf16[4,128,128]{2,1,0:T(8,128)(2,1)S(1)}) custom-call(f32[128,1024]{1,0:T(8,128)S(1)} %get-tuple-element.25.bias, bf16[4,1024,128]{2,1,0:T(8,128)(2,1)S(1)} %get-tuple-element.26.query, bf16[4,128,128]{2,1,0:T(8,128)(2,1)S(1)} %get-tuple-element.27.own_key, bf16[512,128]{1,0:T(8,128)(2,1)S(1)} %bitcast.11), custom_call_target="tpu_custom_call" | custom-call | tf_op jit(solution)/shard_map/pallas_call | solution.py:258
  10.8 0.4 %collective-permute-done.3 = bf16[1,128,4,128]{3,2,1,0:T(4,128)(2,1)S(1)} collective-permute-done((bf16[1,128,4,128]{3,2,1,0:T(4,128)(2,1)}, bf16[1,128,4,128]{3,2,1,0:T(4,128)(2,1)S(1)}, u32[]{:S(2)}, u32[]{:S(2)}) %collective-permute-start.3) | collective-permute-done | bytes 131104 | tf_op jit(solution)/shard_map/ppermute | solution.py:224
  11.2 1.0 %shard_map.81 = (bf16[4,4,160,256]{3,2,1,0:T(8,128)(2,1)S(1)}, f32[4,128,128]{2,1,0:T(8,128)S(1)}, bf16[512,128]{1,0:T(8,128)(2,1)S(1)}) custom-call(f32[4,128,1024]{2,1,0:T(8,128)S(1)} %get-tuple-element.28.probs, bf16[4,1024,128]{2,1,0:T(8,128)(2,1)S(1)} %get-tuple-element.26.query, bf16[4,1024,128]{2,1,0:T(8,128)(2,1)S(1)} %get-tuple-element.29.grad, ...), custom_call_target="tpu_custom_call" | custom-call | tf_op jit(solution)/shard_map/pallas_call | solution.py:264
  12.1 0.0 collective-permute-done.1
  12.1 1.8 %collective-permute-start.5 = (bf16[512,128]{1,0:T(8,128)(2,1)S(1)}, bf16[512,128]{1,0:T(8,128)(2,1)S(1)}, u32[]{:S(2)}, u32[]{:S(2)}) collective-permute-start(bf16[512,128]{1,0:T(8,128)(2,1)S(1)} %get-tuple-element.39), channel_id=1, source_target_pairs={{8,0},{16,8},{24,16},{0,24},{9,1},{17,9},{25,17},{1,25},{10,2},{18... | collective-permute-start | bytes 393224 | tf_op jit(solution)/shard_map/ppermute | solution.py:272
  13.9 1.6 %collective-permute-start.4 = (s32[1,5]{1,0:T(1,128)S(1)}, s32[1,5]{1,0:T(1,128)S(1)}, u32[]{:S(2)}, u32[]{:S(2)}) collective-permute-start(s32[1,5]{1,0:T(1,128)S(1)} %add.10), channel_id=1, source_target_pairs={{0,2},{1,3},{2,0},{3,1},{4,6},{5,7},{6,4},{7,5},{8,10},{9,11},{10,... | collective-permute-start | bytes 68 | tf_op jit(solution)/shard_map/ppermute | solution.py:206
  15.5 1.4 %shard_map.82 = (f32[4096,128]{1,0:T(8,128)S(1)}, f32[512,128]{1,0:T(8,128)S(1)}) custom-call(bf16[4,4,160,256]{3,2,1,0:T(8,128)(2,1)S(1)} %get-tuple-element.33.score_grad, bf16[4,128,128]{2,1,0:T(8,128)(2,1)S(1)} %get-tuple-element.27.own_key, bf16[4,128,128]{2,1,0:T(8,128)(2,1)S(1)} %get-tuple-element.34.back_key, ...), custom_call_target="tpu_custom_call" | custom-call | tf_op jit(solution)/shard_map/pallas_call | solution.py:276
  16.9 0.6 %collective-permute-done.4 = s32[1,5]{1,0:T(1,128)S(1)} collective-permute-done((s32[1,5]{1,0:T(1,128)S(1)}, s32[1,5]{1,0:T(1,128)S(1)}, u32[]{:S(2)}, u32[]{:S(2)}) %collective-permute-start.4) | collective-permute-done | bytes 52 | tf_op jit(solution)/shard_map/ppermute | solution.py:206
  17.5 0.3 %collective-permute-done.5.back = bf16[512,128]{1,0:T(8,128)(2,1)S(1)} collective-permute-done((bf16[512,128]{1,0:T(8,128)(2,1)S(1)}, bf16[512,128]{1,0:T(8,128)(2,1)S(1)}, u32[]{:S(2)}, u32[]{:S(2)}) %collective-permute-start.5) | collective-permute-done | bytes 131104 | tf_op jit(solution)/shard_map/ppermute | solution.py:272
  17.7 1.2 %shard_map.83 = (bf16[4096,128]{1,0:T(8,128)(2,1)}, bf16[512,128]{1,0:T(8,128)(2,1)}) custom-call(s32[1,5]{1,0:T(1,128)S(1)} %add.11.count, f32[4096,128]{1,0:T(8,128)S(1)} %get-tuple-element.37.query_in, f32[512,128]{1,0:T(8,128)S(1)} %get-tuple-element.38.own, bf16[512,128]{1,0:T(8,128)(2,1)S(1)} %collective-permute-done.5.back), custom_call_target="tpu_custom_call" | custom-call | tf_op jit(solution)/shard_map/pallas_call | solution.py:282
  (10 shorter events, 0.1 us)
Async XLA Ops:
  0.6 7.6 %copy-start.2 = (bf16[1,128,4,128]{3,2,1,0:T(4,128)(2,1)S(1)}, bf16[1,128,4,128]{3,2,1,0:T(4,128)(2,1)}, u32[]{:S(2)}) copy-start(bf16[1,128,4,128]{3,2,1,0:T(4,128)(2,1)} %param.7) | copy-start | bytes 393220
  0.6 7.6 %copy-start.3 = (bf16[1,128,4,128]{3,2,1,0:T(4,128)(2,1)S(1)}, bf16[1,128,4,128]{3,2,1,0:T(4,128)(2,1)}, u32[]{:S(2)}) copy-start(bf16[1,128,4,128]{3,2,1,0:T(4,128)(2,1)} %param.8) | copy-start | bytes 393220
  0.7 7.2 %copy-start.5 = (s32[1,5]{1,0:T(1,128)S(1)}, s32[1,5]{1,0:T(1,128)}, u32[]{:S(2)}) copy-start(s32[1,5]{1,0:T(1,128)} %bounds.1) | copy-start | bytes 64
  0.7 7.2 %copy-start.4 = (s32[32]{0:T(128)S(1)}, s32[32]{0:T(128)}, u32[]{:S(2)}) copy-start(s32[32]{0:T(128)} %param.11) | copy-start | bytes 388
  0.7 7.5 %copy-start = (bf16[1,128,32,128]{3,2,1,0:T(8,128)(2,1)S(1)}, bf16[1,128,32,128]{3,2,1,0:T(8,128)(2,1)}, u32[]{:S(2)}) copy-start(bf16[1,128,32,128]{3,2,1,0:T(8,128)(2,1)} %param.6) | copy-start | bytes 3145732
  0.7 7.5 %copy-start.1 = (bf16[1,128,32,128]{3,2,1,0:T(8,128)(2,1)S(1)}, bf16[1,128,32,128]{3,2,1,0:T(8,128)(2,1)}, u32[]{:S(2)}) copy-start(bf16[1,128,32,128]{3,2,1,0:T(8,128)(2,1)} %param.9) | copy-start | bytes 3145732
  0.7 9.1 %collective-permute-start.2 = (bf16[1,128,4,128]{3,2,1,0:T(4,128)(2,1)}, bf16[1,128,4,128]{3,2,1,0:T(4,128)(2,1)S(1)}, u32[]{:S(2)}, u32[]{:S(2)}) collective-permute-start(bf16[1,128,4,128]{3,2,1,0:T(4,128)(2,1)} %param.7), channel_id=1, source_target_pairs={{0,8},{8,16},{16,24},{24,0},{1,9},{9,17},{17,25},{25,1},{2,10},{10... | collective-permute-start | bytes 393224 | tf_op jit(solution)/shard_map/ppermute | solution.py:223
  3.7 7.5 %collective-permute-start.3 = (bf16[1,128,4,128]{3,2,1,0:T(4,128)(2,1)}, bf16[1,128,4,128]{3,2,1,0:T(4,128)(2,1)S(1)}, u32[]{:S(2)}, u32[]{:S(2)}) collective-permute-start(bf16[1,128,4,128]{3,2,1,0:T(4,128)(2,1)} %param.8), channel_id=1, source_target_pairs={{0,8},{8,16},{16,24},{24,0},{1,9},{9,17},{17,25},{25,1},{2,10},{10... | collective-permute-start | bytes 393224 | tf_op jit(solution)/shard_map/ppermute | solution.py:224
  5.2 4.6 %collective-permute-start = (s32[1,5]{1,0:T(1,128)}, s32[1,5]{1,0:T(1,128)S(1)}, u32[]{:S(2)}, u32[]{:S(2)}) collective-permute-start(s32[1,5]{1,0:T(1,128)} %bounds.1), channel_id=1, source_target_pairs={{0,4},{1,5},{2,6},{3,7},{4,0},{5,1},{6,2},{7,3},{8,12},{9,13},{10,... | collective-permute-start | bytes 68 | tf_op jit(solution)/shard_map/ppermute | solution.py:206
  9.8 2.4 %collective-permute-start.1 = (s32[1,5]{1,0:T(1,128)S(1)}, s32[1,5]{1,0:T(1,128)S(1)}, u32[]{:S(2)}, u32[]{:S(2)}) collective-permute-start(s32[1,5]{1,0:T(1,128)S(1)} %add.9), channel_id=1, source_target_pairs={{0,1},{1,0},{2,3},{3,2},{4,5},{5,4},{6,7},{7,6},{8,9},{9,8},{10,11... | collective-permute-start | bytes 68 | tf_op jit(solution)/shard_map/ppermute | solution.py:206
  12.1 5.6 %collective-permute-start.5 = (bf16[512,128]{1,0:T(8,128)(2,1)S(1)}, bf16[512,128]{1,0:T(8,128)(2,1)S(1)}, u32[]{:S(2)}, u32[]{:S(2)}) collective-permute-start(bf16[512,128]{1,0:T(8,128)(2,1)S(1)} %get-tuple-element.39), channel_id=1, source_target_pairs={{8,0},{16,8},{24,16},{0,24},{9,1},{17,9},{25,17},{1,25},{10,2},{18... | collective-permute-start | bytes 393224 | tf_op jit(solution)/shard_map/ppermute | solution.py:272
  13.9 3.5 %collective-permute-start.4 = (s32[1,5]{1,0:T(1,128)S(1)}, s32[1,5]{1,0:T(1,128)S(1)}, u32[]{:S(2)}, u32[]{:S(2)}) collective-permute-start(s32[1,5]{1,0:T(1,128)S(1)} %add.10), channel_id=1, source_target_pairs={{0,2},{1,3},{2,0},{3,1},{4,6},{5,7},{6,4},{7,5},{8,10},{9,11},{10,... | collective-permute-start | bytes 68 | tf_op jit(solution)/shard_map/ppermute | solution.py:206

commit v6 on v5

--- a/solution.py
+++ b/solution.py
@@ -88,75 +88,90 @@
     return lax.broadcasted_iota(jnp.int32, shape, 0) <= lax.broadcasted_iota(jnp.int32, shape, 1) // per
 
 
-def product(left, right, g, t, rows, own):
-    here, tok = own.shape[0], left.shape[1]
+def merge(left, right, t, own):
+    here = own.shape[0]
     lo, hi = t * here, (t + 1) * here
-    both = dot(jnp.concatenate([left[g, :hi], right[g, lo:]], axis=0), rows, NT)
-    return stack((both, 0, lo), (jnp.where(own, both[lo:hi], both[hi : hi + here]), 0, here), (both, hi + here, tok + here))
-
-
-def probs_kernel(sizes, bias, query, own_key, back_in, probs, back_key, flat):
+    mid = jnp.where(own, left[lo:hi], right[:here])
+    return stack((left, 0, lo), (mid, 0, here), (right, here, right.shape[0]))
+
+
+def probs_kernel(sizes, bias, query, grad, own_key, own_value, back_in, probs, own_prob_grad, own_delta, back_key, flat):
     tok, heads, groups, per = sizes
     split_heads(back_in, flat, back_key, tok, groups)
     rate = math.log2(math.e) / math.sqrt(query.shape[2])
     own = own_mask(per)
-    for g in range(groups):
-        for t in range(tok * per // BLOCK):
+    here = BLOCK // per
+    for g in range(groups):
+        for t in range(tok // here):
             part = slice(t * BLOCK, (t + 1) * BLOCK)
-            scores = product(own_key, back_key, g, t, query[g, part, :], own) + bias[:, part]
+            lo, hi = t * here, (t + 1) * here
+            both = dot(jnp.concatenate([own_key[g, :hi], back_key[g, lo:]], axis=0), query[g, part, :], NT)
+            scores = merge(both[:hi], both[hi:], t, own) + bias[:, part]
             top = jnp.maximum(jnp.max(scores, axis=0, keepdims=True), -1e29)
             terms = jnp.exp2((scores - top) * rate)
             scale = 1.0 / jnp.maximum(jnp.sum(terms, axis=0, keepdims=True), 1.0)
-            probs[g, :, part] = terms * scale
-
-
-def score_kernel(sizes, probs, query, grad, own_value, value_in, score_grad, own_grad, back, back_value, flat):
+            prob = terms * scale
+            probs[g, t] = prob
+            prob_grad = dot(own_value[g, :hi], grad[g, part, :], NT)
+            own_prob_grad[g, t, :hi] = prob_grad
+            both = prob[:hi] * prob_grad
+            both = stack((both, 0, lo), (jnp.where(own, both[lo:], 0.0), 0, here))
+            own_delta[g, t] = jnp.sum(both, axis=0, keepdims=True)
+
+
+def add_rows(sums, first, piece, here):
+    for i in range(piece.shape[0] // here):
+        block = piece[i * here : (i + 1) * here]
+        sums[first + i] = block if sums[first + i] is None else sums[first + i] + block
+
+
+def score_kernel(sizes, probs, own_delta, query, grad, value_in, back_score, delta_out, back, back_value, flat):
     tok, heads, groups, per = sizes
     split_heads(value_in, flat, back_value, tok, groups)
     here = BLOCK // per
     own = own_mask(per)
     for g in range(groups):
         for t in range(tok // here):
-            part = slice(t * BLOCK, (t + 1) * BLOCK)
-            lo, hi = t * here, (t + 1) * here
-            prob = probs[g, :, part]
-            prob_grad = product(own_value, back_value, g, t, grad[g, part, :], own)
-            delta = jnp.sum(prob * prob_grad, axis=0, keepdims=True)
-            out = prob * (prob_grad - delta)
-            mid = out[lo:hi]
-            score_grad[g, t, :hi, :] = stack((out, 0, lo), (jnp.where(own, mid, 0.0), 0, here)).astype(BF16)
-            score_grad[g, t, hi:, :] = stack((jnp.where(own, 0.0, mid), 0, here), (out, hi, tok)).astype(BF16)
-    for g in range(groups):
-        own_sum, back_sum = [None] * (tok // here), [None] * (tok // here)
-        for t in range(tok // here):
-            both = dot(score_grad[g, t], query[g, t * BLOCK : (t + 1) * BLOCK, :])
-            for i in range(t + 1):
-                piece = both[i * here : (i + 1) * here]
-                own_sum[i] = piece if own_sum[i] is None else own_sum[i] + piece
-            for i in range(t, tok // here):
-                piece = both[(i + 1) * here : (i + 2) * here]
-                back_sum[i] = piece if back_sum[i] is None else back_sum[i] + piece
-        own_grad[g] = jnp.concatenate(own_sum, axis=0)
-        flat[pl.ds(g, tok, stride=groups), :] = jnp.concatenate(back_sum, axis=0)
+            lo = t * here
+            prob = probs[g, t, lo:]
+            prob = stack((jnp.where(own, 0.0, prob[:here]), 0, here), (prob, here, tok - lo))
+            prob_grad = dot(back_value[g, lo:], grad[g, t * BLOCK : (t + 1) * BLOCK, :], NT)
+            delta = own_delta[g, t] + jnp.sum(prob * prob_grad, axis=0, keepdims=True)
+            delta_out[g, t] = delta
+            back_score[g, t, lo:] = (prob * (prob_grad - delta)).astype(BF16)
+    for g in range(groups):
+        sums = [None] * (tok // here)
+        for t in range(tok // here):
+            rows = query[g, t * BLOCK : (t + 1) * BLOCK, :]
+            add_rows(sums, t, dot(back_score[g, t, t * here :, :], rows), here)
+        flat[pl.ds(g, tok, stride=groups), :] = jnp.concatenate(sums, axis=0)
     back[...] = flat[...].astype(BF16)
 
 
-def factor_of(count, tokens, depth):
-    last = count.shape[1] - 1
-    return (tokens / count[0:1, last : last + 1].astype(F32)) * (1.0 / math.sqrt(depth))
-
-
-def query_kernel(sizes, score_grad, own_key, back_key, own_grad, unsort, query_grad, key_grad, part_grad):
+def query_kernel(sizes, probs, own_prob_grad, delta, back_score, query, own_key, back_key, unsort, query_grad, key_grad, part_grad, own_score):
     tok, heads, groups, per = sizes
     depth = own_key.shape[2]
     step = BLOCK // heads
     share = step * per
     here = BLOCK // per
-    for g in range(groups):
-        for t in range(tok // here):
-            keys = jnp.concatenate([own_key[g, : (t + 1) * here], back_key[g, t * here :]], axis=0)
-            part_grad[g, t * BLOCK : (t + 1) * BLOCK, :] = dot(score_grad[g, t], keys, TN)
-        key_grad[pl.ds(g, tok, stride=groups), :] = own_grad[g]
+    own = own_mask(per)
+    for g in range(groups):
+        for t in range(tok // here):
+            lo, hi = t * here, (t + 1) * here
+            out = probs[g, t, :hi] * (own_prob_grad[g, t, :hi] - delta[g, t])
+            own_score[g, t, :hi] = stack((out, 0, lo), (jnp.where(own, out[lo:], 0.0), 0, here)).astype(BF16)
+    for g in range(groups):
+        for t in range(tok // here):
+            lo, hi = t * here, (t + 1) * here
+            keys = jnp.concatenate([own_key[g, :hi], back_key[g, lo:]], axis=0)
+            both = jnp.concatenate([own_score[g, t, :hi], back_score[g, t, lo:]], axis=0)
+            part_grad[g, t * BLOCK : (t + 1) * BLOCK, :] = dot(both, keys, TN)
+    for g in range(groups):
+        sums = [None] * (tok // here)
+        for t in range(tok // here):
+            rows = query[g, t * BLOCK : (t + 1) * BLOCK, :]
+            add_rows(sums, 0, dot(own_score[g, t, : (t + 1) * here, :], rows), here)
+        key_grad[pl.ds(g, tok, stride=groups), :] = jnp.concatenate(sums, axis=0)
     for b in range(0, tok // step, 2):
         both = [
             jnp.concatenate([part_grad[g, (b + i) * share : (b + i + 1) * share, :] for g in range(groups)], axis=0)
@@ -225,7 +240,7 @@
     dp = lax.axis_size("dp")
     paired = dp >= 8 and dp & (dp - 1) == 0
     hops = [1 << i for i in range(dp.bit_length() - 1)] if paired else []
-    count = add_partner(offsets, "dp", hops[-1]) if paired else lax.psum(offsets, "dp")
+    moved = partner(offsets, "dp", hops[-1]) if paired else lax.psum(offsets, "dp")
 
     sorted_shape = (groups, tok * per, depth)
     packed = (tok * groups, depth)
@@ -250,35 +265,38 @@
         value_matrix.reshape(packed),
     )
 
-    count, sorted_query = lax.optimization_barrier((count, sorted_query))
-    for hop in hops[2:-1]:
-        count = add_partner(count, "dp", hop)
-    moved = partner(count, "dp", 1) if paired else count
-
-    probs, back_key = call(
+    tall = (groups, tok // here, tok, BLOCK)
+    line = (groups, tok // here, 1, BLOCK)
+    probs, own_prob_grad, own_delta, back_key = call(
         functools.partial(probs_kernel, sizes),
-        [VMEM] * 4,
-        [((groups, tok, tok * per), F32), (split, BF16)],
+        [VMEM] * 6,
+        [(tall, F32), (tall, F32), (line, F32), (split, BF16)],
         [pltpu.VMEM(packed, F32)],
-    )(bias, sorted_query, own_key, back_key)
-    score_grad, own, back = call(
+    )(bias, sorted_query, sorted_grad, own_key, own_value, back_key)
+    moved, probs = lax.optimization_barrier((moved, probs))
+    if paired:
+        count = offsets + moved
+        for hop in hops[2:-1]:
+            count = add_partner(count, "dp", hop)
+        moved = partner(count, "dp", 1)
+    back_score, delta, back = call(
         functools.partial(score_kernel, sizes),
         [VMEM] * 5,
-        [((groups, tok // here, tok + here, BLOCK), BF16), (split, F32), (packed, BF16)],
+        [(tall, BF16), (line, F32), (packed, BF16)],
         [pltpu.VMEM(split, BF16), pltpu.VMEM(packed, F32)],
-    )(probs, sorted_query, sorted_grad, own_value, back_value)
+    )(probs, own_delta, sorted_query, sorted_grad, back_value)
 
     moved, back = lax.optimization_barrier((moved, back))
     back = lax.ppermute(back, "ctx", behind)
-    if paired:
-        count = add_partner(count + moved, "dp", 2)
+    count, delta = lax.optimization_barrier((count + moved, delta)) if paired else (moved, delta)
+    count = add_partner(count, "dp", 2) if paired else count
 
     plain_grad, own = call(
         functools.partial(query_kernel, sizes),
-        [VMEM] * 5,
+        [VMEM] * 8,
         [((tok * heads, depth), F32), (packed, F32)],
-        [pltpu.VMEM(sorted_shape, F32)],
-    )(score_grad, own_key, back_key, own, unsort)
+        [pltpu.VMEM(sorted_shape, F32), pltpu.VMEM(tall, BF16)],
+    )(probs, own_prob_grad, delta, back_score, sorted_query, own_key, back_key, unsort)
     query_grad, key_grad = call(
         functools.partial(scale_kernel, tokens),
         [VMEM] * 4,

time: 19.1 us -> 18.6 us (0.974)
  waiting for transfers between devices: 2 us -> 1.44 us
    ppermute x3, waiting for transfers between devices: 1.37 us -> 0.44 us  [partner(): lax.ppermute(value, axis, [(i, i ^ hop) for i in range(lax.axis_size(axis...]
    ppermute x1, waiting for transfers between devices: 0.36 us -> 0.77 us  [per_device(): lax.ppermute(value_matrix, 'ctx', ahead).reshape(tok * groups, depth)]
    ppermute x1, waiting for transfers between devices: 0.27 us -> 0.01 us  [per_device(): back = lax.ppermute(back, 'ctx', behind)]
    ppermute x1, waiting for transfers between devices: 0.01 us -> 0.22 us  [per_device(): back_key = lax.ppermute(key_rows, 'ctx', ahead).reshape(tok * groups, depth)]
  transfers between devices with their start and end apart: 6 -> 6, of which waited for: 4 -> 3; matrix products, arithmetic and copies ran while one was open for 0% -> 0% of each run, Pallas kernels for 24% -> 24%
where the time goes in v6:
time: 18.6 us; the launch traced here: 18.4 us
  starting transfers between devices  10.5 us (56%)
  Pallas kernels  5.67 us (30%)
  waiting for transfers between devices  1.44 us (8%)
  between operations  0.79 us (4%)
    ppermute x3, starting transfers between devices, partner(): lax.ppermute(value, axis, [(i, i ^ hop) for i in range(lax.axis_size(axis...  4.23 us
    ppermute x1, starting transfers between devices, per_device(): back_key = lax.ppermute(key_rows, 'ctx', ahead).reshape(tok * groups, depth)  2.99 us
    ppermute x1, starting transfers between devices, per_device(): back = lax.ppermute(back, 'ctx', behind)  1.79 us
    pallas_call x1, Pallas kernels, per_device(): call(functools.partial(query_kernel, sizes), [VMEM] * 8, [((tok * heads,...  1.53 us
    ppermute x1, starting transfers between devices, per_device(): lax.ppermute(value_matrix, 'ctx', ahead).reshape(tok * groups, depth)  1.49 us
    pallas_call x1, Pallas kernels, per_device(): call(functools.partial(scale_kernel, tokens), [VMEM] * 4, [((tok * heads,...  1.2 us
    pallas_call x1, Pallas kernels, per_device(): call(functools.partial(probs_kernel, sizes), [VMEM] * 6, [(tall, F32), (t...  1.1 us
    ppermute x1, waiting for transfers between devices, per_device(): lax.ppermute(value_matrix, 'ctx', ahead).reshape(tok * groups, depth)  0.77 us
  transfers between devices with their start and end apart: 6, of which 3 were waited for; matrix products, arithmetic and copies ran while one was open for 0% of the time, Pallas kernels for 24%

profile of v6, /device:TPU:0, one launch (start us, length us, event | category | flops | bytes accessed | tf_op | source)
XLA Modules:
  0.0 18.4 jit_solution(3513417052984379723)
XLA Ops:
  0.6 0.0 copy-start.2
  0.6 0.0 copy-start.3
  0.7 0.0 copy-start.5
  0.7 0.0 copy-start.4
  0.7 0.0 copy-start.1
  0.7 0.0 copy-start
  0.7 3.0 %collective-permute-start.1 = (bf16[1,128,4,128]{3,2,1,0:T(4,128)(2,1)}, bf16[1,128,4,128]{3,2,1,0:T(4,128)(2,1)S(1)}, u32[]{:S(2)}, u32[]{:S(2)}) collective-permute-start(bf16[1,128,4,128]{3,2,1,0:T(4,128)(2,1)} %param.7), channel_id=1, source_target_pairs={{0,8},{8,16},{16,24},{24,0},{1,9},{9,17},{17,25},{25,1},{2,10},{10... | collective-permute-start | bytes 393224 | tf_op jit(solution)/shard_map/ppermute | solution.py:238
  3.7 1.5 %collective-permute-start.3 = (bf16[1,128,4,128]{3,2,1,0:T(4,128)(2,1)}, bf16[1,128,4,128]{3,2,1,0:T(4,128)(2,1)S(1)}, u32[]{:S(2)}, u32[]{:S(2)}) collective-permute-start(bf16[1,128,4,128]{3,2,1,0:T(4,128)(2,1)} %param.8), channel_id=1, source_target_pairs={{0,8},{8,16},{16,24},{24,0},{1,9},{9,17},{17,25},{25,1},{2,10},{10... | collective-permute-start | bytes 393224 | tf_op jit(solution)/shard_map/ppermute | solution.py:239
  5.2 2.6 %collective-permute-start = (s32[1,5]{1,0:T(1,128)}, s32[1,5]{1,0:T(1,128)S(1)}, u32[]{:S(2)}, u32[]{:S(2)}) collective-permute-start(s32[1,5]{1,0:T(1,128)} %bounds.1), channel_id=1, source_target_pairs={{0,4},{1,5},{2,6},{3,7},{4,0},{5,1},{6,2},{7,3},{8,12},{9,13},{10,... | collective-permute-start | bytes 68 | tf_op jit(solution)/shard_map/ppermute | solution.py:221
  7.8 0.4 %shard_map.78 = (bf16[256,256]{1,0:T(8,128)(2,1)S(1)}, bf16[256,256]{1,0:T(8,128)(2,1)S(1)}, f32[128,1024]{1,0:T(8,128)S(1)}) custom-call(s32[1,5]{1,0:T(1,128)S(1)} %copy-done.5, s32[1,32]{1,0:T(1,128)S(1)} %bitcast.15, s32[128,1024]{1,0:T(8,128)S(1)} %shard_map.77.places), custom_call_target="tpu_custom_call" | custom-call | tf_op jit(solution)/shard_map/pallas_call | solution.py:250
  8.2 0.7 %shard_map.79 = (bf16[4,1024,128]{2,1,0:T(8,128)(2,1)S(1)}, bf16[4,1024,128]{2,1,0:T(8,128)(2,1)S(1)}, bf16[4,128,128]{2,1,0:T(8,128)(2,1)S(1)}, bf16[4,128,128]{2,1,0:T(8,128)(2,1)S(1)}) custom-call(bf16[256,256]{1,0:T(8,128)(2,1)S(1)} %get-tuple-element.27.sort, bf16[4096,128]{1,0:T(8,128)(2,1)S(1)} %bitcast.9, bf16[4096,128]{1,0:T(8,128)(2,1)S(1)} %bitcast.10, ...), custom_call_target="tpu_custom_call" | custom-call | tf_op jit(solution)/shard_map/pallas_call | solution.py:255
  9.0 0.2 %collective-permute-done.1 = bf16[1,128,4,128]{3,2,1,0:T(4,128)(2,1)S(1)} collective-permute-done((bf16[1,128,4,128]{3,2,1,0:T(4,128)(2,1)}, bf16[1,128,4,128]{3,2,1,0:T(4,128)(2,1)S(1)}, u32[]{:S(2)}, u32[]{:S(2)}) %collective-permute-start.1) | collective-permute-done | bytes 131104 | tf_op jit(solution)/shard_map/ppermute | solution.py:238
  9.2 1.1 %shard_map.80 = (f32[4,4,128,256]{3,2,1,0:T(8,128)S(1)}, f32[4,4,128,256]{3,2,1,0:T(8,128)S(1)}, f32[4,4,1,256]{3,2,1,0:T(1,128)S(1)}, bf16[4,128,128]{2,1,0:T(8,128)(2,1)S(1)}) custom-call(f32[128,1024]{1,0:T(8,128)S(1)} %get-tuple-element.26.bias, bf16[4,1024,128]{2,1,0:T(8,128)(2,1)S(1)} %get-tuple-element.28.query, ...), custom_call_target="tpu_custom_call" | custom-call | tf_op jit(solution)/shard_map/pallas_call | solution.py:270
  10.3 0.0 collective-permute-done
  10.3 0.1 collective-permute-start.2
  10.4 0.8 %collective-permute-done.3 = bf16[1,128,4,128]{3,2,1,0:T(4,128)(2,1)S(1)} collective-permute-done((bf16[1,128,4,128]{3,2,1,0:T(4,128)(2,1)}, bf16[1,128,4,128]{3,2,1,0:T(4,128)(2,1)S(1)}, u32[]{:S(2)}, u32[]{:S(2)}) %collective-permute-start.3) | collective-permute-done | bytes 131104 | tf_op jit(solution)/shard_map/ppermute | solution.py:239
  11.2 0.7 %shard_map.81 = (bf16[4,4,128,256]{3,2,1,0:T(8,128)(2,1)S(1)}, f32[4,4,1,256]{3,2,1,0:T(1,128)S(1)}, bf16[512,128]{1,0:T(8,128)(2,1)S(1)}) custom-call(f32[4,4,128,256]{3,2,1,0:T(8,128)S(1)} %get-tuple-element.34.probs, f32[4,4,1,256]{3,2,1,0:T(1,128)S(1)} %get-tuple-element.35.own_delta, bf16[4,1024,128]{2,1,0:T(8,128)(2,1)S(1)} %get-tuple-element.28.query, ...), custom_call_target="tpu_custom_call" | custom-call | tf_op jit(solution)/shard_map/pallas_call | solution.py:282
  11.9 0.0 collective-permute-done.2
  11.9 1.8 %collective-permute-start.5 = (bf16[512,128]{1,0:T(8,128)(2,1)S(1)}, bf16[512,128]{1,0:T(8,128)(2,1)S(1)}, u32[]{:S(2)}, u32[]{:S(2)}) collective-permute-start(bf16[512,128]{1,0:T(8,128)(2,1)S(1)} %get-tuple-element.47), channel_id=1, source_target_pairs={{8,0},{16,8},{24,16},{0,24},{9,1},{17,9},{25,17},{1,25},{10,2},{18... | collective-permute-start | bytes 393224 | tf_op jit(solution)/shard_map/ppermute | solution.py:290
  13.7 1.6 %collective-permute-start.4 = (s32[1,5]{1,0:T(1,128)S(1)}, s32[1,5]{1,0:T(1,128)S(1)}, u32[]{:S(2)}, u32[]{:S(2)}) collective-permute-start(s32[1,5]{1,0:T(1,128)S(1)} %add.10), channel_id=1, source_target_pairs={{0,2},{1,3},{2,0},{3,1},{4,6},{5,7},{6,4},{7,5},{8,10},{9,11},{10,... | collective-permute-start | bytes 68 | tf_op jit(solution)/shard_map/ppermute | solution.py:221
  15.3 1.5 %shard_map.82 = (f32[4096,128]{1,0:T(8,128)S(1)}, f32[512,128]{1,0:T(8,128)S(1)}) custom-call(f32[4,4,128,256]{3,2,1,0:T(8,128)S(1)} %get-tuple-element.34.probs, f32[4,4,128,256]{3,2,1,0:T(8,128)S(1)} %get-tuple-element.40.own_prob_grad, f32[4,4,1,256]{3,2,1,0:T(1,128)S(1)} %get-tuple-element.41.delta, ...), custom_call_target="tpu_custom_call" | custom-call | tf_op jit(solution)/shard_map/pallas_call | solution.py:294
  16.8 0.4 %collective-permute-done.4 = s32[1,5]{1,0:T(1,128)S(1)} collective-permute-done((s32[1,5]{1,0:T(1,128)S(1)}, s32[1,5]{1,0:T(1,128)S(1)}, u32[]{:S(2)}, u32[]{:S(2)}) %collective-permute-start.4) | collective-permute-done | bytes 52 | tf_op jit(solution)/shard_map/ppermute | solution.py:221
  17.2 0.0 collective-permute-done.5.back
  17.2 1.2 %shard_map.83 = (bf16[4096,128]{1,0:T(8,128)(2,1)}, bf16[512,128]{1,0:T(8,128)(2,1)}) custom-call(s32[1,5]{1,0:T(1,128)S(1)} %add.11.count, f32[4096,128]{1,0:T(8,128)S(1)} %get-tuple-element.45.query_in, f32[512,128]{1,0:T(8,128)S(1)} %get-tuple-element.46.own, bf16[512,128]{1,0:T(8,128)(2,1)S(1)} %collective-permute-done.5.back), custom_call_target="tpu_custom_call" | custom-call | tf_op jit(solution)/shard_map/pallas_call | solution.py:300
  (10 shorter events, 0.1 us)
Async XLA Ops:
  0.6 7.6 %copy-start.2 = (bf16[1,128,4,128]{3,2,1,0:T(4,128)(2,1)S(1)}, bf16[1,128,4,128]{3,2,1,0:T(4,128)(2,1)}, u32[]{:S(2)}) copy-start(bf16[1,128,4,128]{3,2,1,0:T(4,128)(2,1)} %param.7) | copy-start | bytes 393220
  0.6 7.6 %copy-start.3 = (bf16[1,128,4,128]{3,2,1,0:T(4,128)(2,1)S(1)}, bf16[1,128,4,128]{3,2,1,0:T(4,128)(2,1)}, u32[]{:S(2)}) copy-start(bf16[1,128,4,128]{3,2,1,0:T(4,128)(2,1)} %param.8) | copy-start | bytes 393220
  0.7 7.2 %copy-start.5 = (s32[1,5]{1,0:T(1,128)S(1)}, s32[1,5]{1,0:T(1,128)}, u32[]{:S(2)}) copy-start(s32[1,5]{1,0:T(1,128)} %bounds.1) | copy-start | bytes 64
  0.7 7.2 %copy-start.4 = (s32[32]{0:T(128)S(1)}, s32[32]{0:T(128)}, u32[]{:S(2)}) copy-start(s32[32]{0:T(128)} %param.11) | copy-start | bytes 388
  0.7 7.5 %copy-start.1 = (bf16[1,128,32,128]{3,2,1,0:T(8,128)(2,1)S(1)}, bf16[1,128,32,128]{3,2,1,0:T(8,128)(2,1)}, u32[]{:S(2)}) copy-start(bf16[1,128,32,128]{3,2,1,0:T(8,128)(2,1)} %param.9) | copy-start | bytes 3145732
  0.7 7.5 %copy-start = (bf16[1,128,32,128]{3,2,1,0:T(8,128)(2,1)S(1)}, bf16[1,128,32,128]{3,2,1,0:T(8,128)(2,1)}, u32[]{:S(2)}) copy-start(bf16[1,128,32,128]{3,2,1,0:T(8,128)(2,1)} %param.6) | copy-start | bytes 3145732
  0.7 8.5 %collective-permute-start.1 = (bf16[1,128,4,128]{3,2,1,0:T(4,128)(2,1)}, bf16[1,128,4,128]{3,2,1,0:T(4,128)(2,1)S(1)}, u32[]{:S(2)}, u32[]{:S(2)}) collective-permute-start(bf16[1,128,4,128]{3,2,1,0:T(4,128)(2,1)} %param.7), channel_id=1, source_target_pairs={{0,8},{8,16},{16,24},{24,0},{1,9},{9,17},{17,25},{25,1},{2,10},{10... | collective-permute-start | bytes 393224 | tf_op jit(solution)/shard_map/ppermute | solution.py:238
  3.7 7.5 %collective-permute-start.3 = (bf16[1,128,4,128]{3,2,1,0:T(4,128)(2,1)}, bf16[1,128,4,128]{3,2,1,0:T(4,128)(2,1)S(1)}, u32[]{:S(2)}, u32[]{:S(2)}) collective-permute-start(bf16[1,128,4,128]{3,2,1,0:T(4,128)(2,1)} %param.8), channel_id=1, source_target_pairs={{0,8},{8,16},{16,24},{24,0},{1,9},{9,17},{17,25},{25,1},{2,10},{10... | collective-permute-start | bytes 393224 | tf_op jit(solution)/shard_map/ppermute | solution.py:239
  5.2 5.1 %collective-permute-start = (s32[1,5]{1,0:T(1,128)}, s32[1,5]{1,0:T(1,128)S(1)}, u32[]{:S(2)}, u32[]{:S(2)}) collective-permute-start(s32[1,5]{1,0:T(1,128)} %bounds.1), channel_id=1, source_target_pairs={{0,4},{1,5},{2,6},{3,7},{4,0},{5,1},{6,2},{7,3},{8,12},{9,13},{10,... | collective-permute-start | bytes 68 | tf_op jit(solution)/shard_map/ppermute | solution.py:221
  10.3 1.6 %collective-permute-start.2 = (s32[1,5]{1,0:T(1,128)S(1)}, s32[1,5]{1,0:T(1,128)S(1)}, u32[]{:S(2)}, u32[]{:S(2)}) collective-permute-start(s32[1,5]{1,0:T(1,128)S(1)} %add.9), channel_id=1, source_target_pairs={{0,1},{1,0},{2,3},{3,2},{4,5},{5,4},{6,7},{7,6},{8,9},{9,8},{10,11... | collective-permute-start | bytes 68 | tf_op jit(solution)/shard_map/ppermute | solution.py:221
  11.9 5.3 %collective-permute-start.5 = (bf16[512,128]{1,0:T(8,128)(2,1)S(1)}, bf16[512,128]{1,0:T(8,128)(2,1)S(1)}, u32[]{:S(2)}, u32[]{:S(2)}) collective-permute-start(bf16[512,128]{1,0:T(8,128)(2,1)S(1)} %get-tuple-element.47), channel_id=1, source_target_pairs={{8,0},{16,8},{24,16},{0,24},{9,1},{17,9},{25,17},{1,25},{10,2},{18... | collective-permute-start | bytes 393224 | tf_op jit(solution)/shard_map/ppermute | solution.py:290
  13.7 3.5 %collective-permute-start.4 = (s32[1,5]{1,0:T(1,128)S(1)}, s32[1,5]{1,0:T(1,128)S(1)}, u32[]{:S(2)}, u32[]{:S(2)}) collective-permute-start(s32[1,5]{1,0:T(1,128)S(1)} %add.10), channel_id=1, source_target_pairs={{0,2},{1,3},{2,0},{3,1},{4,6},{5,7},{6,4},{7,5},{8,10},{9,11},{10,... | collective-permute-start | bytes 68 | tf_op jit(solution)/shard_map/ppermute | solution.py:221

commit v7 on v6

--- a/solution.py
+++ b/solution.py
@@ -185,20 +185,27 @@
         query_grad[(b + 1) * BLOCK : (b + 2) * BLOCK, :] = both[:, depth:]
 
 
-def scale_kernel(tokens, count, query_in, own, back, query_out, key_out, query_grad, key_grad, sems):
+def factor_of(count, tokens, depth):
+    last = count.shape[1] - 1
+    return (tokens / count[0:1, last : last + 1].astype(F32)) * (1.0 / math.sqrt(depth))
+
+
+def query_out_kernel(tokens, count, query_in, query_out, query_grad, sems):
     rows, depth = query_in.shape
-    last = count.shape[1] - 1
-    factor = (tokens / count[0:1, last : last + 1].astype(F32)) * (1.0 / math.sqrt(depth))
-    key_grad[...] = ((own[...] + back[...].astype(F32)) * factor).astype(BF16)
-    copies = [pltpu.make_async_copy(key_grad, key_out, sems.at[0])]
-    copies[0].start()
+    factor = factor_of(count, tokens, depth)
+    copies = []
     for i in range(PIECES):
         part = pl.ds(i * (rows // PIECES), rows // PIECES)
         query_grad[part, :] = (query_in[part, :] * factor).astype(BF16)
-        copies.append(pltpu.make_async_copy(query_grad.at[part], query_out.at[part], sems.at[1 + i]))
+        copies.append(pltpu.make_async_copy(query_grad.at[part], query_out.at[part], sems.at[i]))
         copies[-1].start()
     for copy in copies:
         copy.wait()
+
+
+def key_out_kernel(tokens, count, own, back, key_grad):
+    factor = factor_of(count, tokens, own.shape[1])
+    key_grad[...] = ((own[...] + back[...].astype(F32)) * factor).astype(BF16)
 
 
 VMEM = pl.BlockSpec(memory_space=pltpu.VMEM)
@@ -232,16 +239,17 @@
     sizes = (tok, heads, groups, per)
     ctx = lax.axis_size("ctx")
     tokens = float(offsets.shape[0] * lax.axis_size("dp") * tok * ctx)
-    ahead = [(i, (i + 1) % ctx) for i in range(ctx)]
-    behind = [((i + 1) % ctx, i) for i in range(ctx)]
-
-    back_key = lax.ppermute(key_rows, "ctx", ahead).reshape(tok * groups, depth)
-    back_value = lax.ppermute(value_matrix, "ctx", ahead).reshape(tok * groups, depth)
+    axes, copies = ("ctx", "dp"), lax.axis_size("dp")
+    swap = 1 if copies % 2 == 0 else 0
+    ahead = [(c * copies + i, (c + 1) * copies + i) for c in range(ctx - 1) for i in range(copies)]
+    behind = [(b, a) for a, b in ahead] + [(i ^ swap, (ctx - 1) * copies + i) for i in range(copies)]
+    ahead += [((ctx - 1) * copies + i, i) for i in range(copies)]
+
+    back_key = lax.ppermute(key_rows, axes, ahead).reshape(tok * groups, depth)
+    back_value = lax.ppermute(value_matrix, axes, ahead).reshape(tok * groups, depth)
     dp = lax.axis_size("dp")
     paired = dp >= 8 and dp & (dp - 1) == 0
     hops = [1 << i for i in range(dp.bit_length() - 1)] if paired else []
-    moved = partner(offsets, "dp", hops[-1]) if paired else lax.psum(offsets, "dp")
-
     sorted_shape = (groups, tok * per, depth)
     packed = (tok * groups, depth)
     split = (groups, tok, depth)
@@ -252,6 +260,11 @@
         [VMEM] * 3,
         [((BLOCK, BLOCK), BF16), ((BLOCK, BLOCK), BF16), ((tok, tok * per), F32)],
     )(offsets, query_head_group.reshape(1, heads), places)
+    if paired:
+        count, sort = lax.optimization_barrier((add_partner(offsets, "dp", 1), sort))
+        moved = partner(count, "dp", hops[-1])
+    else:
+        moved = lax.psum(offsets, "dp")
     sorted_query, sorted_grad, own_key, own_value = call(
         functools.partial(arrange_kernel, sizes),
         [VMEM] * 5,
@@ -272,24 +285,28 @@
         [VMEM] * 6,
         [(tall, F32), (tall, F32), (line, F32), (split, BF16)],
         [pltpu.VMEM(packed, F32)],
+        500_000_000,
     )(bias, sorted_query, sorted_grad, own_key, own_value, back_key)
     moved, probs = lax.optimization_barrier((moved, probs))
     if paired:
-        count = offsets + moved
         for hop in hops[2:-1]:
-            count = add_partner(count, "dp", hop)
-        moved = partner(count, "dp", 1)
+            count = count + moved
+            moved = partner(count, "dp", hop)
     back_score, delta, back = call(
         functools.partial(score_kernel, sizes),
         [VMEM] * 5,
         [(tall, BF16), (line, F32), (packed, BF16)],
         [pltpu.VMEM(split, BF16), pltpu.VMEM(packed, F32)],
+        2_000_000_000,
     )(probs, own_delta, sorted_query, sorted_grad, back_value)
 
     moved, back = lax.optimization_barrier((moved, back))
-    back = lax.ppermute(back, "ctx", behind)
-    count, delta = lax.optimization_barrier((count + moved, delta)) if paired else (moved, delta)
-    count = add_partner(count, "dp", 2) if paired else count
+    back = lax.ppermute(back, axes, behind)
+    if paired:
+        count, delta = lax.optimization_barrier((count + moved, delta))
+        count = add_partner(count, "dp", 2)
+    else:
+        count = moved
 
     plain_grad, own = call(
         functools.partial(query_kernel, sizes),
@@ -297,17 +314,14 @@
         [((tok * heads, depth), F32), (packed, F32)],
         [pltpu.VMEM(sorted_shape, F32), pltpu.VMEM(tall, BF16)],
     )(probs, own_prob_grad, delta, back_score, sorted_query, own_key, back_key, unsort)
-    query_grad, key_grad = call(
-        functools.partial(scale_kernel, tokens),
-        [VMEM] * 4,
-        [((tok * heads, depth), BF16), (packed, BF16)],
-        [
-            pltpu.VMEM((tok * heads, depth), BF16),
-            pltpu.VMEM(packed, BF16),
-            pltpu.SemaphoreType.DMA((1 + PIECES,)),
-        ],
+    (query_grad,) = call(
+        functools.partial(query_out_kernel, tokens),
+        [VMEM] * 2,
+        [((tok * heads, depth), BF16)],
+        [pltpu.VMEM((tok * heads, depth), BF16), pltpu.SemaphoreType.DMA((PIECES,))],
         out_spec=HBM,
-    )(count, plain_grad, own, back)
+    )(count, plain_grad)
+    (key_grad,) = call(functools.partial(key_out_kernel, tokens), [VMEM] * 3, [(packed, BF16)])(count, own, back)
     return (query_grad.reshape(query_rows.shape), key_grad.reshape(key_rows.shape))
 
 

time: 18.6 us -> 18.3 us (0.984)
  the two profiles are of different devices: /device:TPU:0 before, /device:TPU:1 now
where the time goes in v7:
time: 18.3 us; the launch traced here: 18.2 us
  starting transfers between devices  10.1 us (55%)
  Pallas kernels  6.46 us (35%)
  between operations  0.79 us (4%)
  waiting for transfers between devices  0.77 us (4%)
    ppermute x3, starting transfers between devices, partner(): lax.ppermute(value, axis, [(i, i ^ hop) for i in range(lax.axis_size(axis...  4.63 us
    ppermute x1, starting transfers between devices, per_device(): back = lax.ppermute(back, axes, behind)  2.18 us
    ppermute x1, starting transfers between devices, per_device(): back_key = lax.ppermute(key_rows, axes, ahead).reshape(tok * groups, depth)  2.09 us
    pallas_call x1, Pallas kernels, per_device(): call(functools.partial(query_kernel, sizes), [VMEM] * 8, [((tok * heads,...  1.55 us
    ppermute x1, starting transfers between devices, per_device(): lax.ppermute(value_matrix, axes, ahead).reshape(tok * groups, depth)  1.21 us
    pallas_call x1, Pallas kernels, per_device(): call(functools.partial(query_out_kernel, tokens), [VMEM] * 2, [((tok * he...  1.17 us
    pallas_call x1, Pallas kernels, per_device(): call(functools.partial(probs_kernel, sizes), [VMEM] * 6, [(tall, F32), (t...  1.11 us
    ppermute x1, waiting for transfers between devices, per_device(): lax.ppermute(value_matrix, axes, ahead).reshape(tok * groups, depth)  0.76 us
  transfers between devices with their start and end apart: 6, of which 1 were waited for; matrix products, arithmetic and copies ran while one was open for 0% of the time, Pallas kernels for 27%

profile of v7, /device:TPU:1, one launch (start us, length us, event | category | flops | bytes accessed | tf_op | source)
XLA Modules:
  0.0 18.2 jit_solution(4524340662886899726)
XLA Ops:
  0.6 0.0 copy-start.2
  0.6 0.0 copy-start.5
  0.7 2.1 %collective-permute-start.2 = (bf16[1,128,4,128]{3,2,1,0:T(4,128)(2,1)}, bf16[1,128,4,128]{3,2,1,0:T(4,128)(2,1)S(1)}, u32[]{:S(2)}, u32[]{:S(2)}) collective-permute-start(bf16[1,128,4,128]{3,2,1,0:T(4,128)(2,1)} %param.7), channel_id=1, source_target_pairs={{0,8},{1,9},{2,10},{3,11},{4,12},{5,13},{6,14},{7,15},{8,16},{9,17... | collective-permute-start | bytes 393224 | tf_op jit(solution)/shard_map/ppermute | solution.py:248
  2.8 1.0 %collective-permute-start = (s32[1,5]{1,0:T(1,128)}, s32[1,5]{1,0:T(1,128)S(1)}, u32[]{:S(2)}, u32[]{:S(2)}) collective-permute-start(s32[1,5]{1,0:T(1,128)} %bounds.1), channel_id=1, source_target_pairs={{0,1},{1,0},{2,3},{3,2},{4,5},{5,4},{6,7},{7,6},{8,9},{9,8},{10,11... | collective-permute-start | bytes 68 | tf_op jit(solution)/shard_map/ppermute | solution.py:228
  3.7 1.2 %collective-permute-start.3 = (bf16[1,128,4,128]{3,2,1,0:T(4,128)(2,1)}, bf16[1,128,4,128]{3,2,1,0:T(4,128)(2,1)S(1)}, u32[]{:S(2)}, u32[]{:S(2)}) collective-permute-start(bf16[1,128,4,128]{3,2,1,0:T(4,128)(2,1)} %param.8), channel_id=1, source_target_pairs={{0,8},{1,9},{2,10},{3,11},{4,12},{5,13},{6,14},{7,15},{8,16},{9,17... | collective-permute-start | bytes 393224 | tf_op jit(solution)/shard_map/ppermute | solution.py:249
  5.0 0.0 copy-done.5
  5.0 0.0 copy-done.4
  5.0 0.4 %shard_map.78 = (bf16[256,256]{1,0:T(8,128)(2,1)S(1)}, bf16[256,256]{1,0:T(8,128)(2,1)S(1)}, f32[128,1024]{1,0:T(8,128)S(1)}) custom-call(s32[1,5]{1,0:T(1,128)S(1)} %copy-done.5, s32[1,32]{1,0:T(1,128)S(1)} %bitcast.14, s32[128,1024]{1,0:T(8,128)S(1)} %shard_map.77.places), custom_call_target="tpu_custom_call" | custom-call | tf_op jit(solution)/shard_map/pallas_call | solution.py:258
  5.4 0.0 collective-permute-done
  5.4 2.4 %collective-permute-start.1 = (s32[1,5]{1,0:T(1,128)S(1)}, s32[1,5]{1,0:T(1,128)S(1)}, u32[]{:S(2)}, u32[]{:S(2)}) collective-permute-start(s32[1,5]{1,0:T(1,128)S(1)} %add.9), channel_id=1, source_target_pairs={{0,4},{1,5},{2,6},{3,7},{4,0},{5,1},{6,2},{7,3},{8,12},{9,13},{10,... | collective-permute-start | bytes 68 | tf_op jit(solution)/shard_map/ppermute | solution.py:228
  7.8 0.0 copy-done.3
  7.8 0.8 %shard_map.79 = (bf16[4,1024,128]{2,1,0:T(8,128)(2,1)S(1)}, bf16[4,1024,128]{2,1,0:T(8,128)(2,1)S(1)}, bf16[4,128,128]{2,1,0:T(8,128)(2,1)S(1)}, bf16[4,128,128]{2,1,0:T(8,128)(2,1)S(1)}) custom-call(bf16[256,256]{1,0:T(8,128)(2,1)S(1)} %get-tuple-element.29.sort, bf16[4096,128]{1,0:T(8,128)(2,1)S(1)} %bitcast.9, bf16[4096,128]{1,0:T(8,128)(2,1)S(1)} %bitcast.10, ...), custom_call_target="tpu_custom_call" | custom-call | tf_op jit(solution)/shard_map/pallas_call | solution.py:268
  8.5 0.0 collective-permute-done.2
  8.6 1.1 %shard_map.80 = (f32[4,4,128,256]{3,2,1,0:T(8,128)S(1)}, f32[4,4,128,256]{3,2,1,0:T(8,128)S(1)}, f32[4,4,1,256]{3,2,1,0:T(1,128)S(1)}, bf16[4,128,128]{2,1,0:T(8,128)(2,1)S(1)}) custom-call(f32[128,1024]{1,0:T(8,128)S(1)} %get-tuple-element.28.bias, bf16[4,1024,128]{2,1,0:T(8,128)(2,1)S(1)} %get-tuple-element.30.query, ...), custom_call_target="tpu_custom_call" | custom-call | flops 500000000 | tf_op jit(solution)/shard_map/pallas_call | solution.py:283
  9.7 0.0 collective-permute-done.1
  9.7 0.8 %collective-permute-done.3 = bf16[1,128,4,128]{3,2,1,0:T(4,128)(2,1)S(1)} collective-permute-done((bf16[1,128,4,128]{3,2,1,0:T(4,128)(2,1)}, bf16[1,128,4,128]{3,2,1,0:T(4,128)(2,1)S(1)}, u32[]{:S(2)}, u32[]{:S(2)}) %collective-permute-start.3) | collective-permute-done | bytes 131104 | tf_op jit(solution)/shard_map/ppermute | solution.py:249
  10.4 0.7 %shard_map.81 = (bf16[4,4,128,256]{3,2,1,0:T(8,128)(2,1)S(1)}, f32[4,4,1,256]{3,2,1,0:T(1,128)S(1)}, bf16[512,128]{1,0:T(8,128)(2,1)S(1)}) custom-call(f32[4,4,128,256]{3,2,1,0:T(8,128)S(1)} %get-tuple-element.36.probs, f32[4,4,1,256]{3,2,1,0:T(1,128)S(1)} %get-tuple-element.37.own_delta, bf16[4,1024,128]{2,1,0:T(8,128)(2,1)S(1)} %get-tuple-element.30.query, ...), custom_call_target="tpu_custom_call" | custom-call | flops 2000000000 | tf_op jit(solution)/shard_map/pallas_call | solution.py:295
  11.2 2.2 %collective-permute-start.5 = (bf16[512,128]{1,0:T(8,128)(2,1)S(1)}, bf16[512,128]{1,0:T(8,128)(2,1)S(1)}, u32[]{:S(2)}, u32[]{:S(2)}) collective-permute-start(bf16[512,128]{1,0:T(8,128)(2,1)S(1)} %get-tuple-element.49), channel_id=1, source_target_pairs={{8,0},{9,1},{10,2},{11,3},{12,4},{13,5},{14,6},{15,7},{16,8},{17,9... | collective-permute-start | bytes 393224 | tf_op jit(solution)/shard_map/ppermute | solution.py:304
  13.4 1.3 %collective-permute-start.4 = (s32[1,5]{1,0:T(1,128)S(1)}, s32[1,5]{1,0:T(1,128)S(1)}, u32[]{:S(2)}, u32[]{:S(2)}) collective-permute-start(s32[1,5]{1,0:T(1,128)S(1)} %add.10), channel_id=1, source_target_pairs={{0,2},{1,3},{2,0},{3,1},{4,6},{5,7},{6,4},{7,5},{8,10},{9,11},{10,... | collective-permute-start | bytes 68 | tf_op jit(solution)/shard_map/ppermute | solution.py:228
  14.7 1.5 %shard_map.82 = (f32[4096,128]{1,0:T(8,128)S(1)}, f32[512,128]{1,0:T(8,128)S(1)}) custom-call(f32[4,4,128,256]{3,2,1,0:T(8,128)S(1)} %get-tuple-element.36.probs, f32[4,4,128,256]{3,2,1,0:T(8,128)S(1)} %get-tuple-element.42.own_prob_grad, f32[4,4,1,256]{3,2,1,0:T(1,128)S(1)} %get-tuple-element.43.delta, ...), custom_call_target="tpu_custom_call" | custom-call | tf_op jit(solution)/shard_map/pallas_call | solution.py:311
  16.2 0.0 collective-permute-done.4
  16.2 1.2 %shard_map.83 = bf16[4096,128]{1,0:T(8,128)(2,1)} custom-call(s32[1,5]{1,0:T(1,128)S(1)} %add.11.count, f32[4096,128]{1,0:T(8,128)S(1)} %get-tuple-element.47.query_in), custom_call_target="tpu_custom_call" | custom-call | tf_op jit(solution)/shard_map/pallas_call | solution.py:317
  17.4 0.0 collective-permute-done.5.back
  17.4 0.8 %shard_map.84 = bf16[512,128]{1,0:T(8,128)(2,1)} custom-call(s32[1,5]{1,0:T(1,128)S(1)} %add.11.count, f32[512,128]{1,0:T(8,128)S(1)} %get-tuple-element.48.own, bf16[512,128]{1,0:T(8,128)(2,1)S(1)} %collective-permute-done.5.back), custom_call_target="tpu_custom_call" | custom-call | tf_op jit(solution)/shard_map/pallas_call | solution.py:324
  (11 shorter events, 0.1 us)
Async XLA Ops:
  0.6 7.1 %copy-start.2 = (bf16[1,128,4,128]{3,2,1,0:T(4,128)(2,1)S(1)}, bf16[1,128,4,128]{3,2,1,0:T(4,128)(2,1)}, u32[]{:S(2)}) copy-start(bf16[1,128,4,128]{3,2,1,0:T(4,128)(2,1)} %param.7) | copy-start | bytes 393220
  0.6 4.4 %copy-start.5 = (s32[1,5]{1,0:T(1,128)S(1)}, s32[1,5]{1,0:T(1,128)}, u32[]{:S(2)}) copy-start(s32[1,5]{1,0:T(1,128)} %bounds.1) | copy-start | bytes 64
  0.7 7.1 %copy-start.3 = (bf16[1,128,4,128]{3,2,1,0:T(4,128)(2,1)S(1)}, bf16[1,128,4,128]{3,2,1,0:T(4,128)(2,1)}, u32[]{:S(2)}) copy-start(bf16[1,128,4,128]{3,2,1,0:T(4,128)(2,1)} %param.8) | copy-start | bytes 393220
  0.7 4.3 %copy-start.4 = (s32[32]{0:T(128)S(1)}, s32[32]{0:T(128)}, u32[]{:S(2)}) copy-start(s32[32]{0:T(128)} %param.11) | copy-start | bytes 388
  0.7 7.1 %copy-start.1 = (bf16[1,128,32,128]{3,2,1,0:T(8,128)(2,1)S(1)}, bf16[1,128,32,128]{3,2,1,0:T(8,128)(2,1)}, u32[]{:S(2)}) copy-start(bf16[1,128,32,128]{3,2,1,0:T(8,128)(2,1)} %param.9) | copy-start | bytes 3145732
  0.7 7.1 %copy-start = (bf16[1,128,32,128]{3,2,1,0:T(8,128)(2,1)S(1)}, bf16[1,128,32,128]{3,2,1,0:T(8,128)(2,1)}, u32[]{:S(2)}) copy-start(bf16[1,128,32,128]{3,2,1,0:T(8,128)(2,1)} %param.6) | copy-start | bytes 3145732
  0.7 7.9 %collective-permute-start.2 = (bf16[1,128,4,128]{3,2,1,0:T(4,128)(2,1)}, bf16[1,128,4,128]{3,2,1,0:T(4,128)(2,1)S(1)}, u32[]{:S(2)}, u32[]{:S(2)}) collective-permute-start(bf16[1,128,4,128]{3,2,1,0:T(4,128)(2,1)} %param.7), channel_id=1, source_target_pairs={{0,8},{1,9},{2,10},{3,11},{4,12},{5,13},{6,14},{7,15},{8,16},{9,17... | collective-permute-start | bytes 393224 | tf_op jit(solution)/shard_map/ppermute | solution.py:248
  2.8 2.6 %collective-permute-start = (s32[1,5]{1,0:T(1,128)}, s32[1,5]{1,0:T(1,128)S(1)}, u32[]{:S(2)}, u32[]{:S(2)}) collective-permute-start(s32[1,5]{1,0:T(1,128)} %bounds.1), channel_id=1, source_target_pairs={{0,1},{1,0},{2,3},{3,2},{4,5},{5,4},{6,7},{7,6},{8,9},{9,8},{10,11... | collective-permute-start | bytes 68 | tf_op jit(solution)/shard_map/ppermute | solution.py:228
  3.7 6.7 %collective-permute-start.3 = (bf16[1,128,4,128]{3,2,1,0:T(4,128)(2,1)}, bf16[1,128,4,128]{3,2,1,0:T(4,128)(2,1)S(1)}, u32[]{:S(2)}, u32[]{:S(2)}) collective-permute-start(bf16[1,128,4,128]{3,2,1,0:T(4,128)(2,1)} %param.8), channel_id=1, source_target_pairs={{0,8},{1,9},{2,10},{3,11},{4,12},{5,13},{6,14},{7,15},{8,16},{9,17... | collective-permute-start | bytes 393224 | tf_op jit(solution)/shard_map/ppermute | solution.py:249
  5.4 4.3 %collective-permute-start.1 = (s32[1,5]{1,0:T(1,128)S(1)}, s32[1,5]{1,0:T(1,128)S(1)}, u32[]{:S(2)}, u32[]{:S(2)}) collective-permute-start(s32[1,5]{1,0:T(1,128)S(1)} %add.9), channel_id=1, source_target_pairs={{0,4},{1,5},{2,6},{3,7},{4,0},{5,1},{6,2},{7,3},{8,12},{9,13},{10,... | collective-permute-start | bytes 68 | tf_op jit(solution)/shard_map/ppermute | solution.py:228
  11.2 6.2 %collective-permute-start.5 = (bf16[512,128]{1,0:T(8,128)(2,1)S(1)}, bf16[512,128]{1,0:T(8,128)(2,1)S(1)}, u32[]{:S(2)}, u32[]{:S(2)}) collective-permute-start(bf16[512,128]{1,0:T(8,128)(2,1)S(1)} %get-tuple-element.49), channel_id=1, source_target_pairs={{8,0},{9,1},{10,2},{11,3},{12,4},{13,5},{14,6},{15,7},{16,8},{17,9... | collective-permute-start | bytes 393224 | tf_op jit(solution)/shard_map/ppermute | solution.py:304
  13.4 2.8 %collective-permute-start.4 = (s32[1,5]{1,0:T(1,128)S(1)}, s32[1,5]{1,0:T(1,128)S(1)}, u32[]{:S(2)}, u32[]{:S(2)}) collective-permute-start(s32[1,5]{1,0:T(1,128)S(1)} %add.10), channel_id=1, source_target_pairs={{0,2},{1,3},{2,0},{3,1},{4,6},{5,7},{6,4},{7,5},{8,10},{9,11},{10,... | collective-permute-start | bytes 68 | tf_op jit(solution)/shard_map/ppermute | solution.py:228

commit v8 on v7

--- a/solution.py
+++ b/solution.py
@@ -13,7 +13,7 @@
 TN = (((0,), (0,)), ((), ()))
 F32, BF16 = jnp.float32, jnp.bfloat16
 BLOCK = 256
-PIECES = 2
+PIECES = 4
 
 
 def dot(a, b, dims=NN):
@@ -148,11 +148,8 @@
     back[...] = flat[...].astype(BF16)
 
 
-def query_kernel(sizes, probs, own_prob_grad, delta, back_score, query, own_key, back_key, unsort, query_grad, key_grad, part_grad, own_score):
-    tok, heads, groups, per = sizes
-    depth = own_key.shape[2]
-    step = BLOCK // heads
-    share = step * per
+def query_kernel(sizes, probs, own_prob_grad, delta, back_score, query, own_key, back_key, part_grad, key_grad, own_score):
+    tok, heads, groups, per = sizes
     here = BLOCK // per
     own = own_mask(per)
     for g in range(groups):
@@ -172,33 +169,34 @@
             rows = query[g, t * BLOCK : (t + 1) * BLOCK, :]
             add_rows(sums, 0, dot(own_score[g, t, : (t + 1) * here, :], rows), here)
         key_grad[pl.ds(g, tok, stride=groups), :] = jnp.concatenate(sums, axis=0)
+
+def factor_of(count, tokens, depth):
+    last = count.shape[1] - 1
+    return (tokens / count[0:1, last : last + 1].astype(F32)) * (1.0 / math.sqrt(depth))
+
+
+def query_out_kernel(sizes, tokens, count, part_grad, unsort, query_out, query_grad, sems):
+    tok, heads, groups, per = sizes
+    depth = part_grad.shape[2]
+    factor = factor_of(count, tokens, depth)
+    step = BLOCK // heads
+    share = step * per
+    rows = tok * heads // PIECES
+    copies = []
     for b in range(0, tok // step, 2):
         both = [
             jnp.concatenate([part_grad[g, (b + i) * share : (b + i + 1) * share, :] for g in range(groups)], axis=0)
             for i in range(2)
         ]
-        both = jnp.concatenate(both, axis=1)
-        high = both.astype(BF16)
-        low = (both - high.astype(F32)).astype(BF16)
-        both = dot(unsort[...], high) + dot(unsort[...], low)
+        both = (jnp.concatenate(both, axis=1) * factor).astype(BF16)
+        both = dot(unsort[...], both).astype(BF16)
         query_grad[b * BLOCK : (b + 1) * BLOCK, :] = both[:, :depth]
         query_grad[(b + 1) * BLOCK : (b + 2) * BLOCK, :] = both[:, depth:]
-
-
-def factor_of(count, tokens, depth):
-    last = count.shape[1] - 1
-    return (tokens / count[0:1, last : last + 1].astype(F32)) * (1.0 / math.sqrt(depth))
-
-
-def query_out_kernel(tokens, count, query_in, query_out, query_grad, sems):
-    rows, depth = query_in.shape
-    factor = factor_of(count, tokens, depth)
-    copies = []
-    for i in range(PIECES):
-        part = pl.ds(i * (rows // PIECES), rows // PIECES)
-        query_grad[part, :] = (query_in[part, :] * factor).astype(BF16)
-        copies.append(pltpu.make_async_copy(query_grad.at[part], query_out.at[part], sems.at[i]))
-        copies[-1].start()
+        done = (b + 2) * BLOCK
+        if done % rows == 0:
+            part = pl.ds(done - rows, rows)
+            copies.append(pltpu.make_async_copy(query_grad.at[part], query_out.at[part], sems.at[len(copies)]))
+            copies[-1].start()
     for copy in copies:
         copy.wait()
 
@@ -243,9 +241,10 @@
     swap = 1 if copies % 2 == 0 else 0
     ahead = [(c * copies + i, (c + 1) * copies + i) for c in range(ctx - 1) for i in range(copies)]
     behind = [(b, a) for a, b in ahead] + [(i ^ swap, (ctx - 1) * copies + i) for i in range(copies)]
+    keys_ahead = ahead + [((ctx - 1) * copies + i, i ^ swap) for i in range(copies)]
     ahead += [((ctx - 1) * copies + i, i) for i in range(copies)]
 
-    back_key = lax.ppermute(key_rows, axes, ahead).reshape(tok * groups, depth)
+    back_key = lax.ppermute(key_rows, axes, keys_ahead).reshape(tok * groups, depth)
     back_value = lax.ppermute(value_matrix, axes, ahead).reshape(tok * groups, depth)
     dp = lax.axis_size("dp")
     paired = dp >= 8 and dp & (dp - 1) == 0
@@ -308,19 +307,19 @@
     else:
         count = moved
 
-    plain_grad, own = call(
+    part_grad, own = call(
         functools.partial(query_kernel, sizes),
-        [VMEM] * 8,
-        [((tok * heads, depth), F32), (packed, F32)],
-        [pltpu.VMEM(sorted_shape, F32), pltpu.VMEM(tall, BF16)],
-    )(probs, own_prob_grad, delta, back_score, sorted_query, own_key, back_key, unsort)
+        [VMEM] * 7,
+        [(sorted_shape, F32), (packed, F32)],
+        [pltpu.VMEM(tall, BF16)],
+    )(probs, own_prob_grad, delta, back_score, sorted_query, own_key, back_key)
     (query_grad,) = call(
-        functools.partial(query_out_kernel, tokens),
-        [VMEM] * 2,
+        functools.partial(query_out_kernel, sizes, tokens),
+        [VMEM] * 3,
         [((tok * heads, depth), BF16)],
         [pltpu.VMEM((tok * heads, depth), BF16), pltpu.SemaphoreType.DMA((PIECES,))],
         out_spec=HBM,
-    )(count, plain_grad)
+    )(count, part_grad, unsort)
     (key_grad,) = call(functools.partial(key_out_kernel, tokens), [VMEM] * 3, [(packed, BF16)])(count, own, back)
     return (query_grad.reshape(query_rows.shape), key_grad.reshape(key_rows.shape))
 

time: 18.3 us -> 18.3 us (level)
  the two profiles are of different devices: /device:TPU:1 before, /device:TPU:0 now
where the time goes in v8:
time: 18.3 us; the launch traced here: 18 us
  starting transfers between devices  9.62 us (53%)
  Pallas kernels  6.01 us (33%)
  waiting for transfers between devices  1.56 us (9%)
  between operations  0.78 us (4%)
    ppermute x3, starting transfers between devices, partner(): lax.ppermute(value, axis, [(i, i ^ hop) for i in range(lax.axis_size(axis...  4.76 us
    ppermute x1, starting transfers between devices, per_device(): lax.ppermute(key_rows, axes, keys_ahead).reshape(tok * groups, depth)  3 us
    ppermute x1, starting transfers between devices, per_device(): lax.ppermute(value_matrix, axes, ahead).reshape(tok * groups, depth)  1.49 us
    pallas_call x1, Pallas kernels, per_device(): call(functools.partial(query_out_kernel, sizes, tokens), [VMEM] * 3, [((t...  1.32 us
    pallas_call x1, Pallas kernels, per_device(): call(functools.partial(probs_kernel, sizes), [VMEM] * 6, [(tall, F32), (t...  1.11 us
    ppermute x1, waiting for transfers between devices, per_device(): lax.ppermute(value_matrix, axes, ahead).reshape(tok * groups, depth)  1 us
    pallas_call x1, Pallas kernels, per_device(): call(functools.partial(query_kernel, sizes), [VMEM] * 7, [(sorted_shape,...  0.97 us
    pallas_call x1, Pallas kernels, per_device(): call(functools.partial(key_out_kernel, tokens), [VMEM] * 3, [(packed, BF1...  0.76 us
  transfers between devices with their start and end apart: 6, of which 2 were waited for; matrix products, arithmetic and copies ran while one was open for 0% of the time, Pallas kernels for 25%

profile of v8, /device:TPU:0, one launch (start us, length us, event | category | flops | bytes accessed | tf_op | source)
XLA Modules:
  0.0 18.0 jit_solution(10783823866010613653)
XLA Ops:
  0.6 0.0 copy-start.2
  0.7 3.0 %collective-permute-start.2 = (bf16[1,128,4,128]{3,2,1,0:T(4,128)(2,1)}, bf16[1,128,4,128]{3,2,1,0:T(4,128)(2,1)S(1)}, u32[]{:S(2)}, u32[]{:S(2)}) collective-permute-start(bf16[1,128,4,128]{3,2,1,0:T(4,128)(2,1)} %param.7), channel_id=1, source_target_pairs={{0,8},{1,9},{2,10},{3,11},{4,12},{5,13},{6,14},{7,15},{8,16},{9,17... | collective-permute-start | bytes 393224 | tf_op jit(solution)/shard_map/ppermute | solution.py:247
  3.7 0.0 collective-permute-start
  3.7 1.5 %collective-permute-start.3 = (bf16[1,128,4,128]{3,2,1,0:T(4,128)(2,1)}, bf16[1,128,4,128]{3,2,1,0:T(4,128)(2,1)S(1)}, u32[]{:S(2)}, u32[]{:S(2)}) collective-permute-start(bf16[1,128,4,128]{3,2,1,0:T(4,128)(2,1)} %param.8), channel_id=1, source_target_pairs={{0,8},{1,9},{2,10},{3,11},{4,12},{5,13},{6,14},{7,15},{8,16},{9,17... | collective-permute-start | bytes 393224 | tf_op jit(solution)/shard_map/ppermute | solution.py:248
  5.2 0.0 copy-done.5
  5.2 0.0 copy-done.4
  5.2 0.4 %shard_map.78 = (bf16[256,256]{1,0:T(8,128)(2,1)S(1)}, bf16[256,256]{1,0:T(8,128)(2,1)S(1)}, f32[128,1024]{1,0:T(8,128)S(1)}) custom-call(s32[1,5]{1,0:T(1,128)S(1)} %copy-done.5, s32[1,32]{1,0:T(1,128)S(1)} %bitcast.14, s32[128,1024]{1,0:T(8,128)S(1)} %shard_map.77.places), custom_call_target="tpu_custom_call" | custom-call | tf_op jit(solution)/shard_map/pallas_call | solution.py:257
  5.6 0.0 collective-permute-done
  5.6 2.7 %collective-permute-start.1 = (s32[1,5]{1,0:T(1,128)S(1)}, s32[1,5]{1,0:T(1,128)S(1)}, u32[]{:S(2)}, u32[]{:S(2)}) collective-permute-start(s32[1,5]{1,0:T(1,128)S(1)} %add.9), channel_id=1, source_target_pairs={{0,4},{1,5},{2,6},{3,7},{4,0},{5,1},{6,2},{7,3},{8,12},{9,13},{10,... | collective-permute-start | bytes 68 | tf_op jit(solution)/shard_map/ppermute | solution.py:226
  8.3 0.0 copy-done.2
  8.3 0.0 copy-done.1
  8.3 0.7 %shard_map.79 = (bf16[4,1024,128]{2,1,0:T(8,128)(2,1)S(1)}, bf16[4,1024,128]{2,1,0:T(8,128)(2,1)S(1)}, bf16[4,128,128]{2,1,0:T(8,128)(2,1)S(1)}, bf16[4,128,128]{2,1,0:T(8,128)(2,1)S(1)}) custom-call(bf16[256,256]{1,0:T(8,128)(2,1)S(1)} %get-tuple-element.29.sort, bf16[4096,128]{1,0:T(8,128)(2,1)S(1)} %bitcast.9, bf16[4096,128]{1,0:T(8,128)(2,1)S(1)} %bitcast.10, ...), custom_call_target="tpu_custom_call" | custom-call | tf_op jit(solution)/shard_map/pallas_call | solution.py:267
  9.0 0.0 collective-permute-done.2
  9.0 1.1 %shard_map.80 = (f32[4,4,128,256]{3,2,1,0:T(8,128)S(1)}, f32[4,4,128,256]{3,2,1,0:T(8,128)S(1)}, f32[4,4,1,256]{3,2,1,0:T(1,128)S(1)}, bf16[4,128,128]{2,1,0:T(8,128)(2,1)S(1)}) custom-call(f32[128,1024]{1,0:T(8,128)S(1)} %get-tuple-element.28.bias, bf16[4,1024,128]{2,1,0:T(8,128)(2,1)S(1)} %get-tuple-element.30.query, ...), custom_call_target="tpu_custom_call" | custom-call | flops 500000000 | tf_op jit(solution)/shard_map/pallas_call | solution.py:282
  10.1 0.0 collective-permute-done.1
  10.2 1.0 %collective-permute-done.3 = bf16[1,128,4,128]{3,2,1,0:T(4,128)(2,1)S(1)} collective-permute-done((bf16[1,128,4,128]{3,2,1,0:T(4,128)(2,1)}, bf16[1,128,4,128]{3,2,1,0:T(4,128)(2,1)S(1)}, u32[]{:S(2)}, u32[]{:S(2)}) %collective-permute-start.3) | collective-permute-done | bytes 131104 | tf_op jit(solution)/shard_map/ppermute | solution.py:248
  11.2 0.7 %shard_map.81 = (bf16[4,4,128,256]{3,2,1,0:T(8,128)(2,1)S(1)}, f32[4,4,1,256]{3,2,1,0:T(1,128)S(1)}, bf16[512,128]{1,0:T(8,128)(2,1)S(1)}) custom-call(f32[4,4,128,256]{3,2,1,0:T(8,128)S(1)} %get-tuple-element.36.probs, f32[4,4,1,256]{3,2,1,0:T(1,128)S(1)} %get-tuple-element.37.own_delta, bf16[4,1024,128]{2,1,0:T(8,128)(2,1)S(1)} %get-tuple-element.30.query, ...), custom_call_target="tpu_custom_call" | custom-call | flops 2000000000 | tf_op jit(solution)/shard_map/pallas_call | solution.py:294
  11.9 0.4 %collective-permute-start.5 = (bf16[512,128]{1,0:T(8,128)(2,1)S(1)}, bf16[512,128]{1,0:T(8,128)(2,1)S(1)}, u32[]{:S(2)}, u32[]{:S(2)}) collective-permute-start(bf16[512,128]{1,0:T(8,128)(2,1)S(1)} %get-tuple-element.49), channel_id=1, source_target_pairs={{8,0},{9,1},{10,2},{11,3},{12,4},{13,5},{14,6},{15,7},{16,8},{17,9... | collective-permute-start | bytes 393224 | tf_op jit(solution)/shard_map/ppermute | solution.py:303
  12.3 2.1 %collective-permute-start.4 = (s32[1,5]{1,0:T(1,128)S(1)}, s32[1,5]{1,0:T(1,128)S(1)}, u32[]{:S(2)}, u32[]{:S(2)}) collective-permute-start(s32[1,5]{1,0:T(1,128)S(1)} %add.10), channel_id=1, source_target_pairs={{0,2},{1,3},{2,0},{3,1},{4,6},{5,7},{6,4},{7,5},{8,10},{9,11},{10,... | collective-permute-start | bytes 68 | tf_op jit(solution)/shard_map/ppermute | solution.py:226
  14.4 1.0 %shard_map.82 = (f32[4,1024,128]{2,1,0:T(8,128)S(1)}, f32[512,128]{1,0:T(8,128)S(1)}) custom-call(f32[4,4,128,256]{3,2,1,0:T(8,128)S(1)} %get-tuple-element.36.probs, f32[4,4,128,256]{3,2,1,0:T(8,128)S(1)} %get-tuple-element.42.own_prob_grad, f32[4,4,1,256]{3,2,1,0:T(1,128)S(1)} %get-tuple-element.43.delta, ...), custom_call_target="tpu_custom_call" | custom-call | tf_op jit(solution)/shard_map/pallas_call | solution.py:310
  15.4 0.5 %collective-permute-done.4 = s32[1,5]{1,0:T(1,128)S(1)} collective-permute-done((s32[1,5]{1,0:T(1,128)S(1)}, s32[1,5]{1,0:T(1,128)S(1)}, u32[]{:S(2)}, u32[]{:S(2)}) %collective-permute-start.4) | collective-permute-done | bytes 52 | tf_op jit(solution)/shard_map/ppermute | solution.py:226
  15.9 1.3 %shard_map.83 = bf16[4096,128]{1,0:T(8,128)(2,1)} custom-call(s32[1,5]{1,0:T(1,128)S(1)} %add.11.count, f32[4,1024,128]{2,1,0:T(8,128)S(1)} %get-tuple-element.46.part_grad, bf16[256,256]{1,0:T(8,128)(2,1)S(1)} %get-tuple-element.47.unsort), custom_call_target="tpu_custom_call" | custom-call | tf_op jit(solution)/shard_map/pallas_call | solution.py:316
  17.2 0.0 collective-permute-done.5.back
  17.2 0.8 %shard_map.84 = bf16[512,128]{1,0:T(8,128)(2,1)} custom-call(s32[1,5]{1,0:T(1,128)S(1)} %add.11.count, f32[512,128]{1,0:T(8,128)S(1)} %get-tuple-element.48.own, bf16[512,128]{1,0:T(8,128)(2,1)S(1)} %collective-permute-done.5.back), custom_call_target="tpu_custom_call" | custom-call | tf_op jit(solution)/shard_map/pallas_call | solution.py:323
  (11 shorter events, 0.1 us)
Async XLA Ops:
  0.6 7.7 %copy-start.2 = (bf16[1,128,4,128]{3,2,1,0:T(4,128)(2,1)S(1)}, bf16[1,128,4,128]{3,2,1,0:T(4,128)(2,1)}, u32[]{:S(2)}) copy-start(bf16[1,128,4,128]{3,2,1,0:T(4,128)(2,1)} %param.7) | copy-start | bytes 393220
  0.6 4.6 %copy-start.5 = (s32[1,5]{1,0:T(1,128)S(1)}, s32[1,5]{1,0:T(1,128)}, u32[]{:S(2)}) copy-start(s32[1,5]{1,0:T(1,128)} %bounds.1) | copy-start | bytes 64
  0.7 7.6 %copy-start.3 = (bf16[1,128,4,128]{3,2,1,0:T(4,128)(2,1)S(1)}, bf16[1,128,4,128]{3,2,1,0:T(4,128)(2,1)}, u32[]{:S(2)}) copy-start(bf16[1,128,4,128]{3,2,1,0:T(4,128)(2,1)} %param.8) | copy-start | bytes 393220
  0.7 4.6 %copy-start.4 = (s32[32]{0:T(128)S(1)}, s32[32]{0:T(128)}, u32[]{:S(2)}) copy-start(s32[32]{0:T(128)} %param.11) | copy-start | bytes 388
  0.7 7.6 %copy-start.1 = (bf16[1,128,32,128]{3,2,1,0:T(8,128)(2,1)S(1)}, bf16[1,128,32,128]{3,2,1,0:T(8,128)(2,1)}, u32[]{:S(2)}) copy-start(bf16[1,128,32,128]{3,2,1,0:T(8,128)(2,1)} %param.9) | copy-start | bytes 3145732
  0.7 7.6 %copy-start = (bf16[1,128,32,128]{3,2,1,0:T(8,128)(2,1)S(1)}, bf16[1,128,32,128]{3,2,1,0:T(8,128)(2,1)}, u32[]{:S(2)}) copy-start(bf16[1,128,32,128]{3,2,1,0:T(8,128)(2,1)} %param.6) | copy-start | bytes 3145732
  0.7 8.3 %collective-permute-start.2 = (bf16[1,128,4,128]{3,2,1,0:T(4,128)(2,1)}, bf16[1,128,4,128]{3,2,1,0:T(4,128)(2,1)S(1)}, u32[]{:S(2)}, u32[]{:S(2)}) collective-permute-start(bf16[1,128,4,128]{3,2,1,0:T(4,128)(2,1)} %param.7), channel_id=1, source_target_pairs={{0,8},{1,9},{2,10},{3,11},{4,12},{5,13},{6,14},{7,15},{8,16},{9,17... | collective-permute-start | bytes 393224 | tf_op jit(solution)/shard_map/ppermute | solution.py:247
  3.7 1.9 %collective-permute-start = (s32[1,5]{1,0:T(1,128)}, s32[1,5]{1,0:T(1,128)S(1)}, u32[]{:S(2)}, u32[]{:S(2)}) collective-permute-start(s32[1,5]{1,0:T(1,128)} %bounds.1), channel_id=1, source_target_pairs={{0,1},{1,0},{2,3},{3,2},{4,5},{5,4},{6,7},{7,6},{8,9},{9,8},{10,11... | collective-permute-start | bytes 68 | tf_op jit(solution)/shard_map/ppermute | solution.py:226
  3.7 7.5 %collective-permute-start.3 = (bf16[1,128,4,128]{3,2,1,0:T(4,128)(2,1)}, bf16[1,128,4,128]{3,2,1,0:T(4,128)(2,1)S(1)}, u32[]{:S(2)}, u32[]{:S(2)}) collective-permute-start(bf16[1,128,4,128]{3,2,1,0:T(4,128)(2,1)} %param.8), channel_id=1, source_target_pairs={{0,8},{1,9},{2,10},{3,11},{4,12},{5,13},{6,14},{7,15},{8,16},{9,17... | collective-permute-start | bytes 393224 | tf_op jit(solution)/shard_map/ppermute | solution.py:248
  5.6 4.5 %collective-permute-start.1 = (s32[1,5]{1,0:T(1,128)S(1)}, s32[1,5]{1,0:T(1,128)S(1)}, u32[]{:S(2)}, u32[]{:S(2)}) collective-permute-start(s32[1,5]{1,0:T(1,128)S(1)} %add.9), channel_id=1, source_target_pairs={{0,4},{1,5},{2,6},{3,7},{4,0},{5,1},{6,2},{7,3},{8,12},{9,13},{10,... | collective-permute-start | bytes 68 | tf_op jit(solution)/shard_map/ppermute | solution.py:226
  11.9 5.3 %collective-permute-start.5 = (bf16[512,128]{1,0:T(8,128)(2,1)S(1)}, bf16[512,128]{1,0:T(8,128)(2,1)S(1)}, u32[]{:S(2)}, u32[]{:S(2)}) collective-permute-start(bf16[512,128]{1,0:T(8,128)(2,1)S(1)} %get-tuple-element.49), channel_id=1, source_target_pairs={{8,0},{9,1},{10,2},{11,3},{12,4},{13,5},{14,6},{15,7},{16,8},{17,9... | collective-permute-start | bytes 393224 | tf_op jit(solution)/shard_map/ppermute | solution.py:303
  12.3 3.6 %collective-permute-start.4 = (s32[1,5]{1,0:T(1,128)S(1)}, s32[1,5]{1,0:T(1,128)S(1)}, u32[]{:S(2)}, u32[]{:S(2)}) collective-permute-start(s32[1,5]{1,0:T(1,128)S(1)} %add.10), channel_id=1, source_target_pairs={{0,2},{1,3},{2,0},{3,1},{4,6},{5,7},{6,4},{7,5},{8,10},{9,11},{10,... | collective-permute-start | bytes 68 | tf_op jit(solution)/shard_map/ppermute | solution.py:226

commit v9 on v7

--- a/solution.py
+++ b/solution.py
@@ -13,7 +13,7 @@
 TN = (((0,), (0,)), ((), ()))
 F32, BF16 = jnp.float32, jnp.bfloat16
 BLOCK = 256
-PIECES = 2
+PIECES = 4
 
 
 def dot(a, b, dims=NN):
@@ -190,9 +190,10 @@
     return (tokens / count[0:1, last : last + 1].astype(F32)) * (1.0 / math.sqrt(depth))
 
 
-def query_out_kernel(tokens, count, query_in, query_out, query_grad, sems):
+def query_out_kernel(tokens, count, query_in, query_out, factor_out, query_grad, sems):
     rows, depth = query_in.shape
     factor = factor_of(count, tokens, depth)
+    factor_out[...] = jnp.broadcast_to(factor, factor_out.shape)
     copies = []
     for i in range(PIECES):
         part = pl.ds(i * (rows // PIECES), rows // PIECES)
@@ -203,11 +204,6 @@
         copy.wait()
 
 
-def key_out_kernel(tokens, count, own, back, key_grad):
-    factor = factor_of(count, tokens, own.shape[1])
-    key_grad[...] = ((own[...] + back[...].astype(F32)) * factor).astype(BF16)
-
-
 VMEM = pl.BlockSpec(memory_space=pltpu.VMEM)
 HBM = pl.BlockSpec(memory_space=pltpu.HBM)
 
@@ -217,7 +213,7 @@
         kernel,
         out_shape=[jax.ShapeDtypeStruct(shape, dtype) for shape, dtype in outs],
         in_specs=ins,
-        out_specs=[out_spec] * len(outs),
+        out_specs=out_spec if isinstance(out_spec, list) else [out_spec] * len(outs),
         scratch_shapes=list(scratch),
         cost_estimate=None if flops is None else pl.CostEstimate(flops=flops, bytes_accessed=0, transcendentals=0),
         compiler_params=pltpu.CompilerParams(vmem_limit_bytes=32 * 1024 * 1024),
@@ -243,9 +239,10 @@
     swap = 1 if copies % 2 == 0 else 0
     ahead = [(c * copies + i, (c + 1) * copies + i) for c in range(ctx - 1) for i in range(copies)]
     behind = [(b, a) for a, b in ahead] + [(i ^ swap, (ctx - 1) * copies + i) for i in range(copies)]
-    ahead += [((ctx - 1) * copies + i, i) for i in range(copies)]
-
-    back_key = lax.ppermute(key_rows, axes, ahead).reshape(tok * groups, depth)
+    keys_ahead = ahead + [((ctx - 1) * copies + i, i ^ swap) for i in range(copies)]
+    ahead = ahead + [((ctx - 1) * copies + i, i) for i in range(copies)]
+
+    back_key = lax.ppermute(key_rows, axes, keys_ahead).reshape(tok * groups, depth)
     back_value = lax.ppermute(value_matrix, axes, ahead).reshape(tok * groups, depth)
     dp = lax.axis_size("dp")
     paired = dp >= 8 and dp & (dp - 1) == 0
@@ -314,14 +311,14 @@
         [((tok * heads, depth), F32), (packed, F32)],
         [pltpu.VMEM(sorted_shape, F32), pltpu.VMEM(tall, BF16)],
     )(probs, own_prob_grad, delta, back_score, sorted_query, own_key, back_key, unsort)
-    (query_grad,) = call(
+    query_grad, factor = call(
         functools.partial(query_out_kernel, tokens),
         [VMEM] * 2,
-        [((tok * heads, depth), BF16)],
+        [((tok * heads, depth), BF16), ((1, depth), F32)],
         [pltpu.VMEM((tok * heads, depth), BF16), pltpu.SemaphoreType.DMA((PIECES,))],
-        out_spec=HBM,
+        out_spec=[HBM, VMEM],
     )(count, plain_grad)
-    (key_grad,) = call(functools.partial(key_out_kernel, tokens), [VMEM] * 3, [(packed, BF16)])(count, own, back)
+    key_grad = ((own + back.astype(F32)) * factor).astype(BF16)
     return (query_grad.reshape(query_rows.shape), key_grad.reshape(key_rows.shape))
 
 

time: 18.3 us -> 18.2 us (level)
  Pallas kernels: 6.46 us -> 5.64 us
  other arithmetic: 0.01 us -> 0.71 us
    pallas_call x1 -> x0, Pallas kernels: 0.76 us -> none  [per_device(): call(functools.partial(key_out_kernel, tokens), [VMEM] * 3, [(packed, BF1...]
    convert_element_type x0 -> x1, other arithmetic: none -> 0.7 us  [per_device(): key_grad = ((own + back.astype(F32)) * factor).astype(BF16)]
where the time goes in v9:
time: 18.2 us; the launch traced here: 18.1 us
  starting transfers between devices  10.1 us (55%)
  Pallas kernels  5.64 us (31%)
  between operations  0.79 us (4%)
  waiting for transfers between devices  0.78 us (4%)
  other arithmetic  0.71 us (4%)
    ppermute x3, starting transfers between devices, partner(): lax.ppermute(value, axis, [(i, i ^ hop) for i in range(lax.axis_size(axis...  4.63 us
    ppermute x1, starting transfers between devices, per_device(): back = lax.ppermute(back, axes, behind)  2.18 us
    ppermute x1, starting transfers between devices, per_device(): lax.ppermute(key_rows, axes, keys_ahead).reshape(tok * groups, depth)  2.1 us
    pallas_call x1, Pallas kernels, per_device(): call(functools.partial(query_kernel, sizes), [VMEM] * 8, [((tok * heads,...  1.54 us
    ppermute x1, starting transfers between devices, per_device(): lax.ppermute(value_matrix, axes, ahead).reshape(tok * groups, depth)  1.21 us
    pallas_call x1, Pallas kernels, per_device(): call(functools.partial(query_out_kernel, tokens), [VMEM] * 2, [((tok * he...  1.12 us
    pallas_call x1, Pallas kernels, per_device(): call(functools.partial(probs_kernel, sizes), [VMEM] * 6, [(tall, F32), (t...  1.11 us
    ppermute x1, waiting for transfers between devices, per_device(): lax.ppermute(value_matrix, axes, ahead).reshape(tok * groups, depth)  0.76 us
  transfers between devices with their start and end apart: 6, of which 1 were waited for; matrix products, arithmetic and copies ran while one was open for 0% of the time, Pallas kernels for 27%

profile of v9, /device:TPU:1, one launch (start us, length us, event | category | flops | bytes accessed | tf_op | source)
XLA Modules:
  0.0 18.1 jit_solution(13058733448560591057)
XLA Ops:
  0.6 0.0 copy-start.2
  0.6 0.0 copy-start.5
  0.7 0.0 copy-start.3
  0.7 0.0 copy-start.4
  0.7 2.1 %collective-permute-start.2 = (bf16[1,128,4,128]{3,2,1,0:T(4,128)(2,1)}, bf16[1,128,4,128]{3,2,1,0:T(4,128)(2,1)S(1)}, u32[]{:S(2)}, u32[]{:S(2)}) collective-permute-start(bf16[1,128,4,128]{3,2,1,0:T(4,128)(2,1)} %param.7), channel_id=1, source_target_pairs={{0,8},{1,9},{2,10},{3,11},{4,12},{5,13},{6,14},{7,15},{8,16},{9,17... | collective-permute-start | bytes 393224 | tf_op jit(solution)/shard_map/ppermute | solution.py:245
  2.8 1.0 %collective-permute-start = (s32[1,5]{1,0:T(1,128)}, s32[1,5]{1,0:T(1,128)S(1)}, u32[]{:S(2)}, u32[]{:S(2)}) collective-permute-start(s32[1,5]{1,0:T(1,128)} %bounds.1), channel_id=1, source_target_pairs={{0,1},{1,0},{2,3},{3,2},{4,5},{5,4},{6,7},{7,6},{8,9},{9,8},{10,11... | collective-permute-start | bytes 68 | tf_op jit(solution)/shard_map/ppermute | solution.py:224
  3.7 1.2 %collective-permute-start.3 = (bf16[1,128,4,128]{3,2,1,0:T(4,128)(2,1)}, bf16[1,128,4,128]{3,2,1,0:T(4,128)(2,1)S(1)}, u32[]{:S(2)}, u32[]{:S(2)}) collective-permute-start(bf16[1,128,4,128]{3,2,1,0:T(4,128)(2,1)} %param.8), channel_id=1, source_target_pairs={{0,8},{1,9},{2,10},{3,11},{4,12},{5,13},{6,14},{7,15},{8,16},{9,17... | collective-permute-start | bytes 393224 | tf_op jit(solution)/shard_map/ppermute | solution.py:246
  5.0 0.4 %shard_map.78 = (bf16[256,256]{1,0:T(8,128)(2,1)S(1)}, bf16[256,256]{1,0:T(8,128)(2,1)S(1)}, f32[128,1024]{1,0:T(8,128)S(1)}) custom-call(s32[1,5]{1,0:T(1,128)S(1)} %copy-done.5, s32[1,32]{1,0:T(1,128)S(1)} %bitcast.16, s32[128,1024]{1,0:T(8,128)S(1)} %shard_map.77.places), custom_call_target="tpu_custom_call" | custom-call | tf_op jit(solution)/shard_map/pallas_call | solution.py:255
  5.4 0.0 collective-permute-done
  5.4 2.4 %collective-permute-start.1 = (s32[1,5]{1,0:T(1,128)S(1)}, s32[1,5]{1,0:T(1,128)S(1)}, u32[]{:S(2)}, u32[]{:S(2)}) collective-permute-start(s32[1,5]{1,0:T(1,128)S(1)} %add.12), channel_id=1, source_target_pairs={{0,4},{1,5},{2,6},{3,7},{4,0},{5,1},{6,2},{7,3},{8,12},{9,13},{10,... | collective-permute-start | bytes 68 | tf_op jit(solution)/shard_map/ppermute | solution.py:224
  7.8 0.0 copy-done.3
  7.8 0.7 %shard_map.79 = (bf16[4,1024,128]{2,1,0:T(8,128)(2,1)S(1)}, bf16[4,1024,128]{2,1,0:T(8,128)(2,1)S(1)}, bf16[4,128,128]{2,1,0:T(8,128)(2,1)S(1)}, bf16[4,128,128]{2,1,0:T(8,128)(2,1)S(1)}) custom-call(bf16[256,256]{1,0:T(8,128)(2,1)S(1)} %get-tuple-element.31.sort, bf16[4096,128]{1,0:T(8,128)(2,1)S(1)} %bitcast.10, bf16[4096,128]{1,0:T(8,128)(2,1)S(1)} %bitcast.11, ...), custom_call_target="tpu_custom_call" | custom-call | tf_op jit(solution)/shard_map/pallas_call | solution.py:265
  8.5 0.0 collective-permute-done.2
  8.6 1.1 %shard_map.80 = (f32[4,4,128,256]{3,2,1,0:T(8,128)S(1)}, f32[4,4,128,256]{3,2,1,0:T(8,128)S(1)}, f32[4,4,1,256]{3,2,1,0:T(1,128)S(1)}, bf16[4,128,128]{2,1,0:T(8,128)(2,1)S(1)}) custom-call(f32[128,1024]{1,0:T(8,128)S(1)} %get-tuple-element.30.bias, bf16[4,1024,128]{2,1,0:T(8,128)(2,1)S(1)} %get-tuple-element.32.query, ...), custom_call_target="tpu_custom_call" | custom-call | flops 500000000 | tf_op jit(solution)/shard_map/pallas_call | solution.py:280
  9.7 0.0 collective-permute-done.1
  9.7 0.8 %collective-permute-done.3 = bf16[1,128,4,128]{3,2,1,0:T(4,128)(2,1)S(1)} collective-permute-done((bf16[1,128,4,128]{3,2,1,0:T(4,128)(2,1)}, bf16[1,128,4,128]{3,2,1,0:T(4,128)(2,1)S(1)}, u32[]{:S(2)}, u32[]{:S(2)}) %collective-permute-start.3) | collective-permute-done | bytes 131104 | tf_op jit(solution)/shard_map/ppermute | solution.py:246
  10.4 0.7 %shard_map.81 = (bf16[4,4,128,256]{3,2,1,0:T(8,128)(2,1)S(1)}, f32[4,4,1,256]{3,2,1,0:T(1,128)S(1)}, bf16[512,128]{1,0:T(8,128)(2,1)S(1)}) custom-call(f32[4,4,128,256]{3,2,1,0:T(8,128)S(1)} %get-tuple-element.38.probs, f32[4,4,1,256]{3,2,1,0:T(1,128)S(1)} %get-tuple-element.39.own_delta, bf16[4,1024,128]{2,1,0:T(8,128)(2,1)S(1)} %get-tuple-element.32.query, ...), custom_call_target="tpu_custom_call" | custom-call | flops 2000000000 | tf_op jit(solution)/shard_map/pallas_call | solution.py:292
  11.2 2.2 %collective-permute-start.5 = (bf16[512,128]{1,0:T(8,128)(2,1)S(1)}, bf16[512,128]{1,0:T(8,128)(2,1)S(1)}, u32[]{:S(2)}, u32[]{:S(2)}) collective-permute-start(bf16[512,128]{1,0:T(8,128)(2,1)S(1)} %get-tuple-element.52), channel_id=1, source_target_pairs={{8,0},{9,1},{10,2},{11,3},{12,4},{13,5},{14,6},{15,7},{16,8},{17,9... | collective-permute-start | bytes 393224 | tf_op jit(solution)/shard_map/ppermute | solution.py:301
  13.4 1.3 %collective-permute-start.4 = (s32[1,5]{1,0:T(1,128)S(1)}, s32[1,5]{1,0:T(1,128)S(1)}, u32[]{:S(2)}, u32[]{:S(2)}) collective-permute-start(s32[1,5]{1,0:T(1,128)S(1)} %add.13), channel_id=1, source_target_pairs={{0,2},{1,3},{2,0},{3,1},{4,6},{5,7},{6,4},{7,5},{8,10},{9,11},{10,... | collective-permute-start | bytes 68 | tf_op jit(solution)/shard_map/ppermute | solution.py:224
  14.7 1.5 %shard_map.82 = (f32[4096,128]{1,0:T(8,128)S(1)}, f32[512,128]{1,0:T(8,128)S(1)}) custom-call(f32[4,4,128,256]{3,2,1,0:T(8,128)S(1)} %get-tuple-element.38.probs, f32[4,4,128,256]{3,2,1,0:T(8,128)S(1)} %get-tuple-element.44.own_prob_grad, f32[4,4,1,256]{3,2,1,0:T(1,128)S(1)} %get-tuple-element.45.delta, ...), custom_call_target="tpu_custom_call" | custom-call | tf_op jit(solution)/shard_map/pallas_call | solution.py:308
  16.2 0.0 collective-permute-done.4
  16.2 1.1 %shard_map.83 = (bf16[4096,128]{1,0:T(8,128)(2,1)}, f32[1,128]{1,0:T(1,128)S(1)}) custom-call(s32[1,5]{1,0:T(1,128)S(1)} %add.14.count, f32[4096,128]{1,0:T(8,128)S(1)} %get-tuple-element.49.query_in), custom_call_target="tpu_custom_call" | custom-call | tf_op jit(solution)/shard_map/pallas_call | solution.py:314
  17.4 0.0 collective-permute-done.5
  17.4 0.7 %multiply_convert_fusion = bf16[512,128]{1,0:T(8,128)(2,1)} fusion(f32[512,128]{1,0:T(8,128)S(1)} %get-tuple-element.51, bf16[512,128]{1,0:T(8,128)(2,1)S(1)} %collective-permute-done.5, f32[128]{0:T(128)S(1)} %bitcast.15), kind=kLoop, calls=%fused_computation | loop fusion | flops 262144 | bytes 524800 | tf_op jit(solution)/shard_map/convert_element_type | solution.py:321
  (11 shorter events, 0.1 us)
Async XLA Ops:
  0.6 7.1 %copy-start.2 = (bf16[1,128,4,128]{3,2,1,0:T(4,128)(2,1)S(1)}, bf16[1,128,4,128]{3,2,1,0:T(4,128)(2,1)}, u32[]{:S(2)}) copy-start(bf16[1,128,4,128]{3,2,1,0:T(4,128)(2,1)} %param.7) | copy-start | bytes 393220
  0.6 4.4 %copy-start.5 = (s32[1,5]{1,0:T(1,128)S(1)}, s32[1,5]{1,0:T(1,128)}, u32[]{:S(2)}) copy-start(s32[1,5]{1,0:T(1,128)} %bounds.1) | copy-start | bytes 64
  0.7 7.1 %copy-start.3 = (bf16[1,128,4,128]{3,2,1,0:T(4,128)(2,1)S(1)}, bf16[1,128,4,128]{3,2,1,0:T(4,128)(2,1)}, u32[]{:S(2)}) copy-start(bf16[1,128,4,128]{3,2,1,0:T(4,128)(2,1)} %param.8) | copy-start | bytes 393220
  0.7 4.3 %copy-start.4 = (s32[32]{0:T(128)S(1)}, s32[32]{0:T(128)}, u32[]{:S(2)}) copy-start(s32[32]{0:T(128)} %param.11) | copy-start | bytes 388
  0.7 7.1 %copy-start.1 = (bf16[1,128,32,128]{3,2,1,0:T(8,128)(2,1)S(1)}, bf16[1,128,32,128]{3,2,1,0:T(8,128)(2,1)}, u32[]{:S(2)}) copy-start(bf16[1,128,32,128]{3,2,1,0:T(8,128)(2,1)} %param.9) | copy-start | bytes 3145732
  0.7 7.1 %copy-start = (bf16[1,128,32,128]{3,2,1,0:T(8,128)(2,1)S(1)}, bf16[1,128,32,128]{3,2,1,0:T(8,128)(2,1)}, u32[]{:S(2)}) copy-start(bf16[1,128,32,128]{3,2,1,0:T(8,128)(2,1)} %param.6) | copy-start | bytes 3145732
  0.7 7.9 %collective-permute-start.2 = (bf16[1,128,4,128]{3,2,1,0:T(4,128)(2,1)}, bf16[1,128,4,128]{3,2,1,0:T(4,128)(2,1)S(1)}, u32[]{:S(2)}, u32[]{:S(2)}) collective-permute-start(bf16[1,128,4,128]{3,2,1,0:T(4,128)(2,1)} %param.7), channel_id=1, source_target_pairs={{0,8},{1,9},{2,10},{3,11},{4,12},{5,13},{6,14},{7,15},{8,16},{9,17... | collective-permute-start | bytes 393224 | tf_op jit(solution)/shard_map/ppermute | solution.py:245
  2.8 2.6 %collective-permute-start = (s32[1,5]{1,0:T(1,128)}, s32[1,5]{1,0:T(1,128)S(1)}, u32[]{:S(2)}, u32[]{:S(2)}) collective-permute-start(s32[1,5]{1,0:T(1,128)} %bounds.1), channel_id=1, source_target_pairs={{0,1},{1,0},{2,3},{3,2},{4,5},{5,4},{6,7},{7,6},{8,9},{9,8},{10,11... | collective-permute-start | bytes 68 | tf_op jit(solution)/shard_map/ppermute | solution.py:224
  3.7 6.7 %collective-permute-start.3 = (bf16[1,128,4,128]{3,2,1,0:T(4,128)(2,1)}, bf16[1,128,4,128]{3,2,1,0:T(4,128)(2,1)S(1)}, u32[]{:S(2)}, u32[]{:S(2)}) collective-permute-start(bf16[1,128,4,128]{3,2,1,0:T(4,128)(2,1)} %param.8), channel_id=1, source_target_pairs={{0,8},{1,9},{2,10},{3,11},{4,12},{5,13},{6,14},{7,15},{8,16},{9,17... | collective-permute-start | bytes 393224 | tf_op jit(solution)/shard_map/ppermute | solution.py:246
  5.4 4.3 %collective-permute-start.1 = (s32[1,5]{1,0:T(1,128)S(1)}, s32[1,5]{1,0:T(1,128)S(1)}, u32[]{:S(2)}, u32[]{:S(2)}) collective-permute-start(s32[1,5]{1,0:T(1,128)S(1)} %add.12), channel_id=1, source_target_pairs={{0,4},{1,5},{2,6},{3,7},{4,0},{5,1},{6,2},{7,3},{8,12},{9,13},{10,... | collective-permute-start | bytes 68 | tf_op jit(solution)/shard_map/ppermute | solution.py:224
  11.2 6.2 %collective-permute-start.5 = (bf16[512,128]{1,0:T(8,128)(2,1)S(1)}, bf16[512,128]{1,0:T(8,128)(2,1)S(1)}, u32[]{:S(2)}, u32[]{:S(2)}) collective-permute-start(bf16[512,128]{1,0:T(8,128)(2,1)S(1)} %get-tuple-element.52), channel_id=1, source_target_pairs={{8,0},{9,1},{10,2},{11,3},{12,4},{13,5},{14,6},{15,7},{16,8},{17,9... | collective-permute-start | bytes 393224 | tf_op jit(solution)/shard_map/ppermute | solution.py:301
  13.4 2.8 %collective-permute-start.4 = (s32[1,5]{1,0:T(1,128)S(1)}, s32[1,5]{1,0:T(1,128)S(1)}, u32[]{:S(2)}, u32[]{:S(2)}) collective-permute-start(s32[1,5]{1,0:T(1,128)S(1)} %add.13), channel_id=1, source_target_pairs={{0,2},{1,3},{2,0},{3,1},{4,6},{5,7},{6,4},{7,5},{8,10},{9,11},{10,... | collective-permute-start | bytes 68 | tf_op jit(solution)/shard_map/ppermute | solution.py:224

commit v10 on v9

--- a/solution.py
+++ b/solution.py
@@ -259,7 +259,7 @@
     )(offsets, query_head_group.reshape(1, heads), places)
     if paired:
         count, sort = lax.optimization_barrier((add_partner(offsets, "dp", 1), sort))
-        moved = partner(count, "dp", hops[-1])
+        moved = partner(count, "dp", hops[-1] | 1)
     else:
         moved = lax.psum(offsets, "dp")
     sorted_query, sorted_grad, own_key, own_value = call(

time: 18.2 us -> 18.2 us (level)
  starting transfers between devices: 10.1 us -> 10.3 us
where the time goes in v10:
time: 18.2 us; the launch traced here: 18.1 us
  starting transfers between devices  10.3 us (57%)
  Pallas kernels  5.64 us (31%)
  between operations  0.79 us (4%)
  other arithmetic  0.71 us (4%)
  waiting for transfers between devices  0.61 us (3%)
    ppermute x3, starting transfers between devices, partner(): lax.ppermute(value, axis, [(i, i ^ hop) for i in range(lax.axis_size(axis...  4.8 us
    ppermute x1, starting transfers between devices, per_device(): back = lax.ppermute(back, axes, behind)  2.18 us
    ppermute x1, starting transfers between devices, per_device(): lax.ppermute(key_rows, axes, keys_ahead).reshape(tok * groups, depth)  2.1 us
    pallas_call x1, Pallas kernels, per_device(): call(functools.partial(query_kernel, sizes), [VMEM] * 8, [((tok * heads,...  1.54 us
    ppermute x1, starting transfers between devices, per_device(): lax.ppermute(value_matrix, axes, ahead).reshape(tok * groups, depth)  1.21 us
    pallas_call x1, Pallas kernels, per_device(): call(functools.partial(query_out_kernel, tokens), [VMEM] * 2, [((tok * he...  1.12 us
    pallas_call x1, Pallas kernels, per_device(): call(functools.partial(probs_kernel, sizes), [VMEM] * 6, [(tall, F32), (t...  1.1 us
    pallas_call x1, Pallas kernels, per_device(): call(functools.partial(arrange_kernel, sizes), [VMEM] * 5, [(sorted_shape...  0.75 us
  transfers between devices with their start and end apart: 6, of which 1 were waited for; matrix products, arithmetic and copies ran while one was open for 0% of the time, Pallas kernels for 27%

profile of v10, /device:TPU:1, one launch (start us, length us, event | category | flops | bytes accessed | tf_op | source)
XLA Modules:
  0.0 18.1 jit_solution(13899384809876824818)
XLA Ops:
  0.6 0.0 copy-start.2
  0.6 0.0 copy-start.5
  0.7 0.0 copy-start.3
  0.7 0.0 copy-start.4
  0.7 2.1 %collective-permute-start.2 = (bf16[1,128,4,128]{3,2,1,0:T(4,128)(2,1)}, bf16[1,128,4,128]{3,2,1,0:T(4,128)(2,1)S(1)}, u32[]{:S(2)}, u32[]{:S(2)}) collective-permute-start(bf16[1,128,4,128]{3,2,1,0:T(4,128)(2,1)} %param.7), channel_id=1, source_target_pairs={{0,8},{1,9},{2,10},{3,11},{4,12},{5,13},{6,14},{7,15},{8,16},{9,17... | collective-permute-start | bytes 393224 | tf_op jit(solution)/shard_map/ppermute | solution.py:245
  2.8 1.0 %collective-permute-start = (s32[1,5]{1,0:T(1,128)}, s32[1,5]{1,0:T(1,128)S(1)}, u32[]{:S(2)}, u32[]{:S(2)}) collective-permute-start(s32[1,5]{1,0:T(1,128)} %bounds.1), channel_id=1, source_target_pairs={{0,1},{1,0},{2,3},{3,2},{4,5},{5,4},{6,7},{7,6},{8,9},{9,8},{10,11... | collective-permute-start | bytes 68 | tf_op jit(solution)/shard_map/ppermute | solution.py:224
  3.7 1.2 %collective-permute-start.3 = (bf16[1,128,4,128]{3,2,1,0:T(4,128)(2,1)}, bf16[1,128,4,128]{3,2,1,0:T(4,128)(2,1)S(1)}, u32[]{:S(2)}, u32[]{:S(2)}) collective-permute-start(bf16[1,128,4,128]{3,2,1,0:T(4,128)(2,1)} %param.8), channel_id=1, source_target_pairs={{0,8},{1,9},{2,10},{3,11},{4,12},{5,13},{6,14},{7,15},{8,16},{9,17... | collective-permute-start | bytes 393224 | tf_op jit(solution)/shard_map/ppermute | solution.py:246
  5.0 0.4 %shard_map.78 = (bf16[256,256]{1,0:T(8,128)(2,1)S(1)}, bf16[256,256]{1,0:T(8,128)(2,1)S(1)}, f32[128,1024]{1,0:T(8,128)S(1)}) custom-call(s32[1,5]{1,0:T(1,128)S(1)} %copy-done.5, s32[1,32]{1,0:T(1,128)S(1)} %bitcast.16, s32[128,1024]{1,0:T(8,128)S(1)} %shard_map.77.places), custom_call_target="tpu_custom_call" | custom-call | tf_op jit(solution)/shard_map/pallas_call | solution.py:255
  5.4 0.0 collective-permute-done
  5.4 2.5 %collective-permute-start.1 = (s32[1,5]{1,0:T(1,128)S(1)}, s32[1,5]{1,0:T(1,128)S(1)}, u32[]{:S(2)}, u32[]{:S(2)}) collective-permute-start(s32[1,5]{1,0:T(1,128)S(1)} %add.12), channel_id=1, source_target_pairs={{0,5},{1,4},{2,7},{3,6},{4,1},{5,0},{6,3},{7,2},{8,13},{9,12},{10,... | collective-permute-start | bytes 68 | tf_op jit(solution)/shard_map/ppermute | solution.py:224
  8.0 0.0 copy-done
  8.0 0.7 %shard_map.79 = (bf16[4,1024,128]{2,1,0:T(8,128)(2,1)S(1)}, bf16[4,1024,128]{2,1,0:T(8,128)(2,1)S(1)}, bf16[4,128,128]{2,1,0:T(8,128)(2,1)S(1)}, bf16[4,128,128]{2,1,0:T(8,128)(2,1)S(1)}) custom-call(bf16[256,256]{1,0:T(8,128)(2,1)S(1)} %get-tuple-element.31.sort, bf16[4096,128]{1,0:T(8,128)(2,1)S(1)} %bitcast.10, bf16[4096,128]{1,0:T(8,128)(2,1)S(1)} %bitcast.11, ...), custom_call_target="tpu_custom_call" | custom-call | tf_op jit(solution)/shard_map/pallas_call | solution.py:265
  8.7 0.0 collective-permute-done.2
  8.7 1.1 %shard_map.80 = (f32[4,4,128,256]{3,2,1,0:T(8,128)S(1)}, f32[4,4,128,256]{3,2,1,0:T(8,128)S(1)}, f32[4,4,1,256]{3,2,1,0:T(1,128)S(1)}, bf16[4,128,128]{2,1,0:T(8,128)(2,1)S(1)}) custom-call(f32[128,1024]{1,0:T(8,128)S(1)} %get-tuple-element.30.bias, bf16[4,1024,128]{2,1,0:T(8,128)(2,1)S(1)} %get-tuple-element.32.query, ...), custom_call_target="tpu_custom_call" | custom-call | flops 500000000 | tf_op jit(solution)/shard_map/pallas_call | solution.py:280
  9.8 0.0 collective-permute-done.1
  9.8 0.6 %collective-permute-done.3 = bf16[1,128,4,128]{3,2,1,0:T(4,128)(2,1)S(1)} collective-permute-done((bf16[1,128,4,128]{3,2,1,0:T(4,128)(2,1)}, bf16[1,128,4,128]{3,2,1,0:T(4,128)(2,1)S(1)}, u32[]{:S(2)}, u32[]{:S(2)}) %collective-permute-start.3) | collective-permute-done | bytes 131104 | tf_op jit(solution)/shard_map/ppermute | solution.py:246
  10.4 0.7 %shard_map.81 = (bf16[4,4,128,256]{3,2,1,0:T(8,128)(2,1)S(1)}, f32[4,4,1,256]{3,2,1,0:T(1,128)S(1)}, bf16[512,128]{1,0:T(8,128)(2,1)S(1)}) custom-call(f32[4,4,128,256]{3,2,1,0:T(8,128)S(1)} %get-tuple-element.38.probs, f32[4,4,1,256]{3,2,1,0:T(1,128)S(1)} %get-tuple-element.39.own_delta, bf16[4,1024,128]{2,1,0:T(8,128)(2,1)S(1)} %get-tuple-element.32.query, ...), custom_call_target="tpu_custom_call" | custom-call | flops 2000000000 | tf_op jit(solution)/shard_map/pallas_call | solution.py:292
  11.2 2.2 %collective-permute-start.5 = (bf16[512,128]{1,0:T(8,128)(2,1)S(1)}, bf16[512,128]{1,0:T(8,128)(2,1)S(1)}, u32[]{:S(2)}, u32[]{:S(2)}) collective-permute-start(bf16[512,128]{1,0:T(8,128)(2,1)S(1)} %get-tuple-element.52), channel_id=1, source_target_pairs={{8,0},{9,1},{10,2},{11,3},{12,4},{13,5},{14,6},{15,7},{16,8},{17,9... | collective-permute-start | bytes 393224 | tf_op jit(solution)/shard_map/ppermute | solution.py:301
  13.4 1.3 %collective-permute-start.4 = (s32[1,5]{1,0:T(1,128)S(1)}, s32[1,5]{1,0:T(1,128)S(1)}, u32[]{:S(2)}, u32[]{:S(2)}) collective-permute-start(s32[1,5]{1,0:T(1,128)S(1)} %add.13), channel_id=1, source_target_pairs={{0,2},{1,3},{2,0},{3,1},{4,6},{5,7},{6,4},{7,5},{8,10},{9,11},{10,... | collective-permute-start | bytes 68 | tf_op jit(solution)/shard_map/ppermute | solution.py:224
  14.7 1.5 %shard_map.82 = (f32[4096,128]{1,0:T(8,128)S(1)}, f32[512,128]{1,0:T(8,128)S(1)}) custom-call(f32[4,4,128,256]{3,2,1,0:T(8,128)S(1)} %get-tuple-element.38.probs, f32[4,4,128,256]{3,2,1,0:T(8,128)S(1)} %get-tuple-element.44.own_prob_grad, f32[4,4,1,256]{3,2,1,0:T(1,128)S(1)} %get-tuple-element.45.delta, ...), custom_call_target="tpu_custom_call" | custom-call | tf_op jit(solution)/shard_map/pallas_call | solution.py:308
  16.2 0.0 collective-permute-done.4
  16.2 1.1 %shard_map.83 = (bf16[4096,128]{1,0:T(8,128)(2,1)}, f32[1,128]{1,0:T(1,128)S(1)}) custom-call(s32[1,5]{1,0:T(1,128)S(1)} %add.14.count, f32[4096,128]{1,0:T(8,128)S(1)} %get-tuple-element.49.query_in), custom_call_target="tpu_custom_call" | custom-call | tf_op jit(solution)/shard_map/pallas_call | solution.py:314
  17.4 0.0 collective-permute-done.5
  17.4 0.7 %multiply_convert_fusion = bf16[512,128]{1,0:T(8,128)(2,1)} fusion(f32[512,128]{1,0:T(8,128)S(1)} %get-tuple-element.51, bf16[512,128]{1,0:T(8,128)(2,1)S(1)} %collective-permute-done.5, f32[128]{0:T(128)S(1)} %bitcast.15), kind=kLoop, calls=%fused_computation | loop fusion | flops 262144 | bytes 524800 | tf_op jit(solution)/shard_map/convert_element_type | solution.py:321
  (11 shorter events, 0.1 us)
Async XLA Ops:
  0.6 7.3 %copy-start.2 = (bf16[1,128,4,128]{3,2,1,0:T(4,128)(2,1)S(1)}, bf16[1,128,4,128]{3,2,1,0:T(4,128)(2,1)}, u32[]{:S(2)}) copy-start(bf16[1,128,4,128]{3,2,1,0:T(4,128)(2,1)} %param.7) | copy-start | bytes 393220
  0.6 4.4 %copy-start.5 = (s32[1,5]{1,0:T(1,128)S(1)}, s32[1,5]{1,0:T(1,128)}, u32[]{:S(2)}) copy-start(s32[1,5]{1,0:T(1,128)} %bounds.1) | copy-start | bytes 64
  0.7 7.3 %copy-start.3 = (bf16[1,128,4,128]{3,2,1,0:T(4,128)(2,1)S(1)}, bf16[1,128,4,128]{3,2,1,0:T(4,128)(2,1)}, u32[]{:S(2)}) copy-start(bf16[1,128,4,128]{3,2,1,0:T(4,128)(2,1)} %param.8) | copy-start | bytes 393220
  0.7 4.3 %copy-start.4 = (s32[32]{0:T(128)S(1)}, s32[32]{0:T(128)}, u32[]{:S(2)}) copy-start(s32[32]{0:T(128)} %param.11) | copy-start | bytes 388
  0.7 7.3 %copy-start.1 = (bf16[1,128,32,128]{3,2,1,0:T(8,128)(2,1)S(1)}, bf16[1,128,32,128]{3,2,1,0:T(8,128)(2,1)}, u32[]{:S(2)}) copy-start(bf16[1,128,32,128]{3,2,1,0:T(8,128)(2,1)} %param.9) | copy-start | bytes 3145732
  0.7 7.3 %copy-start = (bf16[1,128,32,128]{3,2,1,0:T(8,128)(2,1)S(1)}, bf16[1,128,32,128]{3,2,1,0:T(8,128)(2,1)}, u32[]{:S(2)}) copy-start(bf16[1,128,32,128]{3,2,1,0:T(8,128)(2,1)} %param.6) | copy-start | bytes 3145732
  0.7 8.0 %collective-permute-start.2 = (bf16[1,128,4,128]{3,2,1,0:T(4,128)(2,1)}, bf16[1,128,4,128]{3,2,1,0:T(4,128)(2,1)S(1)}, u32[]{:S(2)}, u32[]{:S(2)}) collective-permute-start(bf16[1,128,4,128]{3,2,1,0:T(4,128)(2,1)} %param.7), channel_id=1, source_target_pairs={{0,8},{1,9},{2,10},{3,11},{4,12},{5,13},{6,14},{7,15},{8,16},{9,17... | collective-permute-start | bytes 393224 | tf_op jit(solution)/shard_map/ppermute | solution.py:245
  2.8 2.6 %collective-permute-start = (s32[1,5]{1,0:T(1,128)}, s32[1,5]{1,0:T(1,128)S(1)}, u32[]{:S(2)}, u32[]{:S(2)}) collective-permute-start(s32[1,5]{1,0:T(1,128)} %bounds.1), channel_id=1, source_target_pairs={{0,1},{1,0},{2,3},{3,2},{4,5},{5,4},{6,7},{7,6},{8,9},{9,8},{10,11... | collective-permute-start | bytes 68 | tf_op jit(solution)/shard_map/ppermute | solution.py:224
  3.7 6.7 %collective-permute-start.3 = (bf16[1,128,4,128]{3,2,1,0:T(4,128)(2,1)}, bf16[1,128,4,128]{3,2,1,0:T(4,128)(2,1)S(1)}, u32[]{:S(2)}, u32[]{:S(2)}) collective-permute-start(bf16[1,128,4,128]{3,2,1,0:T(4,128)(2,1)} %param.8), channel_id=1, source_target_pairs={{0,8},{1,9},{2,10},{3,11},{4,12},{5,13},{6,14},{7,15},{8,16},{9,17... | collective-permute-start | bytes 393224 | tf_op jit(solution)/shard_map/ppermute | solution.py:246
  5.4 4.4 %collective-permute-start.1 = (s32[1,5]{1,0:T(1,128)S(1)}, s32[1,5]{1,0:T(1,128)S(1)}, u32[]{:S(2)}, u32[]{:S(2)}) collective-permute-start(s32[1,5]{1,0:T(1,128)S(1)} %add.12), channel_id=1, source_target_pairs={{0,5},{1,4},{2,7},{3,6},{4,1},{5,0},{6,3},{7,2},{8,13},{9,12},{10,... | collective-permute-start | bytes 68 | tf_op jit(solution)/shard_map/ppermute | solution.py:224
  11.2 6.2 %collective-permute-start.5 = (bf16[512,128]{1,0:T(8,128)(2,1)S(1)}, bf16[512,128]{1,0:T(8,128)(2,1)S(1)}, u32[]{:S(2)}, u32[]{:S(2)}) collective-permute-start(bf16[512,128]{1,0:T(8,128)(2,1)S(1)} %get-tuple-element.52), channel_id=1, source_target_pairs={{8,0},{9,1},{10,2},{11,3},{12,4},{13,5},{14,6},{15,7},{16,8},{17,9... | collective-permute-start | bytes 393224 | tf_op jit(solution)/shard_map/ppermute | solution.py:301
  13.4 2.8 %collective-permute-start.4 = (s32[1,5]{1,0:T(1,128)S(1)}, s32[1,5]{1,0:T(1,128)S(1)}, u32[]{:S(2)}, u32[]{:S(2)}) collective-permute-start(s32[1,5]{1,0:T(1,128)S(1)} %add.13), channel_id=1, source_target_pairs={{0,2},{1,3},{2,0},{3,1},{4,6},{5,7},{6,4},{7,5},{8,10},{9,11},{10,... | collective-permute-start | bytes 68 | tf_op jit(solution)/shard_map/ppermute | solution.py:224

commit v11 on v9

--- a/solution.py
+++ b/solution.py
@@ -95,7 +95,7 @@
     return stack((left, 0, lo), (mid, 0, here), (right, here, right.shape[0]))
 
 
-def probs_kernel(sizes, bias, query, grad, own_key, own_value, back_in, probs, own_prob_grad, own_delta, back_key, flat):
+def probs_kernel(sizes, bias, query, grad, own_key, own_value, back_in, probs, own_probs, own_prob_grad, own_delta, back_key, flat):
     tok, heads, groups, per = sizes
     split_heads(back_in, flat, back_key, tok, groups)
     rate = math.log2(math.e) / math.sqrt(query.shape[2])
@@ -111,12 +111,11 @@
             terms = jnp.exp2((scores - top) * rate)
             scale = 1.0 / jnp.maximum(jnp.sum(terms, axis=0, keepdims=True), 1.0)
             prob = terms * scale
-            probs[g, t] = prob
+            own_probs[g, t, :hi] = stack((prob, 0, lo), (jnp.where(own, prob[lo:hi], 0.0), 0, here))
+            probs[g, t, lo:] = stack((jnp.where(own, 0.0, prob[lo:hi]), 0, here), (prob, hi, tok))
             prob_grad = dot(own_value[g, :hi], grad[g, part, :], NT)
             own_prob_grad[g, t, :hi] = prob_grad
-            both = prob[:hi] * prob_grad
-            both = stack((both, 0, lo), (jnp.where(own, both[lo:], 0.0), 0, here))
-            own_delta[g, t] = jnp.sum(both, axis=0, keepdims=True)
+            own_delta[g, t] = jnp.sum(own_probs[g, t, :hi] * prob_grad, axis=0, keepdims=True)
 
 
 def add_rows(sums, first, piece, here):
@@ -134,7 +133,6 @@
         for t in range(tok // here):
             lo = t * here
             prob = probs[g, t, lo:]
-            prob = stack((jnp.where(own, 0.0, prob[:here]), 0, here), (prob, here, tok - lo))
             prob_grad = dot(back_value[g, lo:], grad[g, t * BLOCK : (t + 1) * BLOCK, :], NT)
             delta = own_delta[g, t] + jnp.sum(prob * prob_grad, axis=0, keepdims=True)
             delta_out[g, t] = delta
@@ -159,7 +157,7 @@
         for t in range(tok // here):
             lo, hi = t * here, (t + 1) * here
             out = probs[g, t, :hi] * (own_prob_grad[g, t, :hi] - delta[g, t])
-            own_score[g, t, :hi] = stack((out, 0, lo), (jnp.where(own, out[lo:], 0.0), 0, here)).astype(BF16)
+            own_score[g, t, :hi] = out.astype(BF16)
     for g in range(groups):
         for t in range(tok // here):
             lo, hi = t * here, (t + 1) * here
@@ -277,10 +275,10 @@
 
     tall = (groups, tok // here, tok, BLOCK)
     line = (groups, tok // here, 1, BLOCK)
-    probs, own_prob_grad, own_delta, back_key = call(
+    probs, own_probs, own_prob_grad, own_delta, back_key = call(
         functools.partial(probs_kernel, sizes),
         [VMEM] * 6,
-        [(tall, F32), (tall, F32), (line, F32), (split, BF16)],
+        [(tall, F32), (tall, F32), (tall, F32), (line, F32), (split, BF16)],
         [pltpu.VMEM(packed, F32)],
         500_000_000,
     )(bias, sorted_query, sorted_grad, own_key, own_value, back_key)
@@ -310,7 +308,7 @@
         [VMEM] * 8,
         [((tok * heads, depth), F32), (packed, F32)],
         [pltpu.VMEM(sorted_shape, F32), pltpu.VMEM(tall, BF16)],
-    )(probs, own_prob_grad, delta, back_score, sorted_query, own_key, back_key, unsort)
+    )(own_probs, own_prob_grad, delta, back_score, sorted_query, own_key, back_key, unsort)
     query_grad, factor = call(
         functools.partial(query_out_kernel, tokens),
         [VMEM] * 2,

time: 18.2 us -> 18.2 us (level)
  transfers between devices with their start and end apart: 6 -> 6, of which waited for: 1 -> 1; matrix products, arithmetic and copies ran while one was open for 0% -> 0% of each run, Pallas kernels for 27% -> 28%
where the time goes in v11:
time: 18.2 us; the launch traced here: 18.1 us
  starting transfers between devices  10.1 us (55%)
  Pallas kernels  5.73 us (31%)
  between operations  0.79 us (4%)
  other arithmetic  0.71 us (4%)
  waiting for transfers between devices  0.68 us (4%)
    ppermute x3, starting transfers between devices, partner(): lax.ppermute(value, axis, [(i, i ^ hop) for i in range(lax.axis_size(axis...  4.63 us
    ppermute x1, starting transfers between devices, per_device(): back = lax.ppermute(back, axes, behind)  2.18 us
    ppermute x1, starting transfers between devices, per_device(): lax.ppermute(key_rows, axes, keys_ahead).reshape(tok * groups, depth)  2.1 us
    pallas_call x1, Pallas kernels, per_device(): call(functools.partial(query_kernel, sizes), [VMEM] * 8, [((tok * heads,...  1.54 us
    ppermute x1, starting transfers between devices, per_device(): lax.ppermute(value_matrix, axes, ahead).reshape(tok * groups, depth)  1.21 us
    pallas_call x1, Pallas kernels, per_device(): call(functools.partial(probs_kernel, sizes), [VMEM] * 6, [(tall, F32), (t...  1.2 us
    pallas_call x1, Pallas kernels, per_device(): call(functools.partial(query_out_kernel, tokens), [VMEM] * 2, [((tok * he...  1.12 us
    pallas_call x1, Pallas kernels, per_device(): call(functools.partial(arrange_kernel, sizes), [VMEM] * 5, [(sorted_shape...  0.75 us
  transfers between devices with their start and end apart: 6, of which 1 were waited for; matrix products, arithmetic and copies ran while one was open for 0% of the time, Pallas kernels for 28%

profile of v11, /device:TPU:1, one launch (start us, length us, event | category | flops | bytes accessed | tf_op | source)
XLA Modules:
  0.0 18.1 jit_solution(9681480703997828714)
XLA Ops:
  0.6 0.0 copy-start.2
  0.6 0.0 copy-start.5
  0.7 0.0 copy-start.3
  0.7 0.0 copy-start.4
  0.7 2.1 %collective-permute-start.2 = (bf16[1,128,4,128]{3,2,1,0:T(4,128)(2,1)}, bf16[1,128,4,128]{3,2,1,0:T(4,128)(2,1)S(1)}, u32[]{:S(2)}, u32[]{:S(2)}) collective-permute-start(bf16[1,128,4,128]{3,2,1,0:T(4,128)(2,1)} %param.7), channel_id=1, source_target_pairs={{0,8},{1,9},{2,10},{3,11},{4,12},{5,13},{6,14},{7,15},{8,16},{9,17... | collective-permute-start | bytes 393224 | tf_op jit(solution)/shard_map/ppermute | solution.py:243
  2.8 1.0 %collective-permute-start = (s32[1,5]{1,0:T(1,128)}, s32[1,5]{1,0:T(1,128)S(1)}, u32[]{:S(2)}, u32[]{:S(2)}) collective-permute-start(s32[1,5]{1,0:T(1,128)} %bounds.1), channel_id=1, source_target_pairs={{0,1},{1,0},{2,3},{3,2},{4,5},{5,4},{6,7},{7,6},{8,9},{9,8},{10,11... | collective-permute-start | bytes 68 | tf_op jit(solution)/shard_map/ppermute | solution.py:222
  3.7 1.2 %collective-permute-start.3 = (bf16[1,128,4,128]{3,2,1,0:T(4,128)(2,1)}, bf16[1,128,4,128]{3,2,1,0:T(4,128)(2,1)S(1)}, u32[]{:S(2)}, u32[]{:S(2)}) collective-permute-start(bf16[1,128,4,128]{3,2,1,0:T(4,128)(2,1)} %param.8), channel_id=1, source_target_pairs={{0,8},{1,9},{2,10},{3,11},{4,12},{5,13},{6,14},{7,15},{8,16},{9,17... | collective-permute-start | bytes 393224 | tf_op jit(solution)/shard_map/ppermute | solution.py:244
  5.0 0.4 %shard_map.78 = (bf16[256,256]{1,0:T(8,128)(2,1)S(1)}, bf16[256,256]{1,0:T(8,128)(2,1)S(1)}, f32[128,1024]{1,0:T(8,128)S(1)}) custom-call(s32[1,5]{1,0:T(1,128)S(1)} %copy-done.5, s32[1,32]{1,0:T(1,128)S(1)} %bitcast.16, s32[128,1024]{1,0:T(8,128)S(1)} %shard_map.77.places), custom_call_target="tpu_custom_call" | custom-call | tf_op jit(solution)/shard_map/pallas_call | solution.py:253
  5.4 0.0 collective-permute-done
  5.4 2.4 %collective-permute-start.1 = (s32[1,5]{1,0:T(1,128)S(1)}, s32[1,5]{1,0:T(1,128)S(1)}, u32[]{:S(2)}, u32[]{:S(2)}) collective-permute-start(s32[1,5]{1,0:T(1,128)S(1)} %add.12), channel_id=1, source_target_pairs={{0,4},{1,5},{2,6},{3,7},{4,0},{5,1},{6,2},{7,3},{8,12},{9,13},{10,... | collective-permute-start | bytes 68 | tf_op jit(solution)/shard_map/ppermute | solution.py:222
  7.8 0.0 copy-done.3
  7.8 0.7 %shard_map.79 = (bf16[4,1024,128]{2,1,0:T(8,128)(2,1)S(1)}, bf16[4,1024,128]{2,1,0:T(8,128)(2,1)S(1)}, bf16[4,128,128]{2,1,0:T(8,128)(2,1)S(1)}, bf16[4,128,128]{2,1,0:T(8,128)(2,1)S(1)}) custom-call(bf16[256,256]{1,0:T(8,128)(2,1)S(1)} %get-tuple-element.32.sort, bf16[4096,128]{1,0:T(8,128)(2,1)S(1)} %bitcast.10, bf16[4096,128]{1,0:T(8,128)(2,1)S(1)} %bitcast.11, ...), custom_call_target="tpu_custom_call" | custom-call | tf_op jit(solution)/shard_map/pallas_call | solution.py:263
  8.5 0.0 collective-permute-done.2
  8.6 1.2 %shard_map.80 = (f32[4,4,128,256]{3,2,1,0:T(8,128)S(1)}, f32[4,4,128,256]{3,2,1,0:T(8,128)S(1)}, f32[4,4,128,256]{3,2,1,0:T(8,128)S(1)}, f32[4,4,1,256]{3,2,1,0:T(1,128)S(1)}, bf16[4,128,128]{2,1,0:T(8,128)(2,1)S(1)}) custom-call(f32[128,1024]{1,0:T(8,128)S(1)} %get-tuple-element.31.bias, bf16[4,1024,128]{2,1,0:T(8,128)(2,1)S(1)} %get-tuple-element.33.query, ...), custom_call_target="tpu_custom_call" | custom-call | flops 500000000 | tf_op jit(solution)/shard_map/pallas_call | solution.py:278
  9.8 0.0 collective-permute-done.1
  9.8 0.7 %collective-permute-done.3 = bf16[1,128,4,128]{3,2,1,0:T(4,128)(2,1)S(1)} collective-permute-done((bf16[1,128,4,128]{3,2,1,0:T(4,128)(2,1)}, bf16[1,128,4,128]{3,2,1,0:T(4,128)(2,1)S(1)}, u32[]{:S(2)}, u32[]{:S(2)}) %collective-permute-start.3) | collective-permute-done | bytes 131104 | tf_op jit(solution)/shard_map/ppermute | solution.py:244
  10.4 0.7 %shard_map.81 = (bf16[4,4,128,256]{3,2,1,0:T(8,128)(2,1)S(1)}, f32[4,4,1,256]{3,2,1,0:T(1,128)S(1)}, bf16[512,128]{1,0:T(8,128)(2,1)S(1)}) custom-call(f32[4,4,128,256]{3,2,1,0:T(8,128)S(1)} %get-tuple-element.39.probs, f32[4,4,1,256]{3,2,1,0:T(1,128)S(1)} %get-tuple-element.40.own_delta, bf16[4,1024,128]{2,1,0:T(8,128)(2,1)S(1)} %get-tuple-element.33.query, ...), custom_call_target="tpu_custom_call" | custom-call | flops 2000000000 | tf_op jit(solution)/shard_map/pallas_call | solution.py:290
  11.2 2.2 %collective-permute-start.5 = (bf16[512,128]{1,0:T(8,128)(2,1)S(1)}, bf16[512,128]{1,0:T(8,128)(2,1)S(1)}, u32[]{:S(2)}, u32[]{:S(2)}) collective-permute-start(bf16[512,128]{1,0:T(8,128)(2,1)S(1)} %get-tuple-element.54), channel_id=1, source_target_pairs={{8,0},{9,1},{10,2},{11,3},{12,4},{13,5},{14,6},{15,7},{16,8},{17,9... | collective-permute-start | bytes 393224 | tf_op jit(solution)/shard_map/ppermute | solution.py:299
  13.4 1.3 %collective-permute-start.4 = (s32[1,5]{1,0:T(1,128)S(1)}, s32[1,5]{1,0:T(1,128)S(1)}, u32[]{:S(2)}, u32[]{:S(2)}) collective-permute-start(s32[1,5]{1,0:T(1,128)S(1)} %add.13), channel_id=1, source_target_pairs={{0,2},{1,3},{2,0},{3,1},{4,6},{5,7},{6,4},{7,5},{8,10},{9,11},{10,... | collective-permute-start | bytes 68 | tf_op jit(solution)/shard_map/ppermute | solution.py:222
  14.7 1.5 %shard_map.82 = (f32[4096,128]{1,0:T(8,128)S(1)}, f32[512,128]{1,0:T(8,128)S(1)}) custom-call(f32[4,4,128,256]{3,2,1,0:T(8,128)S(1)} %get-tuple-element.45.probs, f32[4,4,128,256]{3,2,1,0:T(8,128)S(1)} %get-tuple-element.46.own_prob_grad, f32[4,4,1,256]{3,2,1,0:T(1,128)S(1)} %get-tuple-element.47.delta, ...), custom_call_target="tpu_custom_call" | custom-call | tf_op jit(solution)/shard_map/pallas_call | solution.py:306
  16.2 0.0 collective-permute-done.4
  16.2 1.1 %shard_map.83 = (bf16[4096,128]{1,0:T(8,128)(2,1)}, f32[1,128]{1,0:T(1,128)S(1)}) custom-call(s32[1,5]{1,0:T(1,128)S(1)} %add.14.count, f32[4096,128]{1,0:T(8,128)S(1)} %get-tuple-element.51.query_in), custom_call_target="tpu_custom_call" | custom-call | tf_op jit(solution)/shard_map/pallas_call | solution.py:312
  17.4 0.0 collective-permute-done.5
  17.4 0.7 %multiply_convert_fusion = bf16[512,128]{1,0:T(8,128)(2,1)} fusion(f32[512,128]{1,0:T(8,128)S(1)} %get-tuple-element.53, bf16[512,128]{1,0:T(8,128)(2,1)S(1)} %collective-permute-done.5, f32[128]{0:T(128)S(1)} %bitcast.15), kind=kLoop, calls=%fused_computation | loop fusion | flops 262144 | bytes 524800 | tf_op jit(solution)/shard_map/convert_element_type | solution.py:319
  (11 shorter events, 0.1 us)
Async XLA Ops:
  0.6 7.1 %copy-start.2 = (bf16[1,128,4,128]{3,2,1,0:T(4,128)(2,1)S(1)}, bf16[1,128,4,128]{3,2,1,0:T(4,128)(2,1)}, u32[]{:S(2)}) copy-start(bf16[1,128,4,128]{3,2,1,0:T(4,128)(2,1)} %param.7) | copy-start | bytes 393220
  0.6 4.4 %copy-start.5 = (s32[1,5]{1,0:T(1,128)S(1)}, s32[1,5]{1,0:T(1,128)}, u32[]{:S(2)}) copy-start(s32[1,5]{1,0:T(1,128)} %bounds.1) | copy-start | bytes 64
  0.7 7.1 %copy-start.3 = (bf16[1,128,4,128]{3,2,1,0:T(4,128)(2,1)S(1)}, bf16[1,128,4,128]{3,2,1,0:T(4,128)(2,1)}, u32[]{:S(2)}) copy-start(bf16[1,128,4,128]{3,2,1,0:T(4,128)(2,1)} %param.8) | copy-start | bytes 393220
  0.7 4.3 %copy-start.4 = (s32[32]{0:T(128)S(1)}, s32[32]{0:T(128)}, u32[]{:S(2)}) copy-start(s32[32]{0:T(128)} %param.11) | copy-start | bytes 388
  0.7 7.1 %copy-start.1 = (bf16[1,128,32,128]{3,2,1,0:T(8,128)(2,1)S(1)}, bf16[1,128,32,128]{3,2,1,0:T(8,128)(2,1)}, u32[]{:S(2)}) copy-start(bf16[1,128,32,128]{3,2,1,0:T(8,128)(2,1)} %param.9) | copy-start | bytes 3145732
  0.7 7.1 %copy-start = (bf16[1,128,32,128]{3,2,1,0:T(8,128)(2,1)S(1)}, bf16[1,128,32,128]{3,2,1,0:T(8,128)(2,1)}, u32[]{:S(2)}) copy-start(bf16[1,128,32,128]{3,2,1,0:T(8,128)(2,1)} %param.6) | copy-start | bytes 3145732
  0.7 7.9 %collective-permute-start.2 = (bf16[1,128,4,128]{3,2,1,0:T(4,128)(2,1)}, bf16[1,128,4,128]{3,2,1,0:T(4,128)(2,1)S(1)}, u32[]{:S(2)}, u32[]{:S(2)}) collective-permute-start(bf16[1,128,4,128]{3,2,1,0:T(4,128)(2,1)} %param.7), channel_id=1, source_target_pairs={{0,8},{1,9},{2,10},{3,11},{4,12},{5,13},{6,14},{7,15},{8,16},{9,17... | collective-permute-start | bytes 393224 | tf_op jit(solution)/shard_map/ppermute | solution.py:243
  2.8 2.6 %collective-permute-start = (s32[1,5]{1,0:T(1,128)}, s32[1,5]{1,0:T(1,128)S(1)}, u32[]{:S(2)}, u32[]{:S(2)}) collective-permute-start(s32[1,5]{1,0:T(1,128)} %bounds.1), channel_id=1, source_target_pairs={{0,1},{1,0},{2,3},{3,2},{4,5},{5,4},{6,7},{7,6},{8,9},{9,8},{10,11... | collective-permute-start | bytes 68 | tf_op jit(solution)/shard_map/ppermute | solution.py:222
  3.7 6.7 %collective-permute-start.3 = (bf16[1,128,4,128]{3,2,1,0:T(4,128)(2,1)}, bf16[1,128,4,128]{3,2,1,0:T(4,128)(2,1)S(1)}, u32[]{:S(2)}, u32[]{:S(2)}) collective-permute-start(bf16[1,128,4,128]{3,2,1,0:T(4,128)(2,1)} %param.8), channel_id=1, source_target_pairs={{0,8},{1,9},{2,10},{3,11},{4,12},{5,13},{6,14},{7,15},{8,16},{9,17... | collective-permute-start | bytes 393224 | tf_op jit(solution)/shard_map/ppermute | solution.py:244
  5.4 4.4 %collective-permute-start.1 = (s32[1,5]{1,0:T(1,128)S(1)}, s32[1,5]{1,0:T(1,128)S(1)}, u32[]{:S(2)}, u32[]{:S(2)}) collective-permute-start(s32[1,5]{1,0:T(1,128)S(1)} %add.12), channel_id=1, source_target_pairs={{0,4},{1,5},{2,6},{3,7},{4,0},{5,1},{6,2},{7,3},{8,12},{9,13},{10,... | collective-permute-start | bytes 68 | tf_op jit(solution)/shard_map/ppermute | solution.py:222
  11.2 6.2 %collective-permute-start.5 = (bf16[512,128]{1,0:T(8,128)(2,1)S(1)}, bf16[512,128]{1,0:T(8,128)(2,1)S(1)}, u32[]{:S(2)}, u32[]{:S(2)}) collective-permute-start(bf16[512,128]{1,0:T(8,128)(2,1)S(1)} %get-tuple-element.54), channel_id=1, source_target_pairs={{8,0},{9,1},{10,2},{11,3},{12,4},{13,5},{14,6},{15,7},{16,8},{17,9... | collective-permute-start | bytes 393224 | tf_op jit(solution)/shard_map/ppermute | solution.py:299
  13.4 2.8 %collective-permute-start.4 = (s32[1,5]{1,0:T(1,128)S(1)}, s32[1,5]{1,0:T(1,128)S(1)}, u32[]{:S(2)}, u32[]{:S(2)}) collective-permute-start(s32[1,5]{1,0:T(1,128)S(1)} %add.13), channel_id=1, source_target_pairs={{0,2},{1,3},{2,0},{3,1},{4,6},{5,7},{6,4},{7,5},{8,10},{9,11},{10,... | collective-permute-start | bytes 68 | tf_op jit(solution)/shard_map/ppermute | solution.py:222
